TPU v7x, 512 devices: a whole 4x8x8 slice. The times are simulated.
512 devices in a mesh: section: 16 (over y, core), dp: 32 (over z, x).
Axes of the slice: x: 4, y: 8, z: 8, core: 2. Of those that a mesh axis runs over, the one named last changes fastest.
Arguments:
- images: bfloat16 [2, 4096, 256], P(None, 'dp'), may hold values from -6 to 6
- cotangent: bfloat16 [2, 4096, 256], P(None, 'dp'), may hold values from -6 to 6
- w_in: bfloat16 [16, 2, 256, 256], P('section'), may hold values from -0.375 to 0.375
- w_out: bfloat16 [16, 2, 256, 256], P('section'), may hold values from -0.375 to 0.375
- gains: float32 [16, 2, 256], P('section'), may hold values from 0.1 to 1.9
- layer_counts: int32 [16], P('section'), may hold values from 1 to 2
Outputs:
- section_outputs: bfloat16 [16, 2, 4096, 256], P('section', None, 'dp')
- grad_in: float32 [16, 2, 256, 256], P('section', None, 'dp')
- grad_out: float32 [16, 2, 256, 256], P('section', None, 'dp')
- grad_gain: float32 [16, 2, 256], P('section', None, 'dp')
All inputs are finite; a program needn't handle non-finite values.
Results may differ from a plain program's by a relative error of at most 0.04.
Values may be sent and summed in bfloat16 or wider, within the bound.
No kernel may reach another device: no remote copies, remote signals or barrier semaphores. Data moves between devices by JAX's collectives and lax.ppermute only.
A program may use at most 64 MiB of HBM per device.

v0:
```python
import jax
import jax.numpy as jnp
from jax import lax
from jax.sharding import PartitionSpec as P


def from_partner(x, axis, apart):
    return lax.ppermute(x, axis, [(i, i ^ 1 << apart) for i in range(lax.axis_size(axis))])


def passed_along(value, axis, steps):
    count = lax.axis_size(axis)
    initial, last = (max(0, -steps), min(count, count - steps))
    return lax.ppermute(value, axis, [(source, source + steps) for source in range(initial, last)])


def residual_block(inflow, first_w, second_w, gain_rows, active_layers):
    state = inflow
    for layer_index in range(first_w.shape[0]):
        mean_square = jnp.mean(state * state, axis=-1, keepdims=True)
        normed = (state * lax.rsqrt(mean_square + 1e-06) * gain_rows[layer_index]).astype(
            jnp.bfloat16
        )
        pre_act = jnp.dot(normed, first_w[layer_index], preferred_element_type=jnp.float32)
        activation = jax.nn.silu(pre_act).astype(jnp.bfloat16)
        updated = state + jnp.dot(
            activation, second_w[layer_index], preferred_element_type=jnp.float32
        )
        state = jnp.where(layer_index < active_layers, updated, state)
    return state


def block_grads(inflow, upstream, first_w, second_w, gain_rows, active_layers):

    def local_block(inflow_value, first_value, second_value, gain_value):
        return residual_block(inflow_value, first_value, second_value, gain_value, active_layers)

    result, pull_back = jax.vjp(local_block, inflow, first_w, second_w, gain_rows)
    return pull_back(upstream)


def store_entry(buffer, payload, position, condition):
    previous_entry = lax.dynamic_index_in_dim(buffer, position, 0, keepdims=False)
    return lax.dynamic_update_index_in_dim(
        buffer, jnp.where(condition, payload, previous_entry), position, 0
    )


def body(images, cotangent, w_in, w_out, gains, layer_counts):
    sections = lax.axis_size("section")
    half_sections = sections // 2
    bit_count = sections.bit_length() - 1
    section_here = lax.axis_index("section")
    micro_count = images.shape[0]
    first_w = w_in[0]
    second_w = w_out[0]
    gain_rows = gains[0]
    active_layers = layer_counts[0]
    tick_total = micro_count + sections - 1
    bit_order = list(range(bit_count))
    blank_rows = jnp.zeros(images.shape[1:], jnp.bfloat16)

    def route_skip(payload):
        for bit_number in bit_order:
            payload = from_partner(payload, "section", bit_number)
        return payload

    def route_grad(payload):
        for bit_number in bit_order:
            payload = from_partner(payload, "section", bit_number)
        return payload

    def forward_tick(tick_now, loop_state):
        incoming, skip_store, outputs, inflows = loop_state
        micro_index = tick_now - section_here
        working = (micro_index >= 0) & (micro_index < micro_count)
        slot_index = jnp.clip(micro_index, 0, micro_count - 1)
        image_now = lax.dynamic_index_in_dim(
            images, jnp.clip(tick_now, 0, micro_count - 1), 0, keepdims=False
        )
        previous = jnp.where(section_here == 0, image_now, incoming)
        skip_term = jnp.where(
            section_here >= half_sections,
            lax.dynamic_index_in_dim(skip_store, slot_index, 0, keepdims=False),
            blank_rows,
        )
        inflow = previous.astype(jnp.float32) + skip_term.astype(jnp.float32)
        outflow = residual_block(inflow, first_w, second_w, gain_rows, active_layers).astype(
            jnp.bfloat16
        )
        outputs = store_entry(outputs, outflow, slot_index, working)
        inflows = store_entry(inflows, inflow, slot_index, working)
        incoming = passed_along(outflow, "section", 1)
        arrived = route_skip(outflow)
        source_index = tick_now - (sections - 1 - section_here)
        keep_it = (
            (source_index >= 0) & (source_index < micro_count) & (section_here >= half_sections)
        )
        skip_store = store_entry(
            skip_store, arrived, jnp.clip(source_index, 0, micro_count - 1), keep_it
        )
        return (incoming, skip_store, outputs, inflows)

    start_state = (
        blank_rows,
        jnp.zeros(images.shape, jnp.bfloat16),
        jnp.zeros(images.shape, jnp.bfloat16),
        jnp.zeros(images.shape, jnp.float32),
    )
    incoming, skip_store, outputs, inflows = lax.fori_loop(0, tick_total, forward_tick, start_state)

    def backward_tick(tick_now, loop_state):
        incoming, grad_store, acc_in, acc_out, acc_gain = loop_state
        micro_index = tick_now - (sections - 1 - section_here)
        working = (micro_index >= 0) & (micro_index < micro_count)
        slot_index = jnp.clip(micro_index, 0, micro_count - 1)
        cot_now = lax.dynamic_index_in_dim(
            cotangent, jnp.clip(tick_now, 0, micro_count - 1), 0, keepdims=False
        )
        skip_grad = jnp.where(
            section_here < half_sections,
            lax.dynamic_index_in_dim(grad_store, slot_index, 0, keepdims=False),
            blank_rows,
        )
        upstream = jnp.where(
            section_here == sections - 1,
            cot_now.astype(jnp.float32),
            incoming.astype(jnp.float32) + skip_grad.astype(jnp.float32),
        )
        inflow = lax.dynamic_index_in_dim(inflows, slot_index, 0, keepdims=False)
        grad_parts = block_grads(inflow, upstream, first_w, second_w, gain_rows, active_layers)
        sent = grad_parts[0].astype(jnp.bfloat16)
        acc_in = acc_in + jnp.where(working, grad_parts[1].astype(jnp.float32), 0.0)
        acc_out = acc_out + jnp.where(working, grad_parts[2].astype(jnp.float32), 0.0)
        acc_gain = acc_gain + jnp.where(working, grad_parts[3], 0.0)
        incoming = passed_along(sent, "section", -1)
        arrived = route_grad(sent)
        source_index = tick_now - section_here
        keep_it = (
            (source_index >= 0) & (source_index < micro_count) & (section_here < half_sections)
        )
        grad_store = store_entry(
            grad_store, arrived, jnp.clip(source_index, 0, micro_count - 1), keep_it
        )
        return (incoming, grad_store, acc_in, acc_out, acc_gain)

    back_state = (
        blank_rows,
        jnp.zeros(images.shape, jnp.bfloat16),
        jnp.zeros(first_w.shape, jnp.float32),
        jnp.zeros(second_w.shape, jnp.float32),
        jnp.zeros(gain_rows.shape, jnp.float32),
    )
    incoming, grad_store, acc_in, acc_out, acc_gain = lax.fori_loop(
        0, tick_total, backward_tick, back_state
    )
    summed = (
        lax.psum_scatter(acc_in, "dp", scatter_dimension=1, tiled=True),
        lax.psum_scatter(acc_out, "dp", scatter_dimension=1, tiled=True),
        lax.psum_scatter(acc_gain, "dp", scatter_dimension=1, tiled=True),
    )
    return (outputs[None], summed[0][None], summed[1][None], summed[2][None])


def solution(mesh):
    return jax.shard_map(
        body,
        mesh=mesh,
        in_specs=(
            P(None, "dp", None),
            P(None, "dp", None),
            P("section", None, None, None),
            P("section", None, None, None),
            P("section", None, None),
            P("section"),
        ),
        out_specs=(
            P("section", None, "dp", None),
            P("section", None, "dp", None),
            P("section", None, "dp", None),
            P("section", None, "dp"),
        ),
        check_vma=False,
    )
```

profile of v0, /device:TPU:1, one launch (start us, length us, event | category | flops | bytes accessed | tf_op | source)
XLA Modules:
  0.0 1503.9 jit_solution(7182996331860302742)
XLA Ops:
  8.9 493.0 %while.45 = (s32[]{:T(128)}, bf16[128,256]{1,0:T(8,128)(2,1)S(1)}, bf16[2,128,256]{2,1,0:T(8,128)(2,1)S(1)}, bf16[2,128,256]{2,1,0:T(8,128)(2,1)S(1)}, f32[2,128...) while((s32[]{:T(128)}, bf16[128,256]{1,0:T(8,128)(2,1)S(1)}, ...), condition=%wide.region_3.4_spmd, body=%wide.region_0.3_spmd.sunk | while | flops 68583688 | bytes 5125189 | solution.py:110
  10.7 8.8 collective-permute-start.1
  34.1 6.9 collective-permute-done.4
  42.9 5.3 collective-permute-start.1
  63.1 6.8 collective-permute-done.4
  71.8 5.3 collective-permute-start.1
  91.8 6.9 collective-permute-done.4
  100.6 5.4 collective-permute-start.1
  120.7 6.8 collective-permute-done.4
  129.4 5.6 collective-permute-start.1
  149.4 6.8 collective-permute-done.4
  158.2 5.5 collective-permute-start.1
  178.3 6.8 collective-permute-done.4
  187.0 5.6 collective-permute-start.1
  207.0 6.8 collective-permute-done.4
  215.8 5.5 collective-permute-start.1
  235.9 6.8 collective-permute-done.4
  244.6 5.6 collective-permute-start.1
  264.6 6.8 collective-permute-done.4
  273.4 5.5 collective-permute-start.1
  293.5 6.8 collective-permute-done.4
  302.2 5.6 collective-permute-start.1
  322.2 6.8 collective-permute-done.4
  331.0 5.5 collective-permute-start.1
  351.1 6.8 collective-permute-done.4
  359.8 5.6 collective-permute-start.1
  379.8 6.8 collective-permute-done.4
  388.5 5.5 collective-permute-start.1
  408.7 6.8 collective-permute-done.4
  417.4 5.6 collective-permute-start.1
  437.4 6.8 collective-permute-done.4
  446.1 5.5 collective-permute-start.1
  466.3 6.8 collective-permute-done.4
  475.0 5.6 collective-permute-start.1
  495.0 6.8 collective-permute-done.4
  502.8 546.0 %while.46 = (s32[]{:T(128)}, bf16[128,256]{1,0:T(8,128)(2,1)S(1)}, bf16[2,128,256]{2,1,0:T(8,128)(2,1)S(1)}, f32[2,256,256]{2,1,0:T(8,128)S(1)}, f32[2,256,256]{...) while((s32[]{:T(128)}, bf16[128,256]{1,0:T(8,128)(2,1)S(1)}, ...), condition=%wide.region_11.12_spmd.clone, body=%wide.region_4.11_spmd.clone.sunk | while | flops 189598720 | bytes 11371137 | solution.py:154
  505.6 5.5 collective-permute-start.6
  527.9 6.7 collective-permute-done.9
  537.4 5.1 collective-permute-start.6
  561.1 5.3 collective-permute-done.9
  569.2 6.1 collective-permute-start.6
  594.4 4.9 collective-permute-done.9
  621.2 6.4 collective-permute-start.9
  633.1 6.0 collective-permute-start.6
  655.0 6.3 collective-permute-start.9
  685.7 7.7 collective-permute-start.9
  697.9 6.0 collective-permute-start.6
  718.4 7.7 collective-permute-start.9
  730.7 5.0 collective-permute-start.6
  751.5 7.1 collective-permute-start.9
  782.2 7.5 collective-permute-start.9
  794.3 5.6 collective-permute-start.6
  815.7 6.9 collective-permute-start.9
  846.6 8.0 collective-permute-start.9
  878.6 8.0 collective-permute-start.9
  910.7 8.0 collective-permute-start.9
  942.8 8.0 collective-permute-start.9
  974.9 8.0 collective-permute-start.9
  987.5 4.8 collective-permute-start.6
  1007.0 8.0 collective-permute-start.9
  1039.1 8.0 collective-permute-start.9
  1052.4 67.2 %all-reduce.6 = f32[2,256]{1,0:T(2,128)S(1)} all-reduce(f32[2,256]{1,0:T(2,128)S(1)} %get-tuple-element.603), channel_id=4, replica_groups=mesh['section'=16,'dp'=32] {'dp'}, use_global_device_ids=true, to_apply=%region_14.15.clone | all-reduce | flops 512 | bytes 4096
  1120.2 153.3 %reduce-scatter.4.cloned.1.call-done = f32[2,8,256]{2,1,0:T(8,128)} async-done(((f32[2,256,256]{2,1,0:T(8,128)}), f32[2,8,256]{2,1,0:T(8,128)}) %reduce-scatter.4.cloned.1.call-update) | async-done | bytes 16400 | tf_op jit(solution)/shard_map/reduce_scatter | solution.py:158
  1273.5 223.6 %reduce-scatter.6.cloned.1.call-done = f32[2,8,256]{2,1,0:T(8,128)} async-done(((f32[2,256,256]{2,1,0:T(8,128)}), f32[2,8,256]{2,1,0:T(8,128)}) %reduce-scatter.6.cloned.1.call-update) | async-done | bytes 16400 | tf_op jit(solution)/shard_map/reduce_scatter | solution.py:159
  (973 shorter events, 657.9 us)
Async XLA Ops:
  7.2 1266.3 %reduce-scatter.4.cloned.1.call-start = ((), (), s32[]{:S(2)}) async-start(), calls=%async_computation.2 | async-start | bytes 540672 | tf_op jit(solution)/shard_map/reduce_scatter | solution.py:158
  10.7 9.7 collective-permute-start.1
  27.3 13.7 collective-permute-start
  56.0 13.9 collective-permute-start
  60.6 9.3 collective-permute-start.4
  84.9 13.8 collective-permute-start
  89.5 9.2 collective-permute-start.4
  113.8 13.7 collective-permute-start
  118.5 9.0 collective-permute-start.4
  142.8 13.5 collective-permute-start
  147.2 9.1 collective-permute-start.4
  171.4 13.7 collective-permute-start
  176.1 9.0 collective-permute-start.4
  200.4 13.5 collective-permute-start
  204.8 9.0 collective-permute-start.4
  229.0 13.7 collective-permute-start
  233.7 9.0 collective-permute-start.4
  258.0 13.5 collective-permute-start
  262.4 9.1 collective-permute-start.4
  286.6 13.7 collective-permute-start
  315.6 13.5 collective-permute-start
  320.0 9.1 collective-permute-start.4
  344.2 13.7 collective-permute-start
  373.2 13.5 collective-permute-start
  377.6 9.1 collective-permute-start.4
  401.8 13.7 collective-permute-start
  406.5 9.0 collective-permute-start.4
  430.8 13.5 collective-permute-start
  435.2 9.0 collective-permute-start.4
  459.4 13.7 collective-permute-start
  464.1 9.0 collective-permute-start.4
  488.4 13.5 collective-permute-start
  492.8 9.0 collective-permute-start.4
  511.1 16.8 %collective-permute-start.5 = (bf16[128,256]{1,0:T(8,128)(2,1)S(1)}, bf16[128,256]{1,0:T(8,128)(2,1)S(1)}, u32[]{:S(2)}, u32[]{:S(2)}) collective-permute-start(bf16[128,256]{1,0:T(8,128)(2,1)S(1)} %fusion.173), channel_id=1, source_target_pairs={{32,0},{64,32},{96,64},{128,96},{160,128},{192,160},{224,192},{256... | collective-permute-start | bytes 196616 | tf_op jit(solution)/shard_map/while/body/eval_jaxpr/ppermute | solution.py:14
  542.6 18.5 %collective-permute-start.5 = (bf16[128,256]{1,0:T(8,128)(2,1)S(1)}, bf16[128,256]{1,0:T(8,128)(2,1)S(1)}, u32[]{:S(2)}, u32[]{:S(2)}) collective-permute-start(bf16[128,256]{1,0:T(8,128)(2,1)S(1)} %fusion.173), channel_id=1, source_target_pairs={{32,0},{64,32},{96,64},{128,96},{160,128},{192,160},{224,192},{256... | collective-permute-start | bytes 196616 | tf_op jit(solution)/shard_map/while/body/eval_jaxpr/ppermute | solution.py:14
  569.2 9.1 collective-permute-start.6
  575.3 19.1 %collective-permute-start.5 = (bf16[128,256]{1,0:T(8,128)(2,1)S(1)}, bf16[128,256]{1,0:T(8,128)(2,1)S(1)}, u32[]{:S(2)}, u32[]{:S(2)}) collective-permute-start(bf16[128,256]{1,0:T(8,128)(2,1)S(1)} %fusion.173), channel_id=1, source_target_pairs={{32,0},{64,32},{96,64},{128,96},{160,128},{192,160},{224,192},{256... | collective-permute-start | bytes 196616 | tf_op jit(solution)/shard_map/while/body/eval_jaxpr/ppermute | solution.py:14
  589.9 9.4 collective-permute-start.9
  606.7 21.0 %collective-permute-start.5 = (bf16[128,256]{1,0:T(8,128)(2,1)S(1)}, bf16[128,256]{1,0:T(8,128)(2,1)S(1)}, u32[]{:S(2)}, u32[]{:S(2)}) collective-permute-start(bf16[128,256]{1,0:T(8,128)(2,1)S(1)} %fusion.173), channel_id=1, source_target_pairs={{32,0},{64,32},{96,64},{128,96},{160,128},{192,160},{224,192},{256... | collective-permute-start | bytes 196616 | tf_op jit(solution)/shard_map/while/body/eval_jaxpr/ppermute | solution.py:14
  633.1 9.0 collective-permute-start.6
  639.1 22.2 %collective-permute-start.5 = (bf16[128,256]{1,0:T(8,128)(2,1)S(1)}, bf16[128,256]{1,0:T(8,128)(2,1)S(1)}, u32[]{:S(2)}, u32[]{:S(2)}) collective-permute-start(bf16[128,256]{1,0:T(8,128)(2,1)S(1)} %fusion.173), channel_id=1, source_target_pairs={{32,0},{64,32},{96,64},{128,96},{160,128},{192,160},{224,192},{256... | collective-permute-start | bytes 196616 | tf_op jit(solution)/shard_map/while/body/eval_jaxpr/ppermute | solution.py:14
  670.9 22.5 %collective-permute-start.5 = (bf16[128,256]{1,0:T(8,128)(2,1)S(1)}, bf16[128,256]{1,0:T(8,128)(2,1)S(1)}, u32[]{:S(2)}, u32[]{:S(2)}) collective-permute-start(bf16[128,256]{1,0:T(8,128)(2,1)S(1)} %fusion.173), channel_id=1, source_target_pairs={{32,0},{64,32},{96,64},{128,96},{160,128},{192,160},{224,192},{256... | collective-permute-start | bytes 196616 | tf_op jit(solution)/shard_map/while/body/eval_jaxpr/ppermute | solution.py:14
  685.7 9.4 collective-permute-start.9
  703.9 22.3 %collective-permute-start.5 = (bf16[128,256]{1,0:T(8,128)(2,1)S(1)}, bf16[128,256]{1,0:T(8,128)(2,1)S(1)}, u32[]{:S(2)}, u32[]{:S(2)}) collective-permute-start(bf16[128,256]{1,0:T(8,128)(2,1)S(1)} %fusion.173), channel_id=1, source_target_pairs={{32,0},{64,32},{96,64},{128,96},{160,128},{192,160},{224,192},{256... | collective-permute-start | bytes 196616 | tf_op jit(solution)/shard_map/while/body/eval_jaxpr/ppermute | solution.py:14
  718.4 9.5 collective-permute-start.9
  735.7 22.9 %collective-permute-start.5 = (bf16[128,256]{1,0:T(8,128)(2,1)S(1)}, bf16[128,256]{1,0:T(8,128)(2,1)S(1)}, u32[]{:S(2)}, u32[]{:S(2)}) collective-permute-start(bf16[128,256]{1,0:T(8,128)(2,1)S(1)} %fusion.173), channel_id=1, source_target_pairs={{32,0},{64,32},{96,64},{128,96},{160,128},{192,160},{224,192},{256... | collective-permute-start | bytes 196616 | tf_op jit(solution)/shard_map/while/body/eval_jaxpr/ppermute | solution.py:14
  767.7 22.0 %collective-permute-start.5 = (bf16[128,256]{1,0:T(8,128)(2,1)S(1)}, bf16[128,256]{1,0:T(8,128)(2,1)S(1)}, u32[]{:S(2)}, u32[]{:S(2)}) collective-permute-start(bf16[128,256]{1,0:T(8,128)(2,1)S(1)} %fusion.173), channel_id=1, source_target_pairs={{32,0},{64,32},{96,64},{128,96},{160,128},{192,160},{224,192},{256... | collective-permute-start | bytes 196616 | tf_op jit(solution)/shard_map/while/body/eval_jaxpr/ppermute | solution.py:14
  782.2 9.2 collective-permute-start.9
  799.9 22.6 %collective-permute-start.5 = (bf16[128,256]{1,0:T(8,128)(2,1)S(1)}, bf16[128,256]{1,0:T(8,128)(2,1)S(1)}, u32[]{:S(2)}, u32[]{:S(2)}) collective-permute-start(bf16[128,256]{1,0:T(8,128)(2,1)S(1)} %fusion.173), channel_id=1, source_target_pairs={{32,0},{64,32},{96,64},{128,96},{160,128},{192,160},{224,192},{256... | collective-permute-start | bytes 196616 | tf_op jit(solution)/shard_map/while/body/eval_jaxpr/ppermute | solution.py:14
  831.9 22.7 %collective-permute-start.5 = (bf16[128,256]{1,0:T(8,128)(2,1)S(1)}, bf16[128,256]{1,0:T(8,128)(2,1)S(1)}, u32[]{:S(2)}, u32[]{:S(2)}) collective-permute-start(bf16[128,256]{1,0:T(8,128)(2,1)S(1)} %fusion.173), channel_id=1, source_target_pairs={{32,0},{64,32},{96,64},{128,96},{160,128},{192,160},{224,192},{256... | collective-permute-start | bytes 196616 | tf_op jit(solution)/shard_map/while/body/eval_jaxpr/ppermute | solution.py:14
  846.6 9.8 collective-permute-start.9
  864.0 22.7 %collective-permute-start.5 = (bf16[128,256]{1,0:T(8,128)(2,1)S(1)}, bf16[128,256]{1,0:T(8,128)(2,1)S(1)}, u32[]{:S(2)}, u32[]{:S(2)}) collective-permute-start(bf16[128,256]{1,0:T(8,128)(2,1)S(1)} %fusion.173), channel_id=1, source_target_pairs={{32,0},{64,32},{96,64},{128,96},{160,128},{192,160},{224,192},{256... | collective-permute-start | bytes 196616 | tf_op jit(solution)/shard_map/while/body/eval_jaxpr/ppermute | solution.py:14
  878.6 9.8 collective-permute-start.9
  896.1 22.7 %collective-permute-start.5 = (bf16[128,256]{1,0:T(8,128)(2,1)S(1)}, bf16[128,256]{1,0:T(8,128)(2,1)S(1)}, u32[]{:S(2)}, u32[]{:S(2)}) collective-permute-start(bf16[128,256]{1,0:T(8,128)(2,1)S(1)} %fusion.173), channel_id=1, source_target_pairs={{32,0},{64,32},{96,64},{128,96},{160,128},{192,160},{224,192},{256... | collective-permute-start | bytes 196616 | tf_op jit(solution)/shard_map/while/body/eval_jaxpr/ppermute | solution.py:14
  910.7 9.8 collective-permute-start.9
  928.2 22.7 %collective-permute-start.5 = (bf16[128,256]{1,0:T(8,128)(2,1)S(1)}, bf16[128,256]{1,0:T(8,128)(2,1)S(1)}, u32[]{:S(2)}, u32[]{:S(2)}) collective-permute-start(bf16[128,256]{1,0:T(8,128)(2,1)S(1)} %fusion.173), channel_id=1, source_target_pairs={{32,0},{64,32},{96,64},{128,96},{160,128},{192,160},{224,192},{256... | collective-permute-start | bytes 196616 | tf_op jit(solution)/shard_map/while/body/eval_jaxpr/ppermute | solution.py:14
  942.8 9.8 collective-permute-start.9
  960.3 22.7 %collective-permute-start.5 = (bf16[128,256]{1,0:T(8,128)(2,1)S(1)}, bf16[128,256]{1,0:T(8,128)(2,1)S(1)}, u32[]{:S(2)}, u32[]{:S(2)}) collective-permute-start(bf16[128,256]{1,0:T(8,128)(2,1)S(1)} %fusion.173), channel_id=1, source_target_pairs={{32,0},{64,32},{96,64},{128,96},{160,128},{192,160},{224,192},{256... | collective-permute-start | bytes 196616 | tf_op jit(solution)/shard_map/while/body/eval_jaxpr/ppermute | solution.py:14
  974.9 9.8 collective-permute-start.9
  992.4 22.7 %collective-permute-start.5 = (bf16[128,256]{1,0:T(8,128)(2,1)S(1)}, bf16[128,256]{1,0:T(8,128)(2,1)S(1)}, u32[]{:S(2)}, u32[]{:S(2)}) collective-permute-start(bf16[128,256]{1,0:T(8,128)(2,1)S(1)} %fusion.173), channel_id=1, source_target_pairs={{32,0},{64,32},{96,64},{128,96},{160,128},{192,160},{224,192},{256... | collective-permute-start | bytes 196616 | tf_op jit(solution)/shard_map/while/body/eval_jaxpr/ppermute | solution.py:14
  1007.0 9.8 collective-permute-start.9
  1024.4 22.7 %collective-permute-start.5 = (bf16[128,256]{1,0:T(8,128)(2,1)S(1)}, bf16[128,256]{1,0:T(8,128)(2,1)S(1)}, u32[]{:S(2)}, u32[]{:S(2)}) collective-permute-start(bf16[128,256]{1,0:T(8,128)(2,1)S(1)} %fusion.173), channel_id=1, source_target_pairs={{32,0},{64,32},{96,64},{128,96},{160,128},{192,160},{224,192},{256... | collective-permute-start | bytes 196616 | tf_op jit(solution)/shard_map/while/body/eval_jaxpr/ppermute | solution.py:14
  1039.1 9.8 collective-permute-start.9
  1049.7 447.3 %reduce-scatter.6.cloned.1.call-start = ((), (), s32[]{:S(2)}) async-start(), calls=%async_computation.3 | async-start | bytes 540672 | tf_op jit(solution)/shard_map/reduce_scatter | solution.py:159
  (149 other events, 736.7 us)
Sparse Core Ops, SparseCore 0:
  1049.8 223.6 reduce-scatter.3
  1279.1 217.9 reduce-scatter.5
where the time goes:
time: 1510 us; the launch traced here: 1500 us
  waiting for transfers between devices  694 us (46%)
  starting transfers between devices  614 us (41%)
  blocking collectives  67.2 us (4%)
  matrix products  60.6 us (4%)
  local copies, waits for them, and re-layouts  29.1 us (2%)
  other arithmetic  15.5 us (1%)
  between operations  15.5 us (1%)
    ppermute x136, starting transfers between devices, from_partner(): lax.ppermute(x, axis, [(i, i ^ 1 << apart) for i in range(lax.axis_size(a...  523 us
    ppermute x136, waiting for transfers between devices, from_partner(): lax.ppermute(x, axis, [(i, i ^ 1 << apart) for i in range(lax.axis_size(a...  317 us
    reduce_scatter x1, waiting for transfers between devices, body(): lax.psum_scatter(acc_out, 'dp', scatter_dimension=1, tiled=True)  224 us
    reduce_scatter x1, waiting for transfers between devices, body(): lax.psum_scatter(acc_in, 'dp', scatter_dimension=1, tiled=True)  153 us
    ppermute x34, starting transfers between devices, passed_along(): lax.ppermute(value, axis, [(source, source + steps) for source in range(i...  91 us
    unnamed x1, blocking collectives  67.2 us
    dot_general x119, matrix products, residual_block(): jnp.dot(activation, second_w[layer_index], preferred_element_type=jnp.flo...  33.8 us
  transfers between devices with their start and end apart: 172, of which 121 were waited for; matrix products, arithmetic and copies ran while one was open for 2% of the time, Pallas kernels for 0%

commit v1 on v0

v1 whole, which is shorter than its diff:
```python
import functools
import jax
import jax.numpy as jnp
from jax import lax
from jax.experimental import pallas as pl
from jax.experimental.pallas import tpu as pltpu
from jax.sharding import PartitionSpec as P

C = 256
EPS = 1e-06
F32 = jnp.float32
BF16 = jnp.bfloat16


def dot(a, b):
    return jnp.dot(a, b, preferred_element_type=F32)


def dot_t(a, b):
    return lax.dot_general(a, b, (((1,), (1,)), ((), ())), preferred_element_type=F32)


def dot_rows(a, b):
    return lax.dot_general(a, b, (((0,), (0,)), ((), ())), preferred_element_type=F32)


def scale_of(state):
    return lax.rsqrt(jnp.mean(state * state, axis=-1, keepdims=True) + EPS)


def layer_forward(state, gain, first, second):
    normed = (state * scale_of(state) * gain).astype(BF16)
    pre = dot(normed, first)
    act = (pre * jax.nn.sigmoid(pre)).astype(BF16)
    return state + dot(act, second), pre


def layer_backward(grad, state, pre, gain, first, second):
    d_act = dot_t(grad.astype(BF16), second)
    sig = jax.nn.sigmoid(pre)
    slope = sig * (1.0 + pre * (1.0 - sig))
    d_pre = (d_act * slope).astype(BF16)
    d_normed = dot_t(d_pre, first)
    scale = scale_of(state)
    unit = state * scale
    d_unit = d_normed * gain
    inner = jnp.mean(d_unit * unit, axis=-1, keepdims=True)
    return grad + scale * (d_unit - unit * inner)


def weight_copy(w_hbm, w_vmem, sems, section):
    return pltpu.make_async_copy(w_hbm.at[section], w_vmem.at[section], sems.at[section])


def forward_kernel(sections, counts, x_ref, g_ref, w_hbm, out_ref, inflow_ref, state_ref, pre_ref, w_vmem, sems):
    for s in range(sections):
        weight_copy(w_hbm, w_vmem, sems, s).start()
    half = sections // 2
    for s in range(sections):
        weight_copy(w_hbm, w_vmem, sems, s).wait()
        state = (x_ref[...] if s == 0 else out_ref[s - 1]).astype(F32)
        if s >= half:
            state = state + out_ref[sections - 1 - s].astype(F32)
        inflow_ref[s] = state.astype(BF16)
        state_ref[s, 0] = state
        state, pre = layer_forward(state, g_ref[s, 0][None], w_vmem[s, 0], w_vmem[s, 2])
        pre_ref[s, 0] = pre
        out_ref[s] = state.astype(BF16)

        @pl.when(counts[s] > 1)
        def _():
            state_ref[s, 1] = state
            after, pre = layer_forward(state, g_ref[s, 1][None], w_vmem[s, 1], w_vmem[s, 3])
            pre_ref[s, 1] = pre
            out_ref[s] = after.astype(BF16)


def backward_kernel(sections, counts, ct_ref, g_ref, state_ref, pre_ref, w_hbm, up_ref, w_vmem, sent_ref, grad_ref, sems):
    for s in reversed(range(sections)):
        weight_copy(w_hbm, w_vmem, sems, s).start()
    half = sections // 2
    for s in reversed(range(sections)):
        weight_copy(w_hbm, w_vmem, sems, s).wait()
        grad = (ct_ref[...] if s == sections - 1 else sent_ref[s + 1]).astype(F32)
        if s < half:
            grad = grad + sent_ref[sections - 1 - s].astype(F32)
        up_ref[s] = grad.astype(BF16)
        grad_ref[...] = grad

        @pl.when(counts[s] > 1)
        def _():
            grad_ref[...] = layer_backward(
                grad, state_ref[s, 1], pre_ref[s, 1], g_ref[s, 1][None], w_vmem[s, 1], w_vmem[s, 3]
            )

        grad = layer_backward(
            grad_ref[...], state_ref[s, 0], pre_ref[s, 0], g_ref[s, 0][None], w_vmem[s, 0], w_vmem[s, 2]
        )
        sent_ref[s] = grad.astype(BF16)


def owner_kernel(counts, inflow_ref, up_ref, g_ref, w_in_ref, w_out_ref, parts_ref, grad_ref, gw_ref):
    inflow = inflow_ref[...].astype(F32)
    after, pre0 = layer_forward(inflow, g_ref[0][None], w_in_ref[0], w_out_ref[0])
    grad_ref[...] = up_ref[...].astype(F32)

    def gradients(layer, state, pre, grad):
        gain = g_ref[layer][None]
        grad_cast = grad.astype(BF16)
        d_act = dot_t(grad_cast, w_out_ref[layer])
        sig = jax.nn.sigmoid(pre)
        act = (pre * sig).astype(BF16)
        d_pre = (d_act * (sig * (1.0 + pre * (1.0 - sig)))).astype(BF16)
        d_normed = dot_t(d_pre, w_in_ref[layer])
        scale = scale_of(state)
        unit = state * scale
        normed = (unit * gain).astype(BF16)
        gw_ref[layer] = dot_rows(normed, d_pre)
        gw_ref[2 + layer] = dot_rows(act, grad_cast)
        return scale, unit, d_normed * gain

    @pl.when(counts[0] > 1)
    def _():
        grad = grad_ref[...]
        pre1 = dot((after * scale_of(after) * g_ref[1][None]).astype(BF16), w_in_ref[1])
        scale, unit, d_unit = gradients(1, after, pre1, grad)
        inner = jnp.mean(d_unit * unit, axis=-1, keepdims=True)
        grad_ref[...] = grad + scale * (d_unit - unit * inner)

    @pl.when(counts[0] <= 1)
    def _():
        gw_ref[1] = jnp.zeros((C, C), F32)
        gw_ref[3] = jnp.zeros((C, C), F32)

    gradients(0, inflow, pre0, grad_ref[...])

    columns, _, _ = parts_ref.shape
    share = C // columns
    for matrix in range(2):
        both = [gw_ref[2 * matrix + layer].reshape(columns, share, C) for layer in range(2)]
        parts_ref[:, :, matrix * C : (matrix + 1) * C] = jnp.concatenate(both, 1).astype(BF16)


def sum_kernel(parts_ref, w_ref, g_ref, gw_in_ref, gw_out_ref, gain_ref):
    columns, double, _ = parts_ref.shape
    total = parts_ref[0].astype(F32)
    for source in range(1, columns):
        total = total + parts_ref[source].astype(F32)
    share = double // 2
    for layer in range(2):
        rows = total[layer * share : (layer + 1) * share]
        gw_in_ref[layer] = rows[:, :C]
        gw_out_ref[layer] = rows[:, C:]
        product = jnp.sum(rows[:, :C] * w_ref[layer], axis=1, keepdims=True)
        gain_ref[layer] = product / g_ref[layer]


def vmem():
    return pl.BlockSpec(memory_space=pltpu.VMEM)


def smem():
    return pl.BlockSpec(memory_space=pltpu.SMEM)


def hbm():
    return pl.BlockSpec(memory_space=pl.ANY)


def run_forward(counts, x, gains, weights):
    sections = weights.shape[0]
    rows = x.shape[0]
    shape = jax.ShapeDtypeStruct
    return pl.pallas_call(
        functools.partial(forward_kernel, sections),
        out_shape=(
            shape((sections, rows, C), BF16),
            shape((sections, rows, C), BF16),
            shape((sections, 2, rows, C), F32),
            shape((sections, 2, rows, C), F32),
        ),
        in_specs=[smem(), vmem(), vmem(), hbm()],
        out_specs=(vmem(),) * 4,
        scratch_shapes=[pltpu.VMEM(weights.shape, BF16), pltpu.SemaphoreType.DMA((sections,))],
        compiler_params=pltpu.CompilerParams(vmem_limit_bytes=48 * 2**20),
        name="chain_forward",
    )(counts, x, gains, weights)


def run_backward(counts, ct, gains, states, pres, weights):
    sections = weights.shape[0]
    rows = ct.shape[0]
    return pl.pallas_call(
        functools.partial(backward_kernel, sections),
        out_shape=jax.ShapeDtypeStruct((sections, rows, C), BF16),
        in_specs=[smem(), vmem(), vmem(), vmem(), vmem(), hbm()],
        out_specs=vmem(),
        scratch_shapes=[
            pltpu.VMEM(weights.shape, BF16),
            pltpu.VMEM((sections, rows, C), BF16),
            pltpu.VMEM((rows, C), F32),
            pltpu.SemaphoreType.DMA((sections,)),
        ],
        compiler_params=pltpu.CompilerParams(vmem_limit_bytes=48 * 2**20),
        cost_estimate=pl.CostEstimate(flops=4 * 10**9, bytes_accessed=9 * 2**20, transcendentals=10**6),
        name="chain_backward",
    )(counts, ct, gains, states, pres, weights)


def run_owner(counts, inflow, up, gains, w_in, w_out, columns):
    rows = inflow.shape[0]
    return pl.pallas_call(
        owner_kernel,
        out_shape=jax.ShapeDtypeStruct((columns, 2 * C // columns, 2 * C), BF16),
        in_specs=[smem()] + [vmem()] * 5,
        out_specs=vmem(),
        scratch_shapes=[pltpu.VMEM((rows, C), F32), pltpu.VMEM((4, C, C), F32)],
        compiler_params=pltpu.CompilerParams(vmem_limit_bytes=32 * 2**20),
        name="owner_gradients",
    )(counts, inflow, up, gains, w_in, w_out)


def run_sum(parts, w_rows, gain_rows):
    share = C // parts.shape[0]
    shape = jax.ShapeDtypeStruct
    return pl.pallas_call(
        sum_kernel,
        out_shape=(shape((2, share, C), F32), shape((2, share, C), F32), shape((2, share, 1), F32)),
        in_specs=[vmem()] * 3,
        out_specs=(vmem(),) * 3,
        compiler_params=pltpu.CompilerParams(vmem_limit_bytes=16 * 2**20),
        name="sum_parts",
    )(parts, w_rows, gain_rows)


def body(images, cotangent, w_in, w_out, gains, layer_counts):
    sections = lax.axis_size("section")
    columns = lax.axis_size("dp")
    here = lax.axis_index("section")
    micro, pixels, _ = images.shape
    rows = micro * pixels // sections

    weights = lax.all_gather(jnp.concatenate([w_in[0], w_out[0]]), "section", axis=0)
    small = jnp.concatenate([gains[0], jnp.broadcast_to(layer_counts.astype(F32)[:, None], (1, C))])
    small = jnp.broadcast_to(small[None], (sections, 3, C))
    small = lax.all_to_all(small, "section", 0, 0, tiled=True)
    all_gains = small[:, :2]
    all_counts = small[:, 2, 0].astype(jnp.int32)

    def own_rows(x):
        return lax.dynamic_index_in_dim(x.reshape(sections, rows, C), here, 0, keepdims=False)

    outs, inflows, states, pres = run_forward(all_counts, own_rows(images), all_gains, weights)
    there = lax.all_to_all(jnp.concatenate([outs, inflows], 1), "section", 0, 0, tiled=True)
    ups = run_backward(all_counts, own_rows(cotangent), all_gains, states, pres, weights)
    section_outputs = there[:, :rows].reshape(micro, pixels, C)
    inflow = there[:, rows:].reshape(micro * pixels, C)
    up = lax.all_to_all(ups, "section", 0, 0, tiled=True).reshape(micro * pixels, C)

    parts = run_owner(layer_counts, inflow, up, gains[0], w_in[0], w_out[0], columns)
    parts = lax.all_to_all(parts, "dp", 0, 0, tiled=True)
    share = C // columns
    start = lax.axis_index("dp") * share
    w_rows = lax.dynamic_slice_in_dim(w_in[0], start, share, 1).astype(F32)
    gain_rows = lax.dynamic_slice_in_dim(gains[0], start, share, 1)[:, :, None]
    grad_in, grad_out, grad_gain = run_sum(parts, w_rows, gain_rows)
    return section_outputs[None], grad_in[None], grad_out[None], grad_gain[None, :, :, 0]


def solution(mesh):
    return jax.shard_map(
        body,
        mesh=mesh,
        in_specs=(
            P(None, "dp", None),
            P(None, "dp", None),
            P("section", None, None, None),
            P("section", None, None, None),
            P("section", None, None),
            P("section"),
        ),
        out_specs=(
            P("section", None, "dp", None),
            P("section", None, "dp", None),
            P("section", None, "dp", None),
            P("section", None, "dp"),
        ),
        check_vma=False,
    )
```

time: 1510 us -> 157 us (0.10)
  waiting for transfers between devices: 694 us -> 77.6 us
  starting transfers between devices: 614 us -> 32.1 us
  blocking collectives: 67.2 us -> 0 us
  matrix products: 60.6 us -> 0 us
  local copies, waits for them, and re-layouts: 29.1 us -> 2.91 us
  Pallas kernels: 0 us -> 24.9 us
    ppermute x170 -> x0, starting transfers between devices: 614 us -> none  [the longest x136 523 us: from_partner(): lax.ppermute(x, axis, [(i, i ^ 1 << apart) for i in range(lax.axis_size(a...]
    reduce_scatter x2 -> x0, waiting for transfers between devices: 377 us -> none  [the longest x1 224 us: body(): lax.psum_scatter(acc_out, 'dp', scatter_dimension=1, tiled=True)]
    ppermute x170 -> x0, waiting for transfers between devices: 317 us -> none  [the longest x136 317 us: from_partner(): lax.ppermute(x, axis, [(i, i ^ 1 << apart) for i in range(lax.axis_size(a...]
    unnamed x1 -> x0, blocking collectives: 67.2 us -> none
    dot_general x221 -> x0, matrix products: 60.6 us -> none  [the longest x119 33.8 us: residual_block(): jnp.dot(activation, second_w[layer_index], preferred_element_type=jnp.flo...]
    all_gather x0 -> x1, waiting for transfers between devices: none -> 44.8 us  [body(): lax.all_gather(jnp.concatenate([w_in[0], w_out[0]]), 'section', axis=0)]
    all_to_all x0 -> x4, waiting for transfers between devices: none -> 32.8 us  [the longest x1 17.2 us: body(): parts = lax.all_to_all(parts, 'dp', 0, 0, tiled=True)]
    all_to_all x0 -> x4, starting transfers between devices: none -> 32 us  [the longest x1 10.2 us: body(): small = lax.all_to_all(small, 'section', 0, 0, tiled=True)]
  transfers between devices with their start and end apart: 172 -> 5, of which waited for: 121 -> 4; matrix products, arithmetic and copies ran while one was open for 2% -> 2% of each run, Pallas kernels for 0% -> 8%
where the time goes in v1:
time: 157 us; the launch traced here: 156 us
  waiting for transfers between devices  77.6 us (49%)
  starting transfers between devices  32.1 us (20%)
  Pallas kernels  24.9 us (16%)
  between operations  14.8 us (9%)
  other arithmetic  3.69 us (2%)
  local copies, waits for them, and re-layouts  2.91 us (2%)
    all_gather x1, waiting for transfers between devices, body(): lax.all_gather(jnp.concatenate([w_in[0], w_out[0]]), 'section', axis=0)  44.8 us
    all_to_all x1, waiting for transfers between devices, body(): parts = lax.all_to_all(parts, 'dp', 0, 0, tiled=True)  17.2 us
    pallas_call x1, Pallas kernels, run_backward(): pl.pallas_call(functools.partial(backward_kernel, sections), out_shape=ja...  11.8 us
    all_to_all x1, starting transfers between devices, body(): small = lax.all_to_all(small, 'section', 0, 0, tiled=True)  10.2 us
    pallas_call x1, Pallas kernels, run_forward(): pl.pallas_call(functools.partial(forward_kernel, sections), out_shape=(sh...  10.1 us
    all_to_all x1, starting transfers between devices, body(): parts = lax.all_to_all(parts, 'dp', 0, 0, tiled=True)  9.9 us
    all_to_all x1, waiting for transfers between devices, body(): lax.all_to_all(ups, 'section', 0, 0, tiled=True).reshape(micro * pixels, C)  8.5 us
    all_to_all x1, starting transfers between devices, body(): lax.all_to_all(ups, 'section', 0, 0, tiled=True).reshape(micro * pixels, C)  7.24 us
  transfers between devices with their start and end apart: 5, of which 4 were waited for; matrix products, arithmetic and copies ran while one was open for 2% of the time, Pallas kernels for 8%

profile of v1, /device:TPU:1, one launch (start us, length us, event | category | flops | bytes accessed | tf_op | source)
XLA Modules:
  0.0 155.9 jit_solution(7830094871299526075)
XLA Ops:
  7.2 0.0 all-gather.3.cloned.1.call-start
  7.2 1.9 %pad_maximum_fusion = bf16[4,256,256]{2,1,0:T(8,128)(2,1)} fusion(bf16[2,256,256]{2,1,0:T(8,128)(2,1)} %bitcast.24, bf16[2,256,256]{2,1,0:T(8,128)(2,1)} %bitcast.22), kind=kLoop, calls=%fused_computation | loop fusion | flops 262144 | bytes 1048576 | tf_op jit(solution)/shard_map/concatenate | solution.py:243
  9.1 0.0 all-gather.3.cloned.1.call-update
  9.8 0.7 concatenate.9
  10.5 0.6 broadcast_in_dim.22
  11.1 10.2 %all-to-all-start = ((f32[16,3,256]{2,1,0:T(4,128)}), f32[16,3,256]{2,1,0:T(4,128)S(1)}, u32[]{:S(2)}, u32[]{:S(2)}) async-start(f32[16,3,256]{2,1,0:T(4,128)} %broadcast_in_dim.22), calls=%async_computation | async-start | bytes 131072 | tf_op jit(solution)/shard_map/all_to_all | solution.py:246
  21.3 0.7 dynamic-slice_bitcast_fusion
  22.0 7.1 %all-to-all-done = f32[16,3,256]{2,1,0:T(4,128)S(1)} async-done(((f32[16,3,256]{2,1,0:T(4,128)}), f32[16,3,256]{2,1,0:T(4,128)S(1)}, u32[]{:S(2)}, u32[]{:S(2)}) %all-to-all-start) | async-done | bytes 49184 | tf_op jit(solution)/shard_map/all_to_all | solution.py:246
  29.1 0.4 fusion.counts
  29.5 44.8 %all-gather.3.cloned.1.call-done = bf16[64,256,256]{2,1,0:T(8,128)(2,1)} async-done(((bf16[4,256,256]{2,1,0:T(8,128)(2,1)}), bf16[64,256,256]{2,1,0:T(8,128)(2,1)}) %all-gather.3.cloned.1.call-update) | async-done | bytes 8388624 | tf_op jit(solution)/shard_map/all_gather | solution.py:243
  74.3 10.1 %chain_forward.1 = (bf16[16,16,256]{2,1,0:T(8,128)(2,1)S(1)}, bf16[16,16,256]{2,1,0:T(8,128)(2,1)S(1)}, f32[16,2,16,256]{3,2,1,0:T(8,128)S(1)}, f32[16,2,16,256]{3,2,1,0:T(8,128)S(1)}) custom-call(s32[16]{0:T(128)S(1)} %fusion.counts, bf16[16,256]{1,0:T(8,128)(2,1)S(1)} %get-tuple-element.21.x_ref, f32[16,2,256]{2,1,0:T(2,128)S(1)} %slice.17.g_ref, ...), custom_call_target="tpu_custom_call" | custom-call | tf_op jit(solution)/shard_map/chain_forward/pallas_call | solution.py:174
  84.4 0.0 copy-start
  84.4 0.0 copy-start.1
  84.4 0.0 copy-start.2
  84.4 0.8 pad_maximum_fusion.1
  85.2 4.7 %all-to-all-start.1 = ((bf16[16,32,256]{2,1,0:T(8,128)(2,1)}), bf16[16,32,256]{2,1,0:T(8,128)(2,1)S(1)}, u32[]{:S(2)}, u32[]{:S(2)}) async-start(bf16[16,32,256]{2,1,0:T(8,128)(2,1)} %pad_maximum_fusion.1), calls=%async_computation.1 | async-start | bytes 524288 | tf_op jit(solution)/shard_map/all_to_all | solution.py:254
  89.9 11.8 %chain_backward.1 = bf16[16,16,256]{2,1,0:T(8,128)(2,1)} custom-call(s32[16]{0:T(128)S(1)} %fusion.counts, bf16[16,256]{1,0:T(8,128)(2,1)S(1)} %get-tuple-element.20.ct_ref, f32[16,2,256]{2,1,0:T(2,128)S(1)} %slice.17.g_ref, f32[16,2,16,256]{3,2,1,0:T(8,128)S(1)} %get-tuple-element.13.state_ref, f32[16,2,16,256]{3,2,1,0:T(8,128)S(1)} %get-tuple-element.14.pre_ref, ...), custom_call_target="tpu_custom_call" | custom-call | flops 4000000000 | bytes 9437184 | tf_op jit(solution)/shard_map/chain_backward/pallas_call | solution.py:193
  101.8 0.0 all-to-all-done.1
  101.8 7.2 %all-to-all-start.2 = ((bf16[16,16,256]{2,1,0:T(8,128)(2,1)}), bf16[16,16,256]{2,1,0:T(8,128)(2,1)S(1)}, u32[]{:S(2)}, u32[]{:S(2)}) async-start(bf16[16,16,256]{2,1,0:T(8,128)(2,1)} %chain_backward.1), calls=%async_computation.2 | async-start | bytes 262144 | tf_op jit(solution)/shard_map/all_to_all | solution.py:258
  109.0 0.7 fusion.1
  109.7 8.5 %all-to-all-done.2 = bf16[16,16,256]{2,1,0:T(8,128)(2,1)S(1)} async-done(((bf16[16,16,256]{2,1,0:T(8,128)(2,1)}), bf16[16,16,256]{2,1,0:T(8,128)(2,1)S(1)}, u32[]{:S(2)}, u32[]{:S(2)}) %all-to-all-start.2) | async-done | bytes 131104 | tf_op jit(solution)/shard_map/all_to_all | solution.py:258
  118.2 0.0 copy-done
  118.2 0.0 copy-done.1
  118.2 0.0 copy-done.2
  118.2 2.2 %owner_gradients.1 = bf16[32,16,512]{2,1,0:T(8,128)(2,1)} custom-call(s32[1]{0:T(128)S(6)} %copy.13.counts, bf16[256,256]{1,0:T(8,128)(2,1)S(1)} %bitcast.27, bf16[256,256]{1,0:T(8,128)(2,1)S(1)} %bitcast.26, f32[2,256]{1,0:T(2,128)S(1)} %bitcast.29, bf16[2,256,256]{2,1,0:T(8,128)(2,1)S(1)} %bitcast.23, bf16[2,256,256]{2,1,0:T(8,128)(2,1)S(1)} %bitcast.25), custom_call_target="tpu_custom_call" | custom-call | tf_op jit(solution)/shard_map/owner_gradients/pallas_call | solution.py:212
  120.4 9.9 %all-to-all-start.3 = ((bf16[32,16,512]{2,1,0:T(8,128)(2,1)}), bf16[32,16,512]{2,1,0:T(8,128)(2,1)S(1)}, u32[]{:S(2)}, u32[]{:S(2)}) async-start(bf16[32,16,512]{2,1,0:T(8,128)(2,1)} %owner_gradients.1), calls=%async_computation.3 | async-start | bytes 1048576 | tf_op jit(solution)/shard_map/all_to_all | solution.py:261
  130.3 0.1 dynamic-slice_bitcast_fusion.2
  130.4 0.1 copy.12.g_ref
  130.5 17.2 %all-to-all-done.3.parts_ref = bf16[32,16,512]{2,1,0:T(8,128)(2,1)S(1)} async-done(((bf16[32,16,512]{2,1,0:T(8,128)(2,1)}), bf16[32,16,512]{2,1,0:T(8,128)(2,1)S(1)}, u32[]{:S(2)}, u32[]{:S(2)}) %all-to-all-start.3) | async-done | bytes 524320 | tf_op jit(solution)/shard_map/all_to_all | solution.py:261
  147.7 0.7 sum_parts.1
  148.4 0.6 reduce.1
  (2 shorter events, 0.0 us)
Async XLA Ops:
  7.2 67.1 %all-gather.3.cloned.1.call-start = ((), (), s32[]{:S(2)}) async-start(), calls=%async_computation.4 | async-start | bytes 8912896 | tf_op jit(solution)/shard_map/all_gather | solution.py:243
  11.1 18.0 %all-to-all-start = ((f32[16,3,256]{2,1,0:T(4,128)}), f32[16,3,256]{2,1,0:T(4,128)S(1)}, u32[]{:S(2)}, u32[]{:S(2)}) async-start(f32[16,3,256]{2,1,0:T(4,128)} %broadcast_in_dim.22), calls=%async_computation | async-start | bytes 131072 | tf_op jit(solution)/shard_map/all_to_all | solution.py:246
  84.4 33.8 %copy-start = (bf16[1,2,256,256]{3,2,1,0:T(8,128)(2,1)S(1)}, bf16[1,2,256,256]{3,2,1,0:T(8,128)(2,1)}, u32[]{:S(2)}) copy-start(bf16[1,2,256,256]{3,2,1,0:T(8,128)(2,1)} %param.8) | copy-start | bytes 786436
  84.4 33.8 %copy-start.1 = (bf16[1,2,256,256]{3,2,1,0:T(8,128)(2,1)S(1)}, bf16[1,2,256,256]{3,2,1,0:T(8,128)(2,1)}, u32[]{:S(2)}) copy-start(bf16[1,2,256,256]{3,2,1,0:T(8,128)(2,1)} %param.9) | copy-start | bytes 786436
  84.4 33.8 %copy-start.2 = (f32[1,2,256]{2,1,0:T(2,128)S(1)}, f32[1,2,256]{2,1,0:T(2,128)}, u32[]{:S(2)}) copy-start(f32[1,2,256]{2,1,0:T(2,128)} %param.10) | copy-start | bytes 6148
  85.2 16.6 %all-to-all-start.1 = ((bf16[16,32,256]{2,1,0:T(8,128)(2,1)}), bf16[16,32,256]{2,1,0:T(8,128)(2,1)S(1)}, u32[]{:S(2)}, u32[]{:S(2)}) async-start(bf16[16,32,256]{2,1,0:T(8,128)(2,1)} %pad_maximum_fusion.1), calls=%async_computation.1 | async-start | bytes 524288 | tf_op jit(solution)/shard_map/all_to_all | solution.py:254
  101.8 16.4 %all-to-all-start.2 = ((bf16[16,16,256]{2,1,0:T(8,128)(2,1)}), bf16[16,16,256]{2,1,0:T(8,128)(2,1)S(1)}, u32[]{:S(2)}, u32[]{:S(2)}) async-start(bf16[16,16,256]{2,1,0:T(8,128)(2,1)} %chain_backward.1), calls=%async_computation.2 | async-start | bytes 262144 | tf_op jit(solution)/shard_map/all_to_all | solution.py:258
  120.4 27.3 %all-to-all-start.3 = ((bf16[32,16,512]{2,1,0:T(8,128)(2,1)}), bf16[32,16,512]{2,1,0:T(8,128)(2,1)S(1)}, u32[]{:S(2)}, u32[]{:S(2)}) async-start(bf16[32,16,512]{2,1,0:T(8,128)(2,1)} %owner_gradients.1), calls=%async_computation.3 | async-start | bytes 1048576 | tf_op jit(solution)/shard_map/all_to_all | solution.py:261
Sparse Core Ops, SparseCore 0:
  10.1 64.1 all-gather.2

commit v2 on v1

v2 whole, which is shorter than its diff:
```python
import jax
import jax.numpy as jnp
from jax import lax
from jax.experimental import pallas as pl
from jax.experimental.pallas import tpu as pltpu
from jax.sharding import PartitionSpec as P

C = 256
EPS = 1e-06
F32 = jnp.float32
BF16 = jnp.bfloat16
PACK = 4 * C + 16
FIRST, SECOND, MIDDLE, LAST = 0, 1, 3, 6


def dot(a, b):
    return jnp.dot(a, b, preferred_element_type=F32)


def dot_t(a, b):
    return lax.dot_general(a, b, (((1,), (1,)), ((), ())), preferred_element_type=F32)


def dot_rows(a, b):
    return lax.dot_general(a, b, (((0,), (0,)), ((), ())), preferred_element_type=F32)


def scale_of(state):
    return lax.rsqrt(jnp.mean(state * state, axis=-1, keepdims=True) + EPS)


def layer_forward(state, gain, first, second):
    normed = (state * scale_of(state) * gain).astype(BF16)
    pre = dot(normed, first)
    act = (pre * jax.nn.sigmoid(pre)).astype(BF16)
    return state + dot(act, second), pre


def layer_backward(grad, state, pre, gain, first, second):
    d_act = dot_t(grad.astype(BF16), second)
    sig = jax.nn.sigmoid(pre)
    slope = sig * (1.0 + pre * (1.0 - sig))
    d_pre = (d_act * slope).astype(BF16)
    d_normed = dot_t(d_pre, first)
    scale = scale_of(state)
    unit = state * scale
    d_unit = d_normed * gain
    inner = jnp.mean(d_unit * unit, axis=-1, keepdims=True)
    return grad + scale * (d_unit - unit * inner)


def position():
    here = lax.axis_index("section")
    return here // 2, here % 2


class Weights:
    def __init__(self, core, refs, packed, sems):
        self.refs, self.packed, self.sems, self.core = refs, packed, sems, core

    def copy(self, ref, slot):
        return pltpu.make_async_copy(ref, self.packed.at[slot], self.sems.at[slot])

    def start(self, pair):
        same, other = self.refs[2 * pair], self.refs[2 * pair + 1]
        self.copy(same, 2 * pair + self.core).start()
        self.copy(other, 2 * pair + 1 - self.core).start()

    def wait(self, slot):
        self.copy(self.refs[0], slot).wait()

    def tail(self, slot):
        return self.packed[slot, 4 * C :].astype(F32)

    def gain(self, slot, layer):
        tail = self.tail(slot)
        return tail[layer : layer + 1] + tail[2 + layer : 3 + layer] + tail[4 + layer : 5 + layer]

    def first(self, slot, layer):
        return self.packed[slot, layer * C : (layer + 1) * C]

    def second(self, slot, layer):
        return self.packed[slot, (2 + layer) * C : (3 + layer) * C]

    def both(self, slot):
        return jnp.max(self.tail(slot)[8:9]) > 1.5

    def forward(self, slot, state, state_ref, pre_ref, out_ref):
        state_ref[slot, 0] = state
        state, pre = layer_forward(state, self.gain(slot, 0), self.first(slot, 0), self.second(slot, 0))
        pre_ref[slot, 0] = pre
        out_ref[slot] = state.astype(BF16)

        @pl.when(self.both(slot))
        def _():
            state_ref[slot, 1] = state
            after, pre = layer_forward(state, self.gain(slot, 1), self.first(slot, 1), self.second(slot, 1))
            pre_ref[slot, 1] = pre
            out_ref[slot] = after.astype(BF16)

    def backward(self, slot, grad, state_ref, pre_ref, grad_ref):
        grad_ref[...] = grad

        def layer(number):
            return layer_backward(
                grad_ref[...],
                state_ref[slot, number],
                pre_ref[slot, number],
                self.gain(slot, number),
                self.first(slot, number),
                self.second(slot, number),
            )

        @pl.when(self.both(slot))
        def _():
            grad_ref[...] = layer(1)

        return layer(0).astype(BF16)


def pack_kernel(counts, w_in_ref, w_out_ref, g_ref, packed_ref):
    for layer in range(2):
        packed_ref[layer * C : (layer + 1) * C] = w_in_ref[layer]
        packed_ref[(2 + layer) * C : (3 + layer) * C] = w_out_ref[layer]
    gains = g_ref[...]
    coarse = gains.astype(BF16).astype(F32)
    rest = gains - coarse
    fine = rest.astype(BF16).astype(F32)
    count = jnp.full((2, C), counts[0].astype(F32))
    rows = [coarse, fine, rest - fine, jnp.zeros_like(coarse), count, jnp.zeros((6, C), F32)]
    packed_ref[4 * C :] = jnp.concatenate(rows, 0).astype(BF16)


def pair_kernel(chip, x_ref, same, other, outs_ref, last_ref, packed, states, pres, sems):
    here, core = position()

    @pl.when(here == chip)
    def _():
        weights = Weights(core, [same, other], packed, sems)
        weights.start(0)
        state = x_ref[...].astype(F32)
        for slot in range(2):
            weights.wait(slot)
            weights.forward(slot, state, states, pres, outs_ref)
            state = outs_ref[slot].astype(F32)
        last_ref[...] = outs_ref[1]


def middle_forward_kernel(x_ref, hop_ref, *refs):
    refs, (outs_ref, inflow_ref, hop_out, state_ref, pre_ref, packed, sems) = refs[:6], refs[6:]
    here, core = position()

    @pl.when((here == SECOND) | (here == MIDDLE))
    def _():
        weights = Weights(core, refs, packed, sems)
        for pair in range(3):
            weights.start(pair)
        for slot in range(6):
            weights.wait(slot)
            if slot == 0:
                state = jnp.where(here == SECOND, x_ref[...].astype(F32), hop_ref[...].astype(F32))
            else:
                state = outs_ref[slot - 1].astype(F32)
            if slot >= 4:
                state = state + outs_ref[7 - slot].astype(F32)
            inflow_ref[slot] = state.astype(BF16)
            weights.forward(slot, state, state_ref, pre_ref, outs_ref)
        hop_out[0] = outs_ref[5]
        hop_out[1] = outs_ref[1]
        hop_out[2] = outs_ref[0]


def store_by_owner(core, slot, refs, index, value):
    left_same, left_other, right_same, right_other, own_other, own_same = refs
    same, other = ((left_same, left_other), (own_same, own_other), (right_same, right_other))[slot // 2]

    @pl.when(core == slot % 2)
    def _():
        same[index] = value

    @pl.when(core != slot % 2)
    def _():
        other[index] = value


def last_kernel(hop_ref, skip0_ref, skip1_ref, ct_ref, outs_in, inflow_in, *refs):
    refs, refs_out = refs[:6], refs[6:]
    owners, (hop_out, sent_out, up_ref) = refs_out[:6], refs_out[6:9]
    packed, outs_ref, inflow_ref, state_ref, pre_ref, sent_ref, grad_ref, sems = refs_out[9:]
    here, core = position()

    @pl.when(here == LAST)
    def _():
        weights = Weights(core, refs, packed, sems)
        for pair in range(3):
            weights.start(pair)
        skips = [hop_ref.at[1], hop_ref.at[2], skip1_ref.at[1], skip1_ref.at[0], skip0_ref.at[1], skip0_ref.at[0]]
        for slot in range(6):
            weights.wait(slot)
            state = (hop_ref[0] if slot == 0 else outs_ref[slot - 1]).astype(F32)
            state = state + skips[slot][...].astype(F32)
            inflow_ref[slot] = state.astype(BF16)
            weights.forward(slot, state, state_ref, pre_ref, outs_ref)
        for slot in reversed(range(6)):
            up_ref[slot] = ct_ref[...] if slot == 5 else sent_ref[slot + 1]
            grad = up_ref[slot].astype(F32)
            sent_ref[slot] = weights.backward(slot, grad, state_ref, pre_ref, grad_ref)
        hop_out[...] = sent_ref[:2]
        sent_out[...] = sent_ref[2:]
        for slot in range(6):
            store_by_owner(core, slot, owners, 0, outs_ref[slot])
            store_by_owner(core, slot, owners, 1, inflow_ref[slot])

    @pl.when((here == SECOND) | (here == MIDDLE))
    def _():
        for slot in range(6):
            store_by_owner(core, slot, owners, 0, outs_in[slot])
            store_by_owner(core, slot, owners, 1, inflow_in[slot])


def middle_backward_kernel(hop_ref, state_ref, pre_ref, *refs):
    refs, (hop_out, up_ref, packed, sent_ref, grad_ref, sems) = refs[:6], refs[6:]
    here, core = position()

    @pl.when(here == MIDDLE)
    def _():
        weights = Weights(core, refs, packed, sems)
        for pair in reversed(range(3)):
            weights.start(pair)
        skips = [hop_ref.at[1], hop_ref.at[0], sent_ref.at[5], sent_ref.at[4]]
        for slot in reversed(range(6)):
            weights.wait(slot)
            grad = (hop_ref[0] if slot == 5 else sent_ref[slot + 1]).astype(F32)
            if slot < 4:
                grad = grad + skips[slot][...].astype(F32)
            up_ref[slot] = grad.astype(BF16)
            sent_ref[slot] = weights.backward(slot, grad, state_ref, pre_ref, grad_ref)
        hop_out[...] = sent_ref[0]


def first_backward_kernel(hop_ref, skip_ref, state_ref, pre_ref, up_middle, up_last, *refs):
    refs, refs_out = refs[:4], refs[4:]
    owners, (packed, sent_ref, grad_ref, sems) = refs_out[:6], refs_out[6:]
    here, core = position()
    everything = (slice(None), slice(None))

    @pl.when(here == SECOND)
    def _():
        weights = Weights(core, refs, packed, sems)
        for pair in reversed(range(2)):
            weights.start(pair)
        for slot in reversed(range(4)):
            weights.wait(slot)
            grad = (hop_ref[...] if slot == 3 else sent_ref[slot + 1]).astype(F32)
            grad = grad + skip_ref[3 - slot].astype(F32)
            store_by_owner(core, slot, owners, everything, grad.astype(BF16))
            if slot:
                sent_ref[slot] = weights.backward(slot, grad, state_ref, pre_ref, grad_ref)

    for chip, source in ((MIDDLE, up_middle), (LAST, up_last)):

        @pl.when(here == chip)
        def _():
            for slot in range(6):
                store_by_owner(core, slot, owners, everything, source[slot])


def owner_kernel(counts, g_ref, w_in_ref, w_out_ref, *refs):
    rows, ups, (out_ref, parts_ref, inflow_ref, grad_ref, gw_ref) = refs[:6], refs[6:12], refs[12:]
    here, core = position()
    active = (here == SECOND) | (here == MIDDLE) | (here == LAST)

    def arrived(refs, index):
        left_same, left_other, right_same, right_other, own_other, own_same = [ref[index].astype(F32) for ref in refs]
        same = left_same + right_same + jnp.where(active, own_same, 0.0)
        return same, left_other + right_other + own_other

    pixels = grad_ref.shape[0] // 2
    at_same = pl.ds(pl.multiple_of(core * pixels, pixels), pixels)
    at_other = pl.ds(pl.multiple_of((1 - core) * pixels, pixels), pixels)
    same, other = arrived(rows, 0)
    out_ref[core] = same.astype(BF16)
    out_ref[1 - core] = other.astype(BF16)
    same, other = arrived(rows, 1)
    inflow_ref[at_same] = same
    inflow_ref[at_other] = other
    same, other = arrived(ups, (slice(None), slice(None)))
    grad_ref[at_same] = same
    grad_ref[at_other] = other

    inflow = inflow_ref[...]
    after, pre0 = layer_forward(inflow, g_ref[0][None], w_in_ref[0], w_out_ref[0])

    def gradients(layer, state, pre, grad):
        gain = g_ref[layer][None]
        grad_cast = grad.astype(BF16)
        d_act = dot_t(grad_cast, w_out_ref[layer])
        sig = jax.nn.sigmoid(pre)
        act = (pre * sig).astype(BF16)
        d_pre = (d_act * (sig * (1.0 + pre * (1.0 - sig)))).astype(BF16)
        scale = scale_of(state)
        unit = state * scale
        normed = (unit * gain).astype(BF16)
        gw_ref[layer] = dot_rows(normed, d_pre)
        gw_ref[2 + layer] = dot_rows(act, grad_cast)
        return scale, unit, d_pre, gain

    @pl.when(counts[0] > 1)
    def _():
        grad = grad_ref[...]
        pre1 = dot((after * scale_of(after) * g_ref[1][None]).astype(BF16), w_in_ref[1])
        scale, unit, d_pre, gain = gradients(1, after, pre1, grad)
        d_unit = dot_t(d_pre, w_in_ref[1]) * gain
        inner = jnp.mean(d_unit * unit, axis=-1, keepdims=True)
        grad_ref[...] = grad + scale * (d_unit - unit * inner)

    @pl.when(counts[0] <= 1)
    def _():
        gw_ref[1] = jnp.zeros((C, C), F32)
        gw_ref[3] = jnp.zeros((C, C), F32)

    gradients(0, inflow, pre0, grad_ref[...])

    columns, double, _ = parts_ref.shape
    for matrix in range(2):
        both = [gw_ref[2 * matrix + layer].reshape(columns, double // 2, C) for layer in range(2)]
        parts_ref[:, :, matrix * C : (matrix + 1) * C] = jnp.concatenate(both, 1).astype(BF16)


def sum_kernel(parts_ref, w_ref, g_ref, gw_in_ref, gw_out_ref, gain_ref):
    columns, double, _ = parts_ref.shape
    total = parts_ref[0].astype(F32)
    for source in range(1, columns):
        total = total + parts_ref[source].astype(F32)
    share = double // 2
    for layer in range(2):
        rows = total[layer * share : (layer + 1) * share]
        gw_in_ref[layer] = rows[:, :C]
        gw_out_ref[layer] = rows[:, C:]
        product = jnp.sum(rows[:, :C] * w_ref[layer], axis=1, keepdims=True)
        gain_ref[layer] = product / g_ref[layer]


def vmem():
    return pl.BlockSpec(memory_space=pltpu.VMEM)


def smem():
    return pl.BlockSpec(memory_space=pltpu.SMEM)


def hbm():
    return pl.BlockSpec(memory_space=pl.ANY)


def call(kernel, name, inputs, outputs, scratch=(), flops=10**8):
    specs = {"vmem": vmem, "smem": smem, "hbm": hbm}
    outputs = [jax.ShapeDtypeStruct(shape, dtype) for shape, dtype in outputs]
    return pl.pallas_call(
        kernel,
        out_shape=outputs,
        in_specs=[specs[memory]() for memory, _ in inputs],
        out_specs=[vmem() for _ in outputs],
        scratch_shapes=list(scratch),
        compiler_params=pltpu.CompilerParams(vmem_limit_bytes=32 * 2**20),
        cost_estimate=pl.CostEstimate(flops=flops, bytes_accessed=2**20, transcendentals=0),
        name=name,
    )(*[array for _, array in inputs])


def at_vmem(*arrays):
    return [("vmem", array) for array in arrays]


def at_hbm(*arrays):
    return [("hbm", array) for array in arrays]


def move(value, chips, cross=False):
    pairs = [(2 * a + core, 2 * b + (1 - core if cross else core)) for a, b in chips for core in range(2)]
    return lax.ppermute(value, "section", pairs)


def packed_scratch(slots):
    return pltpu.VMEM((slots, PACK, C), BF16)


def kept(slots, pixels):
    return pltpu.VMEM((slots, 2, pixels, C), F32)


def body(images, cotangent, w_in, w_out, gains, layer_counts):
    columns = lax.axis_size("dp")
    core = lax.axis_index("section") % 2
    micro, pixels, _ = images.shape
    tile = (pixels, C)
    dma = pltpu.SemaphoreType.DMA
    x = lax.dynamic_index_in_dim(images, core, 0, keepdims=False)
    ct = lax.dynamic_index_in_dim(cotangent, core, 0, keepdims=False)

    (own,) = call(pack_kernel, "pack", [("smem", layer_counts)] + at_vmem(w_in[0], w_out[0], gains[0]), [((PACK, C), BF16)])
    partner = move(own, [(chip, chip) for chip in (FIRST, SECOND, MIDDLE, LAST)], cross=True)
    left = move(own, [(chip - 1, chip) for chip in (SECOND, MIDDLE, LAST)])
    right = move(own, [(chip + 1, chip) for chip in (MIDDLE, LAST)])

    def pair(chip, value):
        return call(
            lambda *refs: pair_kernel(chip, *refs),
            "pair_forward",
            at_vmem(value) + at_hbm(own, partner),
            [((2,) + tile, BF16), (tile, BF16)],
            [packed_scratch(2), kept(2, pixels), kept(2, pixels), dma((2,))],
        )

    outs_a, last_a = pair(FIRST, x)
    outs_b, last_b = pair(SECOND, move(last_a, [(FIRST, SECOND)]))
    hop = move(last_b, [(SECOND, MIDDLE)])
    skip0 = move(outs_a, [(FIRST, LAST)])
    skip1 = move(outs_b, [(SECOND, LAST)])
    left_partner = move(left, [(chip, chip) for chip in (SECOND, MIDDLE, LAST)], cross=True)
    right_partner = move(right, [(chip, chip) for chip in (MIDDLE, LAST)], cross=True)
    weights = at_hbm(left, left_partner, own, partner, right, right_partner)
    six, state_shape = (6,) + tile, (6, 2) + tile

    outs, inflows, hop, states, pres = call(
        middle_forward_kernel,
        "middle_forward",
        at_vmem(x, hop) + weights,
        [(six, BF16), (six, BF16), ((3,) + tile, BF16), (state_shape, F32), (state_shape, F32)],
        [packed_scratch(6), dma((6,))],
    )
    hop = move(hop, [(MIDDLE, LAST)])
    *to_owners, hop, skips, ups_last = call(
        last_kernel,
        "last_both",
        at_vmem(hop, skip0, skip1, ct, outs, inflows) + weights,
        [((2,) + tile, BF16)] * 6 + [((2,) + tile, BF16), ((4,) + tile, BF16), (six, BF16)],
        [
            packed_scratch(6),
            pltpu.VMEM(six, BF16),
            pltpu.VMEM(six, BF16),
            kept(6, pixels),
            kept(6, pixels),
            pltpu.VMEM(six, BF16),
            pltpu.VMEM(tile, F32),
            dma((6,)),
        ],
    )
    hop = move(hop, [(LAST, MIDDLE)])
    skips = move(skips, [(LAST, SECOND)])

    def deliver(values):
        left_same, left_other, right_same, right_other, own_other, own_same = values
        lefts = [(chip, chip - 1) for chip in (SECOND, MIDDLE, LAST)]
        rights = [(chip, chip + 1) for chip in (MIDDLE, LAST)]
        owns = [(chip, chip) for chip in (SECOND, MIDDLE, LAST)]
        return [
            move(left_same, lefts),
            move(left_other, lefts, cross=True),
            move(right_same, rights),
            move(right_other, rights, cross=True),
            move(own_other, owns, cross=True),
            own_same,
        ]

    rows = deliver(to_owners)
    hop, ups_middle = call(
        middle_backward_kernel,
        "middle_backward",
        at_vmem(hop, states, pres) + weights,
        [(tile, BF16), (six, BF16)],
        [packed_scratch(6), pltpu.VMEM(six, BF16), pltpu.VMEM(tile, F32), dma((6,))],
    )
    hop = move(hop, [(MIDDLE, SECOND)])
    to_owners = call(
        first_backward_kernel,
        "first_backward",
        at_vmem(hop, skips, states, pres, ups_middle, ups_last) + weights[:4],
        [(tile, BF16)] * 6,
        [packed_scratch(4), pltpu.VMEM((4,) + tile, BF16), pltpu.VMEM(tile, F32), dma((4,))],
    )
    ups = deliver(to_owners)

    share = C // columns
    section_outputs, parts = call(
        owner_kernel,
        "owner_gradients",
        [("smem", layer_counts)] + at_vmem(gains[0], w_in[0], w_out[0], *rows, *ups),
        [((micro, pixels, C), BF16), ((columns, 2 * share, 2 * C), BF16)],
        [pltpu.VMEM((micro * pixels, C), F32)] * 2 + [pltpu.VMEM((4, C, C), F32)],
    )
    parts = lax.all_to_all(parts, "dp", 0, 0, tiled=True)
    start = lax.axis_index("dp") * share
    w_rows = lax.dynamic_slice_in_dim(w_in[0], start, share, 1).astype(F32)
    gain_rows = lax.dynamic_slice_in_dim(gains[0], start, share, 1)[:, :, None]
    grad_in, grad_out, grad_gain = call(
        sum_kernel,
        "sum_parts",
        at_vmem(parts, w_rows, gain_rows),
        [((2, share, C), F32), ((2, share, C), F32), ((2, share, 1), F32)],
    )
    return section_outputs[None], grad_in[None], grad_out[None], grad_gain[None, :, :, 0]


def solution(mesh):
    return jax.shard_map(
        body,
        mesh=mesh,
        in_specs=(
            P(None, "dp", None),
            P(None, "dp", None),
            P("section", None, None, None),
            P("section", None, None, None),
            P("section", None, None),
            P("section"),
        ),
        out_specs=(
            P("section", None, "dp", None),
            P("section", None, "dp", None),
            P("section", None, "dp", None),
            P("section", None, "dp"),
        ),
        check_vma=False,
    )
```

time: 157 us -> 119 us (0.76)
  waiting for transfers between devices: 77.6 us -> 56.4 us
  Pallas kernels: 24.9 us -> 3.84 us
  starting transfers between devices: 32.1 us -> 51.7 us
  between operations: 14.8 us -> 1.78 us
  other arithmetic: 3.69 us -> 0.65 us
    all_gather x1 -> x0, waiting for transfers between devices: 44.8 us -> none  [body(): lax.all_gather(jnp.concatenate([w_in[0], w_out[0]]), 'section', axis=0)]
    ppermute x0 -> x23, waiting for transfers between devices: none -> 40 us  [move(): return lax.ppermute(value, 'section', pairs)]
    ppermute x0 -> x23, starting transfers between devices: none -> 38.8 us  [move(): return lax.ppermute(value, 'section', pairs)]
    all_to_all x3 -> x0, starting transfers between devices: 22.1 us -> none  [the longest x1 10.2 us: body(): small = lax.all_to_all(small, 'section', 0, 0, tiled=True)]
    pallas_call x4 -> x9, Pallas kernels: 24.9 us -> 3.84 us  [call(): pl.pallas_call(kernel, out_shape=outputs, in_specs=[specs[memory]() for m...]
    all_to_all x3 -> x0, waiting for transfers between devices: 15.6 us -> none  [the longest x1 8.5 us: body(): lax.all_to_all(ups, 'section', 0, 0, tiled=True).reshape(micro * pixels, C)]
    all_to_all x1, starting transfers between devices: 9.9 us -> 12.9 us  [body(): parts = lax.all_to_all(parts, 'dp', 0, 0, tiled=True)]
    concatenate x2 -> x0, other arithmetic: 2.66 us -> none  [the longest x1 1.9 us: body(): jnp.concatenate([w_in[0], w_out[0]])]
  transfers between devices with their start and end apart: 5 -> 24, of which waited for: 4 -> 8; matrix products, arithmetic and copies ran while one was open for 2% -> 0% of each run, Pallas kernels for 8% -> 1%
where the time goes in v2:
time: 119 us; the launch traced here: 117 us
  waiting for transfers between devices  56.4 us (47%)
  starting transfers between devices  51.7 us (43%)
  Pallas kernels  3.84 us (3%)
  local copies, waits for them, and re-layouts  2.8 us (2%)
  between operations  1.78 us (1%)
    ppermute x23, waiting for transfers between devices, move(): return lax.ppermute(value, 'section', pairs)  40 us
    ppermute x23, starting transfers between devices, move(): return lax.ppermute(value, 'section', pairs)  38.8 us
    all_to_all x1, waiting for transfers between devices, body(): parts = lax.all_to_all(parts, 'dp', 0, 0, tiled=True)  16.4 us
    all_to_all x1, starting transfers between devices, body(): parts = lax.all_to_all(parts, 'dp', 0, 0, tiled=True)  12.9 us
    pallas_call x9, Pallas kernels, call(): pl.pallas_call(kernel, out_shape=outputs, in_specs=[specs[memory]() for m...  3.84 us
    unnamed x16, local copies, waits for them, and re-layouts  2.61 us
  transfers between devices with their start and end apart: 24, of which 8 were waited for; matrix products, arithmetic and copies ran while one was open for 0% of the time, Pallas kernels for 1%

profile of v2, /device:TPU:1, one launch (start us, length us, event | category | flops | bytes accessed | tf_op | source)
XLA Modules:
  0.0 117.2 jit_solution(18193023972438160680)
XLA Ops:
  0.6 0.0 copy-start
  1.3 0.0 copy-start.1
  1.3 0.9 copy-done.1
  2.3 0.9 copy-done.3
  3.2 0.7 copy-done.5
  3.9 0.1 pack.1.refs_1_.refs_2_
  4.0 4.1 %collective-permute-start.3 = (bf16[1040,256]{1,0:T(8,128)(2,1)S(1)}, bf16[1040,256]{1,0:T(8,128)(2,1)S(1)}, u32[]{:S(2)}, u32[]{:S(2)}) collective-permute-start(bf16[1040,256]{1,0:T(8,128)(2,1)S(1)} %pack.1.refs_1_.refs_2_), channel_id=1, source_target_pairs={{0,64},{32,96},{128,192},{160,224},{320,384},{352,416},{1,65},{33,... | collective-permute-start | bytes 1597448 | tf_op jit(solution)/shard_map/ppermute | solution.py:381
  8.0 0.7 collective-permute-start.5
  8.7 6.0 %collective-permute-start = (bf16[1040,256]{1,0:T(8,128)(2,1)S(1)}, bf16[1040,256]{1,0:T(8,128)(2,1)S(1)}, u32[]{:S(2)}, u32[]{:S(2)}) collective-permute-start(bf16[1040,256]{1,0:T(8,128)(2,1)S(1)} %pack.1.refs_1_.refs_2_), channel_id=1, source_target_pairs={{0,32},{32,0},{64,96},{96,64},{192,224},{224,192},{384,416},{416,3... | collective-permute-start | bytes 1597448 | tf_op jit(solution)/shard_map/ppermute | solution.py:381
  14.8 0.7 collective-permute-done.3.refs_0_
  15.5 0.7 collective-permute-start.4
  16.2 0.0 collective-permute-done.5.refs_4_
  16.2 0.7 collective-permute-start.6
  17.0 0.0 collective-permute-done.refs_2_.refs_3_
  17.0 0.9 pair_forward.2
  17.9 9.3 %collective-permute-start.1 = (bf16[128,256]{1,0:T(8,128)(2,1)S(1)}, bf16[128,256]{1,0:T(8,128)(2,1)S(1)}, u32[]{:S(2)}, u32[]{:S(2)}) collective-permute-start(bf16[128,256]{1,0:T(8,128)(2,1)S(1)} %get-tuple-element.35), channel_id=1, source_target_pairs={{0,64},{32,96},{1,65},{33,97},{2,66},{34,98},{3,67},{35,99},{4,68}... | collective-permute-start | bytes 196616 | tf_op jit(solution)/shard_map/ppermute | solution.py:381
  27.1 1.5 %collective-permute-done.1.refs_0_ = bf16[128,256]{1,0:T(8,128)(2,1)S(1)} collective-permute-done((bf16[128,256]{1,0:T(8,128)(2,1)S(1)}, bf16[128,256]{1,0:T(8,128)(2,1)S(1)}, u32[]{:S(2)}, u32[]{:S(2)}) %collective-permute-start.1) | collective-permute-done | bytes 65568 | tf_op jit(solution)/shard_map/ppermute | solution.py:381
  28.7 0.0 copy-start.7
  28.7 0.8 collective-permute-start.2
  29.5 0.0 collective-permute-done.4.refs_1_
  29.5 0.0 collective-permute-done.6.refs_5_
  29.5 0.1 middle_forward.1
  29.6 0.7 collective-permute-start.7
  30.3 3.9 %collective-permute-start.8 = (bf16[2,128,256]{2,1,0:T(8,128)(2,1)S(1)}, bf16[2,128,256]{2,1,0:T(8,128)(2,1)S(1)}, u32[]{:S(2)}, u32[]{:S(2)}) collective-permute-start(bf16[2,128,256]{2,1,0:T(8,128)(2,1)S(1)} %get-tuple-element.38), channel_id=1, source_target_pairs={{0,384},{32,416},{1,385},{33,417},{2,386},{34,418},{3,387},{35,419... | collective-permute-start | bytes 393224 | tf_op jit(solution)/shard_map/ppermute | solution.py:381
  34.2 0.7 collective-permute-start.9
  34.9 1.8 %collective-permute-done.8.skip0_ref = bf16[2,128,256]{2,1,0:T(8,128)(2,1)S(1)} collective-permute-done((bf16[2,128,256]{2,1,0:T(8,128)(2,1)S(1)}, bf16[2,128,256]{2,1,0:T(8,128)(2,1)S(1)}, u32[]{:S(2)}, u32[]{:S(2)}) %collective-permute-start.8) | collective-permute-done | bytes 131104 | tf_op jit(solution)/shard_map/ppermute | solution.py:381
  36.7 0.0 collective-permute-done.9.skip1_ref
  36.7 0.0 collective-permute-done.7.hop_ref
  36.7 0.1 last_both.1
  36.8 0.7 collective-permute-start.17
  37.5 0.7 collective-permute-start.15
  38.2 0.1 middle_backward.1
  38.3 0.7 collective-permute-start.16
  38.9 1.3 %collective-permute-start.10 = (bf16[2,128,256]{2,1,0:T(8,128)(2,1)S(1)}, bf16[2,128,256]{2,1,0:T(8,128)(2,1)S(1)}, u32[]{:S(2)}, u32[]{:S(2)}) collective-permute-start(bf16[2,128,256]{2,1,0:T(8,128)(2,1)S(1)} %get-tuple-element.42), channel_id=1, source_target_pairs={{64,0},{96,32},{192,128},{224,160},{384,320},{416,352},{65,1},{97,... | collective-permute-start | bytes 393224 | tf_op jit(solution)/shard_map/ppermute | solution.py:381
  40.2 1.3 %collective-permute-start.11 = (bf16[2,128,256]{2,1,0:T(8,128)(2,1)S(1)}, bf16[2,128,256]{2,1,0:T(8,128)(2,1)S(1)}, u32[]{:S(2)}, u32[]{:S(2)}) collective-permute-start(bf16[2,128,256]{2,1,0:T(8,128)(2,1)S(1)} %get-tuple-element.43), channel_id=1, source_target_pairs={{64,32},{96,0},{192,160},{224,128},{384,352},{416,320},{65,33},{97... | collective-permute-start | bytes 393224 | tf_op jit(solution)/shard_map/ppermute | solution.py:381
  41.5 0.8 collective-permute-start.12
  42.4 0.0 collective-permute-done.16.hop_ref
  42.4 0.7 collective-permute-start.13
  43.1 0.7 collective-permute-start.14
  43.8 0.0 copy-start.2
  43.8 0.0 copy-start.4
  43.8 0.0 copy-start.6
  43.8 0.1 first_backward.1
  43.9 5.7 %collective-permute-done.10.refs_0_ = bf16[2,128,256]{2,1,0:T(8,128)(2,1)S(1)} collective-permute-done((bf16[2,128,256]{2,1,0:T(8,128)(2,1)S(1)}, bf16[2,128,256]{2,1,0:T(8,128)(2,1)S(1)}, u32[]{:S(2)}, u32[]{:S(2)}) %collective-permute-start.10) | collective-permute-done | bytes 131104 | tf_op jit(solution)/shard_map/ppermute | solution.py:381
  49.5 1.3 %collective-permute-start.18 = (bf16[128,256]{1,0:T(8,128)(2,1)S(1)}, bf16[128,256]{1,0:T(8,128)(2,1)S(1)}, u32[]{:S(2)}, u32[]{:S(2)}) collective-permute-start(bf16[128,256]{1,0:T(8,128)(2,1)S(1)} %get-tuple-element.55), channel_id=1, source_target_pairs={{64,0},{96,32},{192,128},{224,160},{384,320},{416,352},{65,1},{97,... | collective-permute-start | bytes 196616 | tf_op jit(solution)/shard_map/ppermute | solution.py:381
  50.8 2.9 %collective-permute-done.11.refs_1_ = bf16[2,128,256]{2,1,0:T(8,128)(2,1)S(1)} collective-permute-done((bf16[2,128,256]{2,1,0:T(8,128)(2,1)S(1)}, bf16[2,128,256]{2,1,0:T(8,128)(2,1)S(1)}, u32[]{:S(2)}, u32[]{:S(2)}) %collective-permute-start.11) | collective-permute-done | bytes 131104 | tf_op jit(solution)/shard_map/ppermute | solution.py:381
  53.7 1.3 %collective-permute-start.19 = (bf16[128,256]{1,0:T(8,128)(2,1)S(1)}, bf16[128,256]{1,0:T(8,128)(2,1)S(1)}, u32[]{:S(2)}, u32[]{:S(2)}) collective-permute-start(bf16[128,256]{1,0:T(8,128)(2,1)S(1)} %get-tuple-element.56), channel_id=1, source_target_pairs={{64,32},{96,0},{192,160},{224,128},{384,352},{416,320},{65,33},{97... | collective-permute-start | bytes 196616 | tf_op jit(solution)/shard_map/ppermute | solution.py:381
  55.0 0.0 collective-permute-done.12.refs_2_
  55.0 0.7 collective-permute-start.20
  55.7 0.0 collective-permute-done.13.refs_3_
  55.7 0.7 collective-permute-start.21
  56.4 0.0 collective-permute-done.14.refs_4_
  56.4 0.7 collective-permute-start.22
  57.1 25.9 %collective-permute-done.18.refs_6_ = bf16[128,256]{1,0:T(8,128)(2,1)S(1)} collective-permute-done((bf16[128,256]{1,0:T(8,128)(2,1)S(1)}, bf16[128,256]{1,0:T(8,128)(2,1)S(1)}, u32[]{:S(2)}, u32[]{:S(2)}) %collective-permute-start.18) | collective-permute-done | bytes 65568 | tf_op jit(solution)/shard_map/ppermute | solution.py:381
  82.9 1.5 %collective-permute-done.19.refs_7_ = bf16[128,256]{1,0:T(8,128)(2,1)S(1)} collective-permute-done((bf16[128,256]{1,0:T(8,128)(2,1)S(1)}, bf16[128,256]{1,0:T(8,128)(2,1)S(1)}, u32[]{:S(2)}, u32[]{:S(2)}) %collective-permute-start.19) | collective-permute-done | bytes 65568 | tf_op jit(solution)/shard_map/ppermute | solution.py:381
  84.4 0.0 collective-permute-done.21.refs_9_
  84.5 0.0 collective-permute-done.22.refs_10_
  84.5 1.9 %owner_gradients.1 = (bf16[2,128,256]{2,1,0:T(8,128)(2,1)}, bf16[32,16,512]{2,1,0:T(8,128)(2,1)}) custom-call(s32[1]{0:T(128)S(6)} %copy.12.counts, f32[2,256]{1,0:T(2,128)S(1)} %bitcast.21, bf16[2,256,256]{2,1,0:T(8,128)(2,1)S(1)} %bitcast.17, bf16[2,256,256]{2,1,0:T(8,128)(2,1)S(1)} %bitcast.19, bf16[2,128,256]{2,1,0:T(8,128)(2,1)S(1)} %collective-permute-done.10.refs_0_, ...), custom_call_target="tpu_custom_call" | custom-call | flops 100000000 | bytes 1048576 | tf_op jit(solution)/shard_map/owner_gradients/pallas_call | solution.py:359
  86.4 12.9 %all-to-all-start = ((bf16[32,16,512]{2,1,0:T(8,128)(2,1)}), bf16[32,16,512]{2,1,0:T(8,128)(2,1)S(1)}, u32[]{:S(2)}, u32[]{:S(2)}) async-start(bf16[32,16,512]{2,1,0:T(8,128)(2,1)} %get-tuple-element.62), calls=%async_computation | async-start | bytes 1048576 | tf_op jit(solution)/shard_map/all_to_all | solution.py:492
  99.3 0.1 dynamic-slice_bitcast_fusion.2
  99.4 0.1 copy.11.g_ref
  99.5 16.4 %all-to-all-done.parts_ref = bf16[32,16,512]{2,1,0:T(8,128)(2,1)S(1)} async-done(((bf16[32,16,512]{2,1,0:T(8,128)(2,1)}), bf16[32,16,512]{2,1,0:T(8,128)(2,1)S(1)}, u32[]{:S(2)}, u32[]{:S(2)}) %all-to-all-start) | async-done | bytes 524320 | tf_op jit(solution)/shard_map/all_to_all | solution.py:492
  115.9 0.7 sum_parts.1
  116.6 0.6 reduce
  (15 shorter events, 0.1 us)
Async XLA Ops:
  0.6 16.3 %copy-start = (bf16[2,128,256]{2,1,0:T(8,128)(2,1)S(1)}, bf16[2,128,256]{2,1,0:T(8,128)(2,1)}, u32[]{:S(2)}) copy-start(bf16[2,128,256]{2,1,0:T(8,128)(2,1)} %param.6) | copy-start | bytes 393220
  1.3 1.0 copy-start.1
  2.3 0.9 copy-start.3
  3.2 0.7 copy-start.5
  4.0 11.5 %collective-permute-start.3 = (bf16[1040,256]{1,0:T(8,128)(2,1)S(1)}, bf16[1040,256]{1,0:T(8,128)(2,1)S(1)}, u32[]{:S(2)}, u32[]{:S(2)}) collective-permute-start(bf16[1040,256]{1,0:T(8,128)(2,1)S(1)} %pack.1.refs_1_.refs_2_), channel_id=1, source_target_pairs={{0,64},{32,96},{128,192},{160,224},{320,384},{352,416},{1,65},{33,... | collective-permute-start | bytes 1597448 | tf_op jit(solution)/shard_map/ppermute | solution.py:381
  8.0 8.2 %collective-permute-start.5 = (bf16[1040,256]{1,0:T(8,128)(2,1)S(1)}, bf16[1040,256]{1,0:T(8,128)(2,1)S(1)}, u32[]{:S(2)}, u32[]{:S(2)}) collective-permute-start(bf16[1040,256]{1,0:T(8,128)(2,1)S(1)} %pack.1.refs_1_.refs_2_), channel_id=1, source_target_pairs={{256,192},{288,224},{448,384},{480,416},{257,193},{289,225},{449,3... | collective-permute-start | bytes 1597448 | tf_op jit(solution)/shard_map/ppermute | solution.py:381
  8.7 8.2 %collective-permute-start = (bf16[1040,256]{1,0:T(8,128)(2,1)S(1)}, bf16[1040,256]{1,0:T(8,128)(2,1)S(1)}, u32[]{:S(2)}, u32[]{:S(2)}) collective-permute-start(bf16[1040,256]{1,0:T(8,128)(2,1)S(1)} %pack.1.refs_1_.refs_2_), channel_id=1, source_target_pairs={{0,32},{32,0},{64,96},{96,64},{192,224},{224,192},{384,416},{416,3... | collective-permute-start | bytes 1597448 | tf_op jit(solution)/shard_map/ppermute | solution.py:381
  15.5 14.0 %collective-permute-start.4 = (bf16[1040,256]{1,0:T(8,128)(2,1)S(1)}, bf16[1040,256]{1,0:T(8,128)(2,1)S(1)}, u32[]{:S(2)}, u32[]{:S(2)}) collective-permute-start(bf16[1040,256]{1,0:T(8,128)(2,1)S(1)} %collective-permute-done.3.refs_0_), channel_id=1, source_target_pairs={{64,96},{96,64},{192,224},{224,192},{384,416},{416,384},{65,97},{9... | collective-permute-start | bytes 1597448 | tf_op jit(solution)/shard_map/ppermute | solution.py:381
  16.2 13.3 %collective-permute-start.6 = (bf16[1040,256]{1,0:T(8,128)(2,1)S(1)}, bf16[1040,256]{1,0:T(8,128)(2,1)S(1)}, u32[]{:S(2)}, u32[]{:S(2)}) collective-permute-start(bf16[1040,256]{1,0:T(8,128)(2,1)S(1)} %collective-permute-done.5.refs_4_), channel_id=1, source_target_pairs={{192,224},{224,192},{384,416},{416,384},{193,225},{225,193},{385,4... | collective-permute-start | bytes 1597448 | tf_op jit(solution)/shard_map/ppermute | solution.py:381
  17.9 10.8 %collective-permute-start.1 = (bf16[128,256]{1,0:T(8,128)(2,1)S(1)}, bf16[128,256]{1,0:T(8,128)(2,1)S(1)}, u32[]{:S(2)}, u32[]{:S(2)}) collective-permute-start(bf16[128,256]{1,0:T(8,128)(2,1)S(1)} %get-tuple-element.35), channel_id=1, source_target_pairs={{0,64},{32,96},{1,65},{33,97},{2,66},{34,98},{3,67},{35,99},{4,68}... | collective-permute-start | bytes 196616 | tf_op jit(solution)/shard_map/ppermute | solution.py:381
  28.7 6.2 %copy-start.7 = (bf16[2,128,256]{2,1,0:T(8,128)(2,1)S(1)}, bf16[2,128,256]{2,1,0:T(8,128)(2,1)}, u32[]{:S(2)}) copy-start(bf16[2,128,256]{2,1,0:T(8,128)(2,1)} %param.7) | copy-start | bytes 393220
  28.7 0.8 collective-permute-start.2
  29.6 7.1 %collective-permute-start.7 = (bf16[3,128,256]{2,1,0:T(8,128)(2,1)S(1)}, bf16[3,128,256]{2,1,0:T(8,128)(2,1)S(1)}, u32[]{:S(2)}, u32[]{:S(2)}) collective-permute-start(bf16[3,128,256]{2,1,0:T(8,128)(2,1)S(1)} %get-tuple-element.37), channel_id=1, source_target_pairs={{192,384},{224,416},{193,385},{225,417},{194,386},{226,418},{195,3... | collective-permute-start | bytes 589832 | tf_op jit(solution)/shard_map/ppermute | solution.py:381
  30.3 6.5 %collective-permute-start.8 = (bf16[2,128,256]{2,1,0:T(8,128)(2,1)S(1)}, bf16[2,128,256]{2,1,0:T(8,128)(2,1)S(1)}, u32[]{:S(2)}, u32[]{:S(2)}) collective-permute-start(bf16[2,128,256]{2,1,0:T(8,128)(2,1)S(1)} %get-tuple-element.38), channel_id=1, source_target_pairs={{0,384},{32,416},{1,385},{33,417},{2,386},{34,418},{3,387},{35,419... | collective-permute-start | bytes 393224 | tf_op jit(solution)/shard_map/ppermute | solution.py:381
  34.2 2.5 %collective-permute-start.9 = (bf16[2,128,256]{2,1,0:T(8,128)(2,1)S(1)}, bf16[2,128,256]{2,1,0:T(8,128)(2,1)S(1)}, u32[]{:S(2)}, u32[]{:S(2)}) collective-permute-start(bf16[2,128,256]{2,1,0:T(8,128)(2,1)S(1)} %get-tuple-element.39), channel_id=1, source_target_pairs={{64,384},{96,416},{65,385},{97,417},{66,386},{98,418},{67,387},{99... | collective-permute-start | bytes 393224 | tf_op jit(solution)/shard_map/ppermute | solution.py:381
  36.8 6.3 %collective-permute-start.17 = (bf16[4,128,256]{2,1,0:T(8,128)(2,1)S(1)}, bf16[4,128,256]{2,1,0:T(8,128)(2,1)S(1)}, u32[]{:S(2)}, u32[]{:S(2)}) collective-permute-start(bf16[4,128,256]{2,1,0:T(8,128)(2,1)S(1)} %get-tuple-element.52), channel_id=1, source_target_pairs={{384,64},{416,96},{385,65},{417,97},{386,66},{418,98},{387,67},{41... | collective-permute-start | bytes 786440 | tf_op jit(solution)/shard_map/ppermute | solution.py:381
  37.5 0.7 collective-permute-start.15
  38.3 4.1 %collective-permute-start.16 = (bf16[128,256]{1,0:T(8,128)(2,1)S(1)}, bf16[128,256]{1,0:T(8,128)(2,1)S(1)}, u32[]{:S(2)}, u32[]{:S(2)}) collective-permute-start(bf16[128,256]{1,0:T(8,128)(2,1)S(1)} %get-tuple-element.51), channel_id=1, source_target_pairs={{192,64},{224,96},{193,65},{225,97},{194,66},{226,98},{195,67},{22... | collective-permute-start | bytes 196616 | tf_op jit(solution)/shard_map/ppermute | solution.py:381
  38.9 10.6 %collective-permute-start.10 = (bf16[2,128,256]{2,1,0:T(8,128)(2,1)S(1)}, bf16[2,128,256]{2,1,0:T(8,128)(2,1)S(1)}, u32[]{:S(2)}, u32[]{:S(2)}) collective-permute-start(bf16[2,128,256]{2,1,0:T(8,128)(2,1)S(1)} %get-tuple-element.42), channel_id=1, source_target_pairs={{64,0},{96,32},{192,128},{224,160},{384,320},{416,352},{65,1},{97,... | collective-permute-start | bytes 393224 | tf_op jit(solution)/shard_map/ppermute | solution.py:381
  40.2 13.5 %collective-permute-start.11 = (bf16[2,128,256]{2,1,0:T(8,128)(2,1)S(1)}, bf16[2,128,256]{2,1,0:T(8,128)(2,1)S(1)}, u32[]{:S(2)}, u32[]{:S(2)}) collective-permute-start(bf16[2,128,256]{2,1,0:T(8,128)(2,1)S(1)} %get-tuple-element.43), channel_id=1, source_target_pairs={{64,32},{96,0},{192,160},{224,128},{384,352},{416,320},{65,33},{97... | collective-permute-start | bytes 393224 | tf_op jit(solution)/shard_map/ppermute | solution.py:381
  41.5 13.5 %collective-permute-start.12 = (bf16[2,128,256]{2,1,0:T(8,128)(2,1)S(1)}, bf16[2,128,256]{2,1,0:T(8,128)(2,1)S(1)}, u32[]{:S(2)}, u32[]{:S(2)}) collective-permute-start(bf16[2,128,256]{2,1,0:T(8,128)(2,1)S(1)} %get-tuple-element.44), channel_id=1, source_target_pairs={{192,256},{224,288},{384,448},{416,480},{193,257},{225,289},{385,4... | collective-permute-start | bytes 393224 | tf_op jit(solution)/shard_map/ppermute | solution.py:381
  42.4 13.3 %collective-permute-start.13 = (bf16[2,128,256]{2,1,0:T(8,128)(2,1)S(1)}, bf16[2,128,256]{2,1,0:T(8,128)(2,1)S(1)}, u32[]{:S(2)}, u32[]{:S(2)}) collective-permute-start(bf16[2,128,256]{2,1,0:T(8,128)(2,1)S(1)} %get-tuple-element.45), channel_id=1, source_target_pairs={{192,288},{224,256},{384,480},{416,448},{193,289},{225,257},{385,4... | collective-permute-start | bytes 393224 | tf_op jit(solution)/shard_map/ppermute | solution.py:381
  43.1 13.3 %collective-permute-start.14 = (bf16[2,128,256]{2,1,0:T(8,128)(2,1)S(1)}, bf16[2,128,256]{2,1,0:T(8,128)(2,1)S(1)}, u32[]{:S(2)}, u32[]{:S(2)}) collective-permute-start(bf16[2,128,256]{2,1,0:T(8,128)(2,1)S(1)} %get-tuple-element.46), channel_id=1, source_target_pairs={{64,96},{96,64},{192,224},{224,192},{384,416},{416,384},{65,97},{9... | collective-permute-start | bytes 393224 | tf_op jit(solution)/shard_map/ppermute | solution.py:381
  43.8 40.7 %copy-start.2 = (bf16[1,2,256,256]{3,2,1,0:T(8,128)(2,1)S(1)}, bf16[1,2,256,256]{3,2,1,0:T(8,128)(2,1)}, u32[]{:S(2)}) copy-start(bf16[1,2,256,256]{3,2,1,0:T(8,128)(2,1)} %param.8) | copy-start | bytes 786436
  43.8 40.7 %copy-start.4 = (bf16[1,2,256,256]{3,2,1,0:T(8,128)(2,1)S(1)}, bf16[1,2,256,256]{3,2,1,0:T(8,128)(2,1)}, u32[]{:S(2)}) copy-start(bf16[1,2,256,256]{3,2,1,0:T(8,128)(2,1)} %param.9) | copy-start | bytes 786436
  43.8 40.7 %copy-start.6 = (f32[1,2,256]{2,1,0:T(2,128)S(1)}, f32[1,2,256]{2,1,0:T(2,128)}, u32[]{:S(2)}) copy-start(f32[1,2,256]{2,1,0:T(2,128)} %param.10) | copy-start | bytes 6148
  49.5 33.4 %collective-permute-start.18 = (bf16[128,256]{1,0:T(8,128)(2,1)S(1)}, bf16[128,256]{1,0:T(8,128)(2,1)S(1)}, u32[]{:S(2)}, u32[]{:S(2)}) collective-permute-start(bf16[128,256]{1,0:T(8,128)(2,1)S(1)} %get-tuple-element.55), channel_id=1, source_target_pairs={{64,0},{96,32},{192,128},{224,160},{384,320},{416,352},{65,1},{97,... | collective-permute-start | bytes 196616 | tf_op jit(solution)/shard_map/ppermute | solution.py:381
  53.7 30.7 %collective-permute-start.19 = (bf16[128,256]{1,0:T(8,128)(2,1)S(1)}, bf16[128,256]{1,0:T(8,128)(2,1)S(1)}, u32[]{:S(2)}, u32[]{:S(2)}) collective-permute-start(bf16[128,256]{1,0:T(8,128)(2,1)S(1)} %get-tuple-element.56), channel_id=1, source_target_pairs={{64,32},{96,0},{192,160},{224,128},{384,352},{416,320},{65,33},{97... | collective-permute-start | bytes 196616 | tf_op jit(solution)/shard_map/ppermute | solution.py:381
  55.0 29.4 %collective-permute-start.20 = (bf16[128,256]{1,0:T(8,128)(2,1)S(1)}, bf16[128,256]{1,0:T(8,128)(2,1)S(1)}, u32[]{:S(2)}, u32[]{:S(2)}) collective-permute-start(bf16[128,256]{1,0:T(8,128)(2,1)S(1)} %get-tuple-element.57), channel_id=1, source_target_pairs={{192,256},{224,288},{384,448},{416,480},{193,257},{225,289},{385,4... | collective-permute-start | bytes 196616 | tf_op jit(solution)/shard_map/ppermute | solution.py:381
  55.7 28.7 %collective-permute-start.21 = (bf16[128,256]{1,0:T(8,128)(2,1)S(1)}, bf16[128,256]{1,0:T(8,128)(2,1)S(1)}, u32[]{:S(2)}, u32[]{:S(2)}) collective-permute-start(bf16[128,256]{1,0:T(8,128)(2,1)S(1)} %get-tuple-element.58), channel_id=1, source_target_pairs={{192,288},{224,256},{384,480},{416,448},{193,289},{225,257},{385,4... | collective-permute-start | bytes 196616 | tf_op jit(solution)/shard_map/ppermute | solution.py:381
  56.4 28.0 %collective-permute-start.22 = (bf16[128,256]{1,0:T(8,128)(2,1)S(1)}, bf16[128,256]{1,0:T(8,128)(2,1)S(1)}, u32[]{:S(2)}, u32[]{:S(2)}) collective-permute-start(bf16[128,256]{1,0:T(8,128)(2,1)S(1)} %get-tuple-element.59), channel_id=1, source_target_pairs={{64,96},{96,64},{192,224},{224,192},{384,416},{416,384},{65,97},{9... | collective-permute-start | bytes 196616 | tf_op jit(solution)/shard_map/ppermute | solution.py:381
  86.4 29.5 %all-to-all-start = ((bf16[32,16,512]{2,1,0:T(8,128)(2,1)}), bf16[32,16,512]{2,1,0:T(8,128)(2,1)S(1)}, u32[]{:S(2)}, u32[]{:S(2)}) async-start(bf16[32,16,512]{2,1,0:T(8,128)(2,1)} %get-tuple-element.62), calls=%async_computation | async-start | bytes 1048576 | tf_op jit(solution)/shard_map/all_to_all | solution.py:492

commit v3 on v2

--- a/solution.py
+++ b/solution.py
@@ -118,56 +118,71 @@
         return layer(0).astype(BF16)
 
 
-def pack_kernel(counts, w_in_ref, w_out_ref, g_ref, packed_ref):
-    for layer in range(2):
-        packed_ref[layer * C : (layer + 1) * C] = w_in_ref[layer]
-        packed_ref[(2 + layer) * C : (3 + layer) * C] = w_out_ref[layer]
+def pack_kernel(counts, w_in_ref, w_out_ref, g_ref, packed_ref, tail_ref, sems):
+    copies = [
+        pltpu.make_async_copy(ref.at[layer], packed_ref.at[pl.ds((2 * side + layer) * C, C)], sems.at[2 * side + layer])
+        for side, ref in enumerate((w_in_ref, w_out_ref))
+        for layer in range(2)
+    ]
+    for copy in copies:
+        copy.start()
     gains = g_ref[...]
     coarse = gains.astype(BF16).astype(F32)
     rest = gains - coarse
     fine = rest.astype(BF16).astype(F32)
     count = jnp.full((2, C), counts[0].astype(F32))
     rows = [coarse, fine, rest - fine, jnp.zeros_like(coarse), count, jnp.zeros((6, C), F32)]
-    packed_ref[4 * C :] = jnp.concatenate(rows, 0).astype(BF16)
-
-
-def pair_kernel(chip, x_ref, same, other, outs_ref, last_ref, packed, states, pres, sems):
+    tail_ref[...] = jnp.concatenate(rows, 0).astype(BF16)
+    copies.append(pltpu.make_async_copy(tail_ref, packed_ref.at[pl.ds(4 * C, 16)], sems.at[4]))
+    copies[-1].start()
+    for copy in copies:
+        copy.wait()
+
+
+def pair_kernel(chip, x_ref, same, other, outs_ref, last_ref, rows_same, rows_other, packed, states, pres, sems):
     here, core = position()
+
+    def keep(slot, index, value):
+        @pl.when(core == slot)
+        def _():
+            rows_same[index] = value
+
+        @pl.when(core != slot)
+        def _():
+            rows_other[index] = value
 
     @pl.when(here == chip)
     def _():
         weights = Weights(core, [same, other], packed, sems)
         weights.start(0)
-        state = x_ref[...].astype(F32)
+        state = (x_ref[core] if chip == FIRST else x_ref[...]).astype(F32)
         for slot in range(2):
             weights.wait(slot)
             weights.forward(slot, state, states, pres, outs_ref)
+            keep(slot, 0, outs_ref[slot])
+            keep(slot, 1, state.astype(BF16))
             state = outs_ref[slot].astype(F32)
         last_ref[...] = outs_ref[1]
 
 
-def middle_forward_kernel(x_ref, hop_ref, *refs):
+def middle_forward_kernel(hop_ref, *refs):
     refs, (outs_ref, inflow_ref, hop_out, state_ref, pre_ref, packed, sems) = refs[:6], refs[6:]
     here, core = position()
 
-    @pl.when((here == SECOND) | (here == MIDDLE))
+    @pl.when(here == MIDDLE)
     def _():
         weights = Weights(core, refs, packed, sems)
         for pair in range(3):
             weights.start(pair)
         for slot in range(6):
             weights.wait(slot)
-            if slot == 0:
-                state = jnp.where(here == SECOND, x_ref[...].astype(F32), hop_ref[...].astype(F32))
-            else:
-                state = outs_ref[slot - 1].astype(F32)
+            state = (hop_ref[...] if slot == 0 else outs_ref[slot - 1]).astype(F32)
             if slot >= 4:
                 state = state + outs_ref[7 - slot].astype(F32)
             inflow_ref[slot] = state.astype(BF16)
             weights.forward(slot, state, state_ref, pre_ref, outs_ref)
         hop_out[0] = outs_ref[5]
-        hop_out[1] = outs_ref[1]
-        hop_out[2] = outs_ref[0]
+        hop_out[1:] = outs_ref[:2]
 
 
 def store_by_owner(core, slot, refs, index, value):
@@ -189,12 +204,17 @@
     packed, outs_ref, inflow_ref, state_ref, pre_ref, sent_ref, grad_ref, sems = refs_out[9:]
     here, core = position()
 
+    def keep_rows(slots, outs, inflows):
+        for slot in slots:
+            store_by_owner(core, slot, owners, 0, outs[slot])
+            store_by_owner(core, slot, owners, 1, inflows[slot])
+
     @pl.when(here == LAST)
     def _():
         weights = Weights(core, refs, packed, sems)
         for pair in range(3):
             weights.start(pair)
-        skips = [hop_ref.at[1], hop_ref.at[2], skip1_ref.at[1], skip1_ref.at[0], skip0_ref.at[1], skip0_ref.at[0]]
+        skips = [hop_ref.at[2], hop_ref.at[1]] + [ref.at[index] for ref in (skip1_ref, skip0_ref) for index in (1, 0)]
         for slot in range(6):
             weights.wait(slot)
             state = (hop_ref[0] if slot == 0 else outs_ref[slot - 1]).astype(F32)
@@ -202,25 +222,32 @@
             inflow_ref[slot] = state.astype(BF16)
             weights.forward(slot, state, state_ref, pre_ref, outs_ref)
         for slot in reversed(range(6)):
-            up_ref[slot] = ct_ref[...] if slot == 5 else sent_ref[slot + 1]
+            up_ref[slot] = ct_ref[core] if slot == 5 else sent_ref[slot + 1]
             grad = up_ref[slot].astype(F32)
             sent_ref[slot] = weights.backward(slot, grad, state_ref, pre_ref, grad_ref)
         hop_out[...] = sent_ref[:2]
         sent_out[...] = sent_ref[2:]
-        for slot in range(6):
-            store_by_owner(core, slot, owners, 0, outs_ref[slot])
-            store_by_owner(core, slot, owners, 1, inflow_ref[slot])
-
-    @pl.when((here == SECOND) | (here == MIDDLE))
-    def _():
-        for slot in range(6):
-            store_by_owner(core, slot, owners, 0, outs_in[slot])
-            store_by_owner(core, slot, owners, 1, inflow_in[slot])
-
-
-def middle_backward_kernel(hop_ref, state_ref, pre_ref, *refs):
-    refs, (hop_out, up_ref, packed, sent_ref, grad_ref, sems) = refs[:6], refs[6:]
+        keep_rows(range(6), outs_ref, inflow_ref)
+
+    @pl.when(here == MIDDLE)
+    def _():
+        keep_rows(range(6), outs_in, inflow_in)
+
+
+def middle_backward_kernel(hop_ref, state_ref, pre_ref, x_ref, *refs):
+    refs, low_refs, refs_out = refs[:6], refs[6:8] + refs[2:4], refs[8:]
+    hop_out, up_ref, low_state, low_pre, packed, sent_ref, grad_ref, sems = refs_out
     here, core = position()
+
+    @pl.when(here == SECOND)
+    def _():
+        weights = Weights(core, low_refs, packed, sems)
+        for pair in range(2):
+            weights.start(pair)
+        for slot in range(4):
+            weights.wait(slot)
+            state = (x_ref[core] if slot == 0 else sent_ref[slot - 1]).astype(F32)
+            weights.forward(slot, state, low_state, low_pre, sent_ref)
 
     @pl.when(here == MIDDLE)
     def _():
@@ -239,9 +266,28 @@
 
 
 def first_backward_kernel(hop_ref, skip_ref, state_ref, pre_ref, up_middle, up_last, *refs):
-    refs, refs_out = refs[:4], refs[4:]
-    owners, (packed, sent_ref, grad_ref, sems) = refs_out[:6], refs_out[6:]
+    rows, refs, refs_out = refs[:6], refs[6:10], refs[10:]
+    away, own, (packed, sent_ref, grad_ref, sems, role_sems) = refs_out[:4], refs_out[4:6], refs_out[6:]
     here, core = position()
+    owners = list(away) + [ref.at[2] for ref in own]
+
+    def rows_copies(other, same):
+        return [
+            pltpu.make_async_copy(source, target.at[pl.ds(0, 2)], role_sems.at[number])
+            for number, (source, target) in enumerate(zip((other, same), own))
+        ]
+
+    for chips, (other, same) in (
+        ((here == MIDDLE) | (here == LAST), rows[:2]),
+        (here == FIRST, (rows[3], rows[2])),
+        (here == SECOND, (rows[5], rows[4])),
+    ):
+
+        @pl.when(chips)
+        def _():
+            for copy in rows_copies(other, same):
+                copy.start()
+
     everything = (slice(None), slice(None))
 
     @pl.when(here == SECOND)
@@ -264,29 +310,40 @@
             for slot in range(6):
                 store_by_owner(core, slot, owners, everything, source[slot])
 
+    @pl.when((here <= SECOND) | (here == MIDDLE) | (here == LAST))
+    def _():
+        for copy in rows_copies(*rows[:2]):
+            copy.wait()
+
 
 def owner_kernel(counts, g_ref, w_in_ref, w_out_ref, *refs):
-    rows, ups, (out_ref, parts_ref, inflow_ref, grad_ref, gw_ref) = refs[:6], refs[6:12], refs[12:]
+    pieces, (out_ref, parts_ref, inflow_ref, grad_ref, gw_ref) = refs[:10], refs[10:]
+    rows, ups, own = pieces[:4], pieces[4:8], (pieces[9], pieces[8])
     here, core = position()
-    active = (here == SECOND) | (here == MIDDLE) | (here == LAST)
-
-    def arrived(refs, index):
-        left_same, left_other, right_same, right_other, own_other, own_same = [ref[index].astype(F32) for ref in refs]
-        same = left_same + right_same + jnp.where(active, own_same, 0.0)
-        return same, left_other + right_other + own_other
-
     pixels = grad_ref.shape[0] // 2
-    at_same = pl.ds(pl.multiple_of(core * pixels, pixels), pixels)
-    at_other = pl.ds(pl.multiple_of((1 - core) * pixels, pixels), pixels)
-    same, other = arrived(rows, 0)
-    out_ref[core] = same.astype(BF16)
-    out_ref[1 - core] = other.astype(BF16)
-    same, other = arrived(rows, 1)
-    inflow_ref[at_same] = same
-    inflow_ref[at_other] = other
-    same, other = arrived(ups, (slice(None), slice(None)))
-    grad_ref[at_same] = same
-    grad_ref[at_other] = other
+    places = [pl.ds(pl.multiple_of(side * pixels, pixels), pixels) for side in (core, 1 - core)]
+    everything = (slice(None), slice(None))
+
+    def take_rows(chips, refs):
+        @pl.when(chips)
+        def _():
+            for ref, side, place in zip(refs, (core, 1 - core), places):
+                out_ref[side] = ref[0]
+                inflow_ref[place] = ref[1].astype(F32)
+
+    def take_ups(chips, refs, index):
+        @pl.when(chips)
+        def _():
+            for ref, place in zip(refs, places):
+                grad_ref[place] = ref[index].astype(F32)
+
+    holds = (here == SECOND) | (here == MIDDLE) | (here == LAST)
+    take_rows(holds | (here == FIRST), own)
+    take_rows((here == MIDDLE - 1) | (here == LAST - 1), rows[:2])
+    take_rows((here == MIDDLE + 1) | (here == LAST + 1), rows[2:])
+    take_ups(holds, own, 2)
+    take_ups((here == SECOND - 1) | (here == MIDDLE - 1) | (here == LAST - 1), ups[:2], everything)
+    take_ups((here == MIDDLE + 1) | (here == LAST + 1), ups[2:], everything)
 
     inflow = inflow_ref[...]
     after, pre0 = layer_forward(inflow, g_ref[0][None], w_in_ref[0], w_out_ref[0])
@@ -337,8 +394,12 @@
         rows = total[layer * share : (layer + 1) * share]
         gw_in_ref[layer] = rows[:, :C]
         gw_out_ref[layer] = rows[:, C:]
-        product = jnp.sum(rows[:, :C] * w_ref[layer], axis=1, keepdims=True)
-        gain_ref[layer] = product / g_ref[layer]
+        product = rows[:, :C] * w_ref[layer]
+        ones = jnp.ones((1, C), F32)
+        product = lax.dot_general(
+            ones, product, (((1,), (1,)), ((), ())), precision=lax.Precision.HIGHEST, preferred_element_type=F32
+        )
+        gain_ref[layer : layer + 1] = product / g_ref[layer : layer + 1]
 
 
 def vmem():
@@ -350,10 +411,10 @@
 
 
 def hbm():
-    return pl.BlockSpec(memory_space=pl.ANY)
-
-
-def call(kernel, name, inputs, outputs, scratch=(), flops=10**8):
+    return pl.BlockSpec(memory_space=pltpu.HBM)
+
+
+def call(kernel, name, inputs, outputs, scratch=(), us=1, limit=32 * 2**20):
     specs = {"vmem": vmem, "smem": smem, "hbm": hbm}
     outputs = [jax.ShapeDtypeStruct(shape, dtype) for shape, dtype in outputs]
     return pl.pallas_call(
@@ -362,8 +423,8 @@
         in_specs=[specs[memory]() for memory, _ in inputs],
         out_specs=[vmem() for _ in outputs],
         scratch_shapes=list(scratch),
-        compiler_params=pltpu.CompilerParams(vmem_limit_bytes=32 * 2**20),
-        cost_estimate=pl.CostEstimate(flops=flops, bytes_accessed=2**20, transcendentals=0),
+        compiler_params=pltpu.CompilerParams(vmem_limit_bytes=limit),
+        cost_estimate=pl.CostEstimate(flops=us * 10**9, bytes_accessed=2**20, transcendentals=0),
         name=name,
     )(*[array for _, array in inputs])
 
@@ -391,50 +452,62 @@
 
 def body(images, cotangent, w_in, w_out, gains, layer_counts):
     columns = lax.axis_size("dp")
-    core = lax.axis_index("section") % 2
     micro, pixels, _ = images.shape
     tile = (pixels, C)
     dma = pltpu.SemaphoreType.DMA
-    x = lax.dynamic_index_in_dim(images, core, 0, keepdims=False)
-    ct = lax.dynamic_index_in_dim(cotangent, core, 0, keepdims=False)
-
-    (own,) = call(pack_kernel, "pack", [("smem", layer_counts)] + at_vmem(w_in[0], w_out[0], gains[0]), [((PACK, C), BF16)])
+    barrier = lax.optimization_barrier
+
+    (own,) = call(
+        pack_kernel,
+        "pack",
+        [("smem", layer_counts)] + at_hbm(w_in[0], w_out[0]) + at_vmem(gains[0]),
+        [((PACK, C), BF16)],
+        [pltpu.VMEM((16, C), BF16), dma((5,))],
+    )
+    holders = (MIDDLE, LAST)
     partner = move(own, [(chip, chip) for chip in (FIRST, SECOND, MIDDLE, LAST)], cross=True)
-    left = move(own, [(chip - 1, chip) for chip in (SECOND, MIDDLE, LAST)])
-    right = move(own, [(chip + 1, chip) for chip in (MIDDLE, LAST)])
+    left = move(own, [(chip - 1, chip) for chip in holders])
+    right = move(own, [(chip + 1, chip) for chip in holders])
 
     def pair(chip, value):
         return call(
             lambda *refs: pair_kernel(chip, *refs),
             "pair_forward",
             at_vmem(value) + at_hbm(own, partner),
-            [((2,) + tile, BF16), (tile, BF16)],
+            [((2,) + tile, BF16), (tile, BF16)] + [((2,) + tile, BF16)] * 2,
             [packed_scratch(2), kept(2, pixels), kept(2, pixels), dma((2,))],
         )
 
-    outs_a, last_a = pair(FIRST, x)
-    outs_b, last_b = pair(SECOND, move(last_a, [(FIRST, SECOND)]))
+    outs_a, last_a, *rows_a = pair(FIRST, images)
+    outs_b, last_b, *rows_b = pair(SECOND, move(last_a, [(FIRST, SECOND)]))
     hop = move(last_b, [(SECOND, MIDDLE)])
-    skip0 = move(outs_a, [(FIRST, LAST)])
-    skip1 = move(outs_b, [(SECOND, LAST)])
-    left_partner = move(left, [(chip, chip) for chip in (SECOND, MIDDLE, LAST)], cross=True)
-    right_partner = move(right, [(chip, chip) for chip in (MIDDLE, LAST)], cross=True)
+    left, right, later, hop = barrier((left, right, own, hop))
+    left_partner = move(left, [(chip, chip) for chip in holders], cross=True)
+    right_partner = move(right, [(chip, chip) for chip in holders], cross=True)
     weights = at_hbm(left, left_partner, own, partner, right, right_partner)
-    six, state_shape = (6,) + tile, (6, 2) + tile
+    four, six = (4,) + tile, (6,) + tile
+    four_state, six_state = (4, 2) + tile, (6, 2) + tile
 
     outs, inflows, hop, states, pres = call(
         middle_forward_kernel,
         "middle_forward",
-        at_vmem(x, hop) + weights,
-        [(six, BF16), (six, BF16), ((3,) + tile, BF16), (state_shape, F32), (state_shape, F32)],
+        at_vmem(hop) + weights,
+        [(six, BF16), (six, BF16), ((3,) + tile, BF16), (six_state, F32), (six_state, F32)],
         [packed_scratch(6), dma((6,))],
-    )
+        us=3,
+    )
+    skip0, skip1, hop = barrier((outs_a, outs_b, hop))
     hop = move(hop, [(MIDDLE, LAST)])
+    skip0 = move(skip0, [(FIRST, LAST)])
+    skip1 = move(skip1, [(SECOND, LAST)])
+    low_left = move(later, [(SECOND - 1, SECOND)])
+    low_partner = move(low_left, [(SECOND, SECOND)], cross=True)
+    low_weights = at_hbm(low_left, low_partner, own, partner)
     *to_owners, hop, skips, ups_last = call(
         last_kernel,
         "last_both",
-        at_vmem(hop, skip0, skip1, ct, outs, inflows) + weights,
-        [((2,) + tile, BF16)] * 6 + [((2,) + tile, BF16), ((4,) + tile, BF16), (six, BF16)],
+        at_vmem(hop, skip0, skip1, cotangent, outs, inflows) + weights,
+        [((2,) + tile, BF16)] * 6 + [((2,) + tile, BF16), (four, BF16), (six, BF16)],
         [
             packed_scratch(6),
             pltpu.VMEM(six, BF16),
@@ -445,61 +518,64 @@
             pltpu.VMEM(tile, F32),
             dma((6,)),
         ],
+        us=8,
     )
     hop = move(hop, [(LAST, MIDDLE)])
     skips = move(skips, [(LAST, SECOND)])
 
-    def deliver(values):
-        left_same, left_other, right_same, right_other, own_other, own_same = values
-        lefts = [(chip, chip - 1) for chip in (SECOND, MIDDLE, LAST)]
+    def deliver(chips, *pieces):
+        lefts = [(chip, chip - 1) for chip in chips]
         rights = [(chip, chip + 1) for chip in (MIDDLE, LAST)]
-        owns = [(chip, chip) for chip in (SECOND, MIDDLE, LAST)]
-        return [
-            move(left_same, lefts),
-            move(left_other, lefts, cross=True),
-            move(right_same, rights),
-            move(right_other, rights, cross=True),
-            move(own_other, owns, cross=True),
-            own_same,
-        ]
-
-    rows = deliver(to_owners)
-    hop, ups_middle = call(
+        routes = ((lefts, False), (lefts, True), (rights, False), (rights, True))
+        return [move(piece, *route) for piece, route in zip(pieces, routes) if piece is not None]
+
+    *away, rows_other, rows_same = to_owners
+    rows_left, rows_right = away[:2], deliver((MIDDLE, LAST), None, None, *away[2:])
+    hop, rows_right = barrier((hop, rows_right))
+    hop, ups_middle, low_states, low_pres = call(
         middle_backward_kernel,
         "middle_backward",
-        at_vmem(hop, states, pres) + weights,
-        [(tile, BF16), (six, BF16)],
+        at_vmem(hop, states, pres, images) + weights + low_weights[:2],
+        [(tile, BF16), (six, BF16), (four_state, F32), (four_state, F32)],
         [packed_scratch(6), pltpu.VMEM(six, BF16), pltpu.VMEM(tile, F32), dma((6,))],
-    )
+        us=5,
+    )
+    rows_left, hop = barrier((rows_left, hop))
     hop = move(hop, [(MIDDLE, SECOND)])
-    to_owners = call(
+    rows_left = deliver((MIDDLE, LAST), *rows_left, None, None)
+    rows = rows_left + rows_right
+    *away, own_other, own_same = call(
         first_backward_kernel,
         "first_backward",
-        at_vmem(hop, skips, states, pres, ups_middle, ups_last) + weights[:4],
-        [(tile, BF16)] * 6,
-        [packed_scratch(4), pltpu.VMEM((4,) + tile, BF16), pltpu.VMEM(tile, F32), dma((4,))],
-    )
-    ups = deliver(to_owners)
+        at_vmem(hop, skips, low_states, low_pres, ups_middle, ups_last)
+        + at_hbm(rows_other, rows_same, *rows_a, *rows_b)
+        + low_weights,
+        [(tile, BF16)] * 4 + [((3,) + tile, BF16)] * 2,
+        [packed_scratch(4), pltpu.VMEM(four, BF16), pltpu.VMEM(tile, F32), dma((4,)), dma((2,))],
+        us=3,
+    )
+    ups = deliver((SECOND, MIDDLE, LAST), *away)
+    own_other = move(own_other, [(chip, chip) for chip in (FIRST, SECOND, MIDDLE, LAST)], cross=True)
 
     share = C // columns
     section_outputs, parts = call(
         owner_kernel,
         "owner_gradients",
-        [("smem", layer_counts)] + at_vmem(gains[0], w_in[0], w_out[0], *rows, *ups),
+        [("smem", layer_counts)] + at_vmem(gains[0], w_in[0], w_out[0], *rows, *ups, own_other, own_same),
         [((micro, pixels, C), BF16), ((columns, 2 * share, 2 * C), BF16)],
         [pltpu.VMEM((micro * pixels, C), F32)] * 2 + [pltpu.VMEM((4, C, C), F32)],
     )
     parts = lax.all_to_all(parts, "dp", 0, 0, tiled=True)
     start = lax.axis_index("dp") * share
     w_rows = lax.dynamic_slice_in_dim(w_in[0], start, share, 1).astype(F32)
-    gain_rows = lax.dynamic_slice_in_dim(gains[0], start, share, 1)[:, :, None]
+    gain_rows = lax.dynamic_slice_in_dim(gains[0], start, share, 1)
     grad_in, grad_out, grad_gain = call(
         sum_kernel,
         "sum_parts",
         at_vmem(parts, w_rows, gain_rows),
-        [((2, share, C), F32), ((2, share, C), F32), ((2, share, 1), F32)],
-    )
-    return section_outputs[None], grad_in[None], grad_out[None], grad_gain[None, :, :, 0]
+        [((2, share, C), F32), ((2, share, C), F32), ((2, share), F32)],
+    )
+    return section_outputs[None], grad_in[None], grad_out[None], grad_gain[None]
 
 
 def solution(mesh):

time: 119 us -> 118 us (level)
  waiting for transfers between devices: 56.4 us -> 46.7 us
  starting transfers between devices: 51.7 us -> 59.3 us
  Pallas kernels: 3.84 us -> 6.41 us
    ppermute x23 -> x24, waiting for transfers between devices: 40 us -> 30.2 us  [move(): return lax.ppermute(value, 'section', pairs)]
    ppermute x23 -> x24, starting transfers between devices: 38.8 us -> 46.5 us  [move(): return lax.ppermute(value, 'section', pairs)]
    pallas_call x9, Pallas kernels: 3.84 us -> 6.41 us  [call(): pl.pallas_call(kernel, out_shape=outputs, in_specs=[specs[memory]() for m...]
  transfers between devices with their start and end apart: 24 -> 25, of which waited for: 8 -> 6; matrix products, arithmetic and copies ran while one was open for 0% -> 0% of each run, Pallas kernels for 1% -> 2%
where the time goes in v3:
time: 118 us; the launch traced here: 117 us
  starting transfers between devices  59.3 us (50%)
  waiting for transfers between devices  46.7 us (40%)
  Pallas kernels  6.41 us (5%)
  local copies, waits for them, and re-layouts  2.68 us (2%)
  between operations  1.74 us (1%)
    ppermute x24, starting transfers between devices, move(): return lax.ppermute(value, 'section', pairs)  46.5 us
    ppermute x24, waiting for transfers between devices, move(): return lax.ppermute(value, 'section', pairs)  30.2 us
    all_to_all x1, waiting for transfers between devices, body(): parts = lax.all_to_all(parts, 'dp', 0, 0, tiled=True)  16.5 us
    all_to_all x1, starting transfers between devices, body(): parts = lax.all_to_all(parts, 'dp', 0, 0, tiled=True)  12.9 us
    pallas_call x9, Pallas kernels, call(): pl.pallas_call(kernel, out_shape=outputs, in_specs=[specs[memory]() for m...  6.41 us
    unnamed x16, local copies, waits for them, and re-layouts  2.6 us
  transfers between devices with their start and end apart: 25, of which 6 were waited for; matrix products, arithmetic and copies ran while one was open for 0% of the time, Pallas kernels for 2%

profile of v3, /device:TPU:1, one launch (start us, length us, event | category | flops | bytes accessed | tf_op | source)
XLA Modules:
  0.0 116.9 jit_solution(10277130454228074982)
XLA Ops:
  1.3 0.0 copy-start
  1.3 0.7 copy-done
  2.0 0.9 copy-done.2
  2.9 0.9 copy-done.4
  3.9 0.7 pack.1.refs_1_.refs_2_.refs_8_
  4.6 8.8 %collective-permute-start = (bf16[1040,256]{1,0:T(8,128)(2,1)S(1)}, bf16[1040,256]{1,0:T(8,128)(2,1)S(1)}, u32[]{:S(2)}, u32[]{:S(2)}) collective-permute-start(bf16[1040,256]{1,0:T(8,128)(2,1)S(1)} %pack.1.refs_1_.refs_2_.refs_8_), channel_id=1, source_target_pairs={{0,32},{32,0},{64,96},{96,64},{192,224},{224,192},{384,416},{416,3... | collective-permute-start | bytes 1597448 | tf_op jit(solution)/shard_map/ppermute | solution.py:442
  13.4 0.7 collective-permute-start.2
  14.1 0.7 collective-permute-start.3
  14.8 0.1 collective-permute-done.refs_2_.refs_3_.refs_9_
  14.9 1.6 %pair_forward.2 = (bf16[2,128,256]{2,1,0:T(8,128)(2,1)S(1)}, bf16[128,256]{1,0:T(8,128)(2,1)S(1)}, bf16[2,128,256]{2,1,0:T(8,128)(2,1)S(1)}, bf16[2,128,256]{2,1,0:T(8,128)(2,1)S(1)}) custom-call(bf16[2,128,256]{2,1,0:T(8,128)(2,1)S(1)} %copy-done.7, bf16[1040,256]{1,0:T(8,128)(2,1)S(1)} %pack.1.refs_1_.refs_2_.refs_8_, ...), custom_call_target="tpu_custom_call" | custom-call | flops 1000000000 | bytes 1048576 | tf_op jit(solution)/shard_map/pair_forward/pallas_call | solution.py:420
  16.5 1.3 %collective-permute-start.1 = (bf16[128,256]{1,0:T(8,128)(2,1)S(1)}, bf16[128,256]{1,0:T(8,128)(2,1)S(1)}, u32[]{:S(2)}, u32[]{:S(2)}) collective-permute-start(bf16[128,256]{1,0:T(8,128)(2,1)S(1)} %get-tuple-element.55), channel_id=1, source_target_pairs={{0,64},{32,96},{1,65},{33,97},{2,66},{34,98},{3,67},{35,99},{4,68}... | collective-permute-start | bytes 196616 | tf_op jit(solution)/shard_map/ppermute | solution.py:442
  17.8 1.3 %collective-permute-done.1.refs_0_ = bf16[128,256]{1,0:T(8,128)(2,1)S(1)} collective-permute-done((bf16[128,256]{1,0:T(8,128)(2,1)S(1)}, bf16[128,256]{1,0:T(8,128)(2,1)S(1)}, u32[]{:S(2)}, u32[]{:S(2)}) %collective-permute-start.1) | collective-permute-done | bytes 65568 | tf_op jit(solution)/shard_map/ppermute | solution.py:442
  19.2 0.0 copy-start.6
  19.2 0.8 collective-permute-start.4
  20.0 0.0 collective-permute-done.2.refs_0_
  20.0 0.0 collective-permute-done.3.refs_4_
  20.0 0.0 collective-permute-done.4.hop_ref
  20.0 0.7 collective-permute-start.5
  20.7 0.7 collective-permute-start.6
  21.4 7.3 %collective-permute-start.13 = (bf16[1040,256]{1,0:T(8,128)(2,1)S(1)}, bf16[1040,256]{1,0:T(8,128)(2,1)S(1)}, u32[]{:S(2)}, u32[]{:S(2)}) collective-permute-start(bf16[1040,256]{1,0:T(8,128)(2,1)S(1)} %pack.1.refs_1_.refs_2_.refs_8_), channel_id=1, source_target_pairs={{0,64},{32,96},{1,65},{33,97},{2,66},{34,98},{3,67},{35,99},{4,68}... | collective-permute-start | bytes 1597448 | tf_op jit(solution)/shard_map/ppermute | solution.py:442
  28.8 0.0 collective-permute-done.5.refs_1_
  28.8 0.0 collective-permute-done.6.refs_5_
  28.8 0.1 middle_forward.1
  28.9 0.7 collective-permute-start.7
  29.6 9.1 %collective-permute-start.8 = (bf16[2,128,256]{2,1,0:T(8,128)(2,1)S(1)}, bf16[2,128,256]{2,1,0:T(8,128)(2,1)S(1)}, u32[]{:S(2)}, u32[]{:S(2)}) collective-permute-start(bf16[2,128,256]{2,1,0:T(8,128)(2,1)S(1)} %get-tuple-element.63), channel_id=1, source_target_pairs={{0,384},{32,416},{1,385},{33,417},{2,386},{34,418},{3,387},{35,419... | collective-permute-start | bytes 393224 | tf_op jit(solution)/shard_map/ppermute | solution.py:442
  38.7 0.7 collective-permute-start.9
  39.4 0.0 collective-permute-done.13.refs_6_
  39.4 0.7 collective-permute-start.14
  40.1 1.3 %collective-permute-done.8.skip0_ref = bf16[2,128,256]{2,1,0:T(8,128)(2,1)S(1)} collective-permute-done((bf16[2,128,256]{2,1,0:T(8,128)(2,1)S(1)}, bf16[2,128,256]{2,1,0:T(8,128)(2,1)S(1)}, u32[]{:S(2)}, u32[]{:S(2)}) %collective-permute-start.8) | collective-permute-done | bytes 131104 | tf_op jit(solution)/shard_map/ppermute | solution.py:442
  41.4 0.0 collective-permute-done.9.skip1_ref
  41.5 0.0 collective-permute-done.7.hop_ref
  41.5 0.1 last_both.1
  41.6 0.7 collective-permute-start.10
  42.2 0.7 collective-permute-start.11
  42.9 0.7 collective-permute-start.12
  43.6 0.7 collective-permute-start.18
  44.3 0.0 collective-permute-done.10.hop_ref
  44.3 0.0 collective-permute-done.11.refs_2_
  44.3 0.0 collective-permute-done.12.refs_3_
  44.3 0.0 collective-permute-done.14.refs_7_
  44.3 0.3 middle_backward.1
  44.6 0.7 collective-permute-start.17
  45.3 0.0 collective-permute-done.18.skip_ref
  45.3 0.0 copy-start.1
  45.3 0.0 copy-start.3
  45.3 0.0 copy-start.5
  45.3 0.4 first_backward.1
  45.8 5.7 %collective-permute-start.23 = (bf16[3,128,256]{2,1,0:T(8,128)(2,1)S(1)}, bf16[3,128,256]{2,1,0:T(8,128)(2,1)S(1)}, u32[]{:S(2)}, u32[]{:S(2)}) collective-permute-start(bf16[3,128,256]{2,1,0:T(8,128)(2,1)S(1)} %get-tuple-element.97), channel_id=1, source_target_pairs={{0,32},{32,0},{64,96},{96,64},{192,224},{224,192},{384,416},{416,3... | collective-permute-start | bytes 589832 | tf_op jit(solution)/shard_map/ppermute | solution.py:442
  51.5 1.3 %collective-permute-start.19 = (bf16[128,256]{1,0:T(8,128)(2,1)S(1)}, bf16[128,256]{1,0:T(8,128)(2,1)S(1)}, u32[]{:S(2)}, u32[]{:S(2)}) collective-permute-start(bf16[128,256]{1,0:T(8,128)(2,1)S(1)} %get-tuple-element.93), channel_id=1, source_target_pairs={{64,0},{96,32},{192,128},{224,160},{384,320},{416,352},{65,1},{97,... | collective-permute-start | bytes 196616 | tf_op jit(solution)/shard_map/ppermute | solution.py:442
  52.8 1.3 %collective-permute-start.20 = (bf16[128,256]{1,0:T(8,128)(2,1)S(1)}, bf16[128,256]{1,0:T(8,128)(2,1)S(1)}, u32[]{:S(2)}, u32[]{:S(2)}) collective-permute-start(bf16[128,256]{1,0:T(8,128)(2,1)S(1)} %get-tuple-element.94), channel_id=1, source_target_pairs={{64,32},{96,0},{192,160},{224,128},{384,352},{416,320},{65,33},{97... | collective-permute-start | bytes 196616 | tf_op jit(solution)/shard_map/ppermute | solution.py:442
  54.1 0.7 collective-permute-start.15
  54.8 0.7 collective-permute-start.16
  55.4 26.5 %collective-permute-done.19.refs_4_ = bf16[128,256]{1,0:T(8,128)(2,1)S(1)} collective-permute-done((bf16[128,256]{1,0:T(8,128)(2,1)S(1)}, bf16[128,256]{1,0:T(8,128)(2,1)S(1)}, u32[]{:S(2)}, u32[]{:S(2)}) %collective-permute-start.19) | collective-permute-done | bytes 65568 | tf_op jit(solution)/shard_map/ppermute | solution.py:442
  82.0 0.7 collective-permute-start.21
  82.6 0.8 collective-permute-done.20.refs_5_
  83.5 0.7 collective-permute-start.22
  84.1 0.0 collective-permute-done.21.refs_6_
  84.1 0.0 collective-permute-done.22.refs_7_
  84.2 0.0 collective-permute-done.23.refs_8_
  84.2 2.4 %owner_gradients.1 = (bf16[2,128,256]{2,1,0:T(8,128)(2,1)}, bf16[32,16,512]{2,1,0:T(8,128)(2,1)}) custom-call(s32[1]{0:T(128)S(6)} %copy.10.counts, f32[2,256]{1,0:T(2,128)S(1)} %bitcast.13, bf16[2,256,256]{2,1,0:T(8,128)(2,1)S(1)} %bitcast.15, bf16[2,256,256]{2,1,0:T(8,128)(2,1)S(1)} %bitcast.17, bf16[2,128,256]{2,1,0:T(8,128)(2,1)S(1)} %collective-permute-done.15.refs_0_, ...), custom_call_target="tpu_custom_call" | custom-call | flops 1000000000 | bytes 1048576 | tf_op jit(solution)/shard_map/owner_gradients/pallas_call | solution.py:420
  86.6 12.9 %all-to-all-start = ((bf16[32,16,512]{2,1,0:T(8,128)(2,1)}), bf16[32,16,512]{2,1,0:T(8,128)(2,1)S(1)}, u32[]{:S(2)}, u32[]{:S(2)}) async-start(bf16[32,16,512]{2,1,0:T(8,128)(2,1)} %get-tuple-element.100), calls=%async_computation | async-start | bytes 1048576 | tf_op jit(solution)/shard_map/all_to_all | solution.py:568
  99.5 0.1 dynamic-slice_bitcast_fusion.g_ref
  99.6 16.5 %all-to-all-done.parts_ref = bf16[32,16,512]{2,1,0:T(8,128)(2,1)S(1)} async-done(((bf16[32,16,512]{2,1,0:T(8,128)(2,1)}), bf16[32,16,512]{2,1,0:T(8,128)(2,1)S(1)}, u32[]{:S(2)}, u32[]{:S(2)}) %all-to-all-start) | async-done | bytes 524320 | tf_op jit(solution)/shard_map/all_to_all | solution.py:568
  116.1 0.8 sum_parts.1
  (13 shorter events, 0.0 us)
Async XLA Ops:
  1.3 0.7 copy-start
  2.0 0.9 copy-start.2
  2.9 0.9 copy-start.4
  3.9 11.1 %copy-start.7 = (bf16[2,128,256]{2,1,0:T(8,128)(2,1)S(1)}, bf16[2,128,256]{2,1,0:T(8,128)(2,1)}, u32[]{:S(2)}) copy-start(bf16[2,128,256]{2,1,0:T(8,128)(2,1)} %x_ref.1) | copy-start | bytes 393220
  4.6 10.3 %collective-permute-start = (bf16[1040,256]{1,0:T(8,128)(2,1)S(1)}, bf16[1040,256]{1,0:T(8,128)(2,1)S(1)}, u32[]{:S(2)}, u32[]{:S(2)}) collective-permute-start(bf16[1040,256]{1,0:T(8,128)(2,1)S(1)} %pack.1.refs_1_.refs_2_.refs_8_), channel_id=1, source_target_pairs={{0,32},{32,0},{64,96},{96,64},{192,224},{224,192},{384,416},{416,3... | collective-permute-start | bytes 1597448 | tf_op jit(solution)/shard_map/ppermute | solution.py:442
  13.4 6.6 %collective-permute-start.2 = (bf16[1040,256]{1,0:T(8,128)(2,1)S(1)}, bf16[1040,256]{1,0:T(8,128)(2,1)S(1)}, u32[]{:S(2)}, u32[]{:S(2)}) collective-permute-start(bf16[1040,256]{1,0:T(8,128)(2,1)S(1)} %pack.1.refs_1_.refs_2_.refs_8_), channel_id=1, source_target_pairs={{128,192},{160,224},{320,384},{352,416},{129,193},{161,225},{321,3... | collective-permute-start | bytes 1597448 | tf_op jit(solution)/shard_map/ppermute | solution.py:442
  14.1 5.9 %collective-permute-start.3 = (bf16[1040,256]{1,0:T(8,128)(2,1)S(1)}, bf16[1040,256]{1,0:T(8,128)(2,1)S(1)}, u32[]{:S(2)}, u32[]{:S(2)}) collective-permute-start(bf16[1040,256]{1,0:T(8,128)(2,1)S(1)} %pack.1.refs_1_.refs_2_.refs_8_), channel_id=1, source_target_pairs={{256,192},{288,224},{448,384},{480,416},{257,193},{289,225},{449,3... | collective-permute-start | bytes 1597448 | tf_op jit(solution)/shard_map/ppermute | solution.py:442
  16.5 2.6 %collective-permute-start.1 = (bf16[128,256]{1,0:T(8,128)(2,1)S(1)}, bf16[128,256]{1,0:T(8,128)(2,1)S(1)}, u32[]{:S(2)}, u32[]{:S(2)}) collective-permute-start(bf16[128,256]{1,0:T(8,128)(2,1)S(1)} %get-tuple-element.55), channel_id=1, source_target_pairs={{0,64},{32,96},{1,65},{33,97},{2,66},{34,98},{3,67},{35,99},{4,68}... | collective-permute-start | bytes 196616 | tf_op jit(solution)/shard_map/ppermute | solution.py:442
  19.2 22.3 %copy-start.6 = (bf16[2,128,256]{2,1,0:T(8,128)(2,1)S(1)}, bf16[2,128,256]{2,1,0:T(8,128)(2,1)}, u32[]{:S(2)}) copy-start(bf16[2,128,256]{2,1,0:T(8,128)(2,1)} %ct_ref.1) | copy-start | bytes 393220
  19.2 0.8 collective-permute-start.4
  20.0 8.8 %collective-permute-start.5 = (bf16[1040,256]{1,0:T(8,128)(2,1)S(1)}, bf16[1040,256]{1,0:T(8,128)(2,1)S(1)}, u32[]{:S(2)}, u32[]{:S(2)}) collective-permute-start(bf16[1040,256]{1,0:T(8,128)(2,1)S(1)} %collective-permute-done.2.refs_0_), channel_id=1, source_target_pairs={{192,224},{224,192},{384,416},{416,384},{193,225},{225,193},{385,4... | collective-permute-start | bytes 1597448 | tf_op jit(solution)/shard_map/ppermute | solution.py:442
  20.7 8.1 %collective-permute-start.6 = (bf16[1040,256]{1,0:T(8,128)(2,1)S(1)}, bf16[1040,256]{1,0:T(8,128)(2,1)S(1)}, u32[]{:S(2)}, u32[]{:S(2)}) collective-permute-start(bf16[1040,256]{1,0:T(8,128)(2,1)S(1)} %collective-permute-done.3.refs_4_), channel_id=1, source_target_pairs={{192,224},{224,192},{384,416},{416,384},{193,225},{225,193},{385,4... | collective-permute-start | bytes 1597448 | tf_op jit(solution)/shard_map/ppermute | solution.py:442
  21.4 18.0 %collective-permute-start.13 = (bf16[1040,256]{1,0:T(8,128)(2,1)S(1)}, bf16[1040,256]{1,0:T(8,128)(2,1)S(1)}, u32[]{:S(2)}, u32[]{:S(2)}) collective-permute-start(bf16[1040,256]{1,0:T(8,128)(2,1)S(1)} %pack.1.refs_1_.refs_2_.refs_8_), channel_id=1, source_target_pairs={{0,64},{32,96},{1,65},{33,97},{2,66},{34,98},{3,67},{35,99},{4,68}... | collective-permute-start | bytes 1597448 | tf_op jit(solution)/shard_map/ppermute | solution.py:442
  28.9 12.6 %collective-permute-start.7 = (bf16[3,128,256]{2,1,0:T(8,128)(2,1)S(1)}, bf16[3,128,256]{2,1,0:T(8,128)(2,1)S(1)}, u32[]{:S(2)}, u32[]{:S(2)}) collective-permute-start(bf16[3,128,256]{2,1,0:T(8,128)(2,1)S(1)} %get-tuple-element.62), channel_id=1, source_target_pairs={{192,384},{224,416},{193,385},{225,417},{194,386},{226,418},{195,3... | collective-permute-start | bytes 589832 | tf_op jit(solution)/shard_map/ppermute | solution.py:442
  29.6 11.9 %collective-permute-start.8 = (bf16[2,128,256]{2,1,0:T(8,128)(2,1)S(1)}, bf16[2,128,256]{2,1,0:T(8,128)(2,1)S(1)}, u32[]{:S(2)}, u32[]{:S(2)}) collective-permute-start(bf16[2,128,256]{2,1,0:T(8,128)(2,1)S(1)} %get-tuple-element.63), channel_id=1, source_target_pairs={{0,384},{32,416},{1,385},{33,417},{2,386},{34,418},{3,387},{35,419... | collective-permute-start | bytes 393224 | tf_op jit(solution)/shard_map/ppermute | solution.py:442
  38.7 2.7 %collective-permute-start.9 = (bf16[2,128,256]{2,1,0:T(8,128)(2,1)S(1)}, bf16[2,128,256]{2,1,0:T(8,128)(2,1)S(1)}, u32[]{:S(2)}, u32[]{:S(2)}) collective-permute-start(bf16[2,128,256]{2,1,0:T(8,128)(2,1)S(1)} %get-tuple-element.64), channel_id=1, source_target_pairs={{64,384},{96,416},{65,385},{97,417},{66,386},{98,418},{67,387},{99... | collective-permute-start | bytes 393224 | tf_op jit(solution)/shard_map/ppermute | solution.py:442
  39.4 4.9 %collective-permute-start.14 = (bf16[1040,256]{1,0:T(8,128)(2,1)S(1)}, bf16[1040,256]{1,0:T(8,128)(2,1)S(1)}, u32[]{:S(2)}, u32[]{:S(2)}) collective-permute-start(bf16[1040,256]{1,0:T(8,128)(2,1)S(1)} %collective-permute-done.13.refs_6_), channel_id=1, source_target_pairs={{64,96},{96,64},{65,97},{97,65},{66,98},{98,66},{67,99},{99,67},{6... | collective-permute-start | bytes 1597448 | tf_op jit(solution)/shard_map/ppermute | solution.py:442
  41.6 2.7 %collective-permute-start.10 = (bf16[2,128,256]{2,1,0:T(8,128)(2,1)S(1)}, bf16[2,128,256]{2,1,0:T(8,128)(2,1)S(1)}, u32[]{:S(2)}, u32[]{:S(2)}) collective-permute-start(bf16[2,128,256]{2,1,0:T(8,128)(2,1)S(1)} %get-tuple-element.69), channel_id=1, source_target_pairs={{384,192},{416,224},{385,193},{417,225},{386,194},{418,226},{387,1... | collective-permute-start | bytes 393224 | tf_op jit(solution)/shard_map/ppermute | solution.py:442
  42.2 2.1 %collective-permute-start.11 = (bf16[2,128,256]{2,1,0:T(8,128)(2,1)S(1)}, bf16[2,128,256]{2,1,0:T(8,128)(2,1)S(1)}, u32[]{:S(2)}, u32[]{:S(2)}) collective-permute-start(bf16[2,128,256]{2,1,0:T(8,128)(2,1)S(1)} %get-tuple-element.70), channel_id=1, source_target_pairs={{192,256},{224,288},{384,448},{416,480},{193,257},{225,289},{385,4... | collective-permute-start | bytes 393224 | tf_op jit(solution)/shard_map/ppermute | solution.py:442
  42.9 1.4 %collective-permute-start.12 = (bf16[2,128,256]{2,1,0:T(8,128)(2,1)S(1)}, bf16[2,128,256]{2,1,0:T(8,128)(2,1)S(1)}, u32[]{:S(2)}, u32[]{:S(2)}) collective-permute-start(bf16[2,128,256]{2,1,0:T(8,128)(2,1)S(1)} %get-tuple-element.71), channel_id=1, source_target_pairs={{192,288},{224,256},{384,480},{416,448},{193,289},{225,257},{385,4... | collective-permute-start | bytes 393224 | tf_op jit(solution)/shard_map/ppermute | solution.py:442
  43.6 1.7 %collective-permute-start.18 = (bf16[4,128,256]{2,1,0:T(8,128)(2,1)S(1)}, bf16[4,128,256]{2,1,0:T(8,128)(2,1)S(1)}, u32[]{:S(2)}, u32[]{:S(2)}) collective-permute-start(bf16[4,128,256]{2,1,0:T(8,128)(2,1)S(1)} %get-tuple-element.82), channel_id=1, source_target_pairs={{384,64},{416,96},{385,65},{417,97},{386,66},{418,98},{387,67},{41... | collective-permute-start | bytes 786440 | tf_op jit(solution)/shard_map/ppermute | solution.py:442
  44.6 0.7 collective-permute-start.17
  45.3 38.9 %copy-start.1 = (f32[1,2,256]{2,1,0:T(2,128)S(1)}, f32[1,2,256]{2,1,0:T(2,128)}, u32[]{:S(2)}) copy-start(f32[1,2,256]{2,1,0:T(2,128)} %param.10) | copy-start | bytes 6148
  45.3 38.9 %copy-start.3 = (bf16[1,2,256,256]{3,2,1,0:T(8,128)(2,1)S(1)}, bf16[1,2,256,256]{3,2,1,0:T(8,128)(2,1)}, u32[]{:S(2)}) copy-start(bf16[1,2,256,256]{3,2,1,0:T(8,128)(2,1)} %param.8) | copy-start | bytes 786436
  45.3 38.9 %copy-start.5 = (bf16[1,2,256,256]{3,2,1,0:T(8,128)(2,1)S(1)}, bf16[1,2,256,256]{3,2,1,0:T(8,128)(2,1)}, u32[]{:S(2)}) copy-start(bf16[1,2,256,256]{3,2,1,0:T(8,128)(2,1)} %param.9) | copy-start | bytes 786436
  45.8 38.4 %collective-permute-start.23 = (bf16[3,128,256]{2,1,0:T(8,128)(2,1)S(1)}, bf16[3,128,256]{2,1,0:T(8,128)(2,1)S(1)}, u32[]{:S(2)}, u32[]{:S(2)}) collective-permute-start(bf16[3,128,256]{2,1,0:T(8,128)(2,1)S(1)} %get-tuple-element.97), channel_id=1, source_target_pairs={{0,32},{32,0},{64,96},{96,64},{192,224},{224,192},{384,416},{416,3... | collective-permute-start | bytes 589832 | tf_op jit(solution)/shard_map/ppermute | solution.py:442
  51.5 30.5 %collective-permute-start.19 = (bf16[128,256]{1,0:T(8,128)(2,1)S(1)}, bf16[128,256]{1,0:T(8,128)(2,1)S(1)}, u32[]{:S(2)}, u32[]{:S(2)}) collective-permute-start(bf16[128,256]{1,0:T(8,128)(2,1)S(1)} %get-tuple-element.93), channel_id=1, source_target_pairs={{64,0},{96,32},{192,128},{224,160},{384,320},{416,352},{65,1},{97,... | collective-permute-start | bytes 196616 | tf_op jit(solution)/shard_map/ppermute | solution.py:442
  52.8 30.7 %collective-permute-start.20 = (bf16[128,256]{1,0:T(8,128)(2,1)S(1)}, bf16[128,256]{1,0:T(8,128)(2,1)S(1)}, u32[]{:S(2)}, u32[]{:S(2)}) collective-permute-start(bf16[128,256]{1,0:T(8,128)(2,1)S(1)} %get-tuple-element.94), channel_id=1, source_target_pairs={{64,32},{96,0},{192,160},{224,128},{384,352},{416,320},{65,33},{97... | collective-permute-start | bytes 196616 | tf_op jit(solution)/shard_map/ppermute | solution.py:442
  54.1 30.1 %collective-permute-start.15 = (bf16[2,128,256]{2,1,0:T(8,128)(2,1)S(1)}, bf16[2,128,256]{2,1,0:T(8,128)(2,1)S(1)}, u32[]{:S(2)}, u32[]{:S(2)}) collective-permute-start(bf16[2,128,256]{2,1,0:T(8,128)(2,1)S(1)} %get-tuple-element.77), channel_id=1, source_target_pairs={{192,128},{224,160},{384,320},{416,352},{193,129},{225,161},{385,3... | collective-permute-start | bytes 393224 | tf_op jit(solution)/shard_map/ppermute | solution.py:442
  54.8 29.4 %collective-permute-start.16 = (bf16[2,128,256]{2,1,0:T(8,128)(2,1)S(1)}, bf16[2,128,256]{2,1,0:T(8,128)(2,1)S(1)}, u32[]{:S(2)}, u32[]{:S(2)}) collective-permute-start(bf16[2,128,256]{2,1,0:T(8,128)(2,1)S(1)} %get-tuple-element.78), channel_id=1, source_target_pairs={{192,160},{224,128},{384,352},{416,320},{193,161},{225,129},{385,3... | collective-permute-start | bytes 393224 | tf_op jit(solution)/shard_map/ppermute | solution.py:442
  82.0 2.2 %collective-permute-start.21 = (bf16[128,256]{1,0:T(8,128)(2,1)S(1)}, bf16[128,256]{1,0:T(8,128)(2,1)S(1)}, u32[]{:S(2)}, u32[]{:S(2)}) collective-permute-start(bf16[128,256]{1,0:T(8,128)(2,1)S(1)} %get-tuple-element.95), channel_id=1, source_target_pairs={{192,256},{224,288},{384,448},{416,480},{193,257},{225,289},{385,4... | collective-permute-start | bytes 196616 | tf_op jit(solution)/shard_map/ppermute | solution.py:442
  83.5 0.7 collective-permute-start.22
  86.6 29.5 %all-to-all-start = ((bf16[32,16,512]{2,1,0:T(8,128)(2,1)}), bf16[32,16,512]{2,1,0:T(8,128)(2,1)S(1)}, u32[]{:S(2)}, u32[]{:S(2)}) async-start(bf16[32,16,512]{2,1,0:T(8,128)(2,1)} %get-tuple-element.100), calls=%async_computation | async-start | bytes 1048576 | tf_op jit(solution)/shard_map/all_to_all | solution.py:568

commit v4 on v3

--- a/solution.py
+++ b/solution.py
@@ -1,3 +1,5 @@
+import functools
+
 import jax
 import jax.numpy as jnp
 from jax import lax
@@ -98,14 +100,14 @@
             pre_ref[slot, 1] = pre
             out_ref[slot] = after.astype(BF16)
 
-    def backward(self, slot, grad, state_ref, pre_ref, grad_ref):
+    def backward(self, slot, grad, state_ref, pre_ref, grad_ref, kept_from=0):
         grad_ref[...] = grad
 
         def layer(number):
             return layer_backward(
                 grad_ref[...],
-                state_ref[slot, number],
-                pre_ref[slot, number],
+                state_ref[slot - kept_from, number],
+                pre_ref[slot - kept_from, number],
                 self.gain(slot, number),
                 self.first(slot, number),
                 self.second(slot, number),
@@ -139,7 +141,7 @@
         copy.wait()
 
 
-def pair_kernel(chip, x_ref, same, other, outs_ref, last_ref, rows_same, rows_other, packed, states, pres, sems):
+def pair_kernel(chip, x_ref, same, other, outs_ref, skip_ref, rows_same, rows_other, packed, states, pres, sems):
     here, core = position()
 
     def keep(slot, index, value):
@@ -155,34 +157,36 @@
     def _():
         weights = Weights(core, [same, other], packed, sems)
         weights.start(0)
-        state = (x_ref[core] if chip == FIRST else x_ref[...]).astype(F32)
+        state = (x_ref[core] if chip == FIRST else x_ref[1]).astype(F32)
         for slot in range(2):
             weights.wait(slot)
             weights.forward(slot, state, states, pres, outs_ref)
             keep(slot, 0, outs_ref[slot])
             keep(slot, 1, state.astype(BF16))
             state = outs_ref[slot].astype(F32)
-        last_ref[...] = outs_ref[1]
-
-
-def middle_forward_kernel(hop_ref, *refs):
-    refs, (outs_ref, inflow_ref, hop_out, state_ref, pre_ref, packed, sems) = refs[:6], refs[6:]
+        if chip == SECOND:
+            skip_ref[:2] = x_ref[...]
+            skip_ref[2:] = outs_ref[...]
+
+
+def middle_forward_kernel(first_slot, hop_ref, *refs):
+    before, refs = (refs[0], refs[1:]) if first_slot else (None, refs)
+    pairs = 1 if first_slot else 2
+    refs, (outs_ref, inflow_ref, state_ref, pre_ref, packed, sems) = refs[: 2 * pairs], refs[2 * pairs :]
     here, core = position()
 
     @pl.when(here == MIDDLE)
     def _():
         weights = Weights(core, refs, packed, sems)
-        for pair in range(3):
+        for pair in range(pairs):
             weights.start(pair)
-        for slot in range(6):
+        for slot in range(2 * pairs):
             weights.wait(slot)
             state = (hop_ref[...] if slot == 0 else outs_ref[slot - 1]).astype(F32)
-            if slot >= 4:
-                state = state + outs_ref[7 - slot].astype(F32)
+            if first_slot:
+                state = state + before[3 - slot].astype(F32)
             inflow_ref[slot] = state.astype(BF16)
             weights.forward(slot, state, state_ref, pre_ref, outs_ref)
-        hop_out[0] = outs_ref[5]
-        hop_out[1:] = outs_ref[:2]
 
 
 def store_by_owner(core, slot, refs, index, value):
@@ -198,26 +202,26 @@
         other[index] = value
 
 
-def last_kernel(hop_ref, skip0_ref, skip1_ref, ct_ref, outs_in, inflow_in, *refs):
+def last_kernel(hop_ref, skip2_ref, skip_ref, ct_ref, outs_low, outs_high, rows_low, rows_high, *refs):
     refs, refs_out = refs[:6], refs[6:]
     owners, (hop_out, sent_out, up_ref) = refs_out[:6], refs_out[6:9]
     packed, outs_ref, inflow_ref, state_ref, pre_ref, sent_ref, grad_ref, sems = refs_out[9:]
     here, core = position()
 
     def keep_rows(slots, outs, inflows):
-        for slot in slots:
-            store_by_owner(core, slot, owners, 0, outs[slot])
-            store_by_owner(core, slot, owners, 1, inflows[slot])
+        for index, slot in enumerate(slots):
+            store_by_owner(core, slot, owners, 0, outs[index])
+            store_by_owner(core, slot, owners, 1, inflows[index])
 
     @pl.when(here == LAST)
     def _():
         weights = Weights(core, refs, packed, sems)
         for pair in range(3):
             weights.start(pair)
-        skips = [hop_ref.at[2], hop_ref.at[1]] + [ref.at[index] for ref in (skip1_ref, skip0_ref) for index in (1, 0)]
+        skips = [skip2_ref.at[index] for index in (1, 0)] + [skip_ref.at[index] for index in (3, 2, 1, 0)]
         for slot in range(6):
             weights.wait(slot)
-            state = (hop_ref[0] if slot == 0 else outs_ref[slot - 1]).astype(F32)
+            state = (hop_ref[...] if slot == 0 else outs_ref[slot - 1]).astype(F32)
             state = state + skips[slot][...].astype(F32)
             inflow_ref[slot] = state.astype(BF16)
             weights.forward(slot, state, state_ref, pre_ref, outs_ref)
@@ -231,11 +235,12 @@
 
     @pl.when(here == MIDDLE)
     def _():
-        keep_rows(range(6), outs_in, inflow_in)
-
-
-def middle_backward_kernel(hop_ref, state_ref, pre_ref, x_ref, *refs):
-    refs, low_refs, refs_out = refs[:6], refs[6:8] + refs[2:4], refs[8:]
+        keep_rows(range(4), outs_low, rows_low)
+        keep_rows(range(4, 6), outs_high, rows_high)
+
+
+def middle_backward_kernel(hop_ref, state_low, pre_low, state_high, pre_high, x_ref, *refs):
+    refs, low_refs, refs_out = refs[:6], refs[6:10], refs[10:]
     hop_out, up_ref, low_state, low_pre, packed, sent_ref, grad_ref, sems = refs_out
     here, core = position()
 
@@ -261,7 +266,10 @@
             if slot < 4:
                 grad = grad + skips[slot][...].astype(F32)
             up_ref[slot] = grad.astype(BF16)
-            sent_ref[slot] = weights.backward(slot, grad, state_ref, pre_ref, grad_ref)
+            if slot < 4:
+                sent_ref[slot] = weights.backward(slot, grad, state_low, pre_low, grad_ref)
+            else:
+                sent_ref[slot] = weights.backward(slot, grad, state_high, pre_high, grad_ref, 4)
         hop_out[...] = sent_ref[0]
 
 
@@ -465,7 +473,7 @@
         [pltpu.VMEM((16, C), BF16), dma((5,))],
     )
     holders = (MIDDLE, LAST)
-    partner = move(own, [(chip, chip) for chip in (FIRST, SECOND, MIDDLE, LAST)], cross=True)
+    low_own = move(own, [(chip, chip) for chip in (FIRST, SECOND)], cross=True)
     left = move(own, [(chip - 1, chip) for chip in holders])
     right = move(own, [(chip + 1, chip) for chip in holders])
 
@@ -473,40 +481,46 @@
         return call(
             lambda *refs: pair_kernel(chip, *refs),
             "pair_forward",
-            at_vmem(value) + at_hbm(own, partner),
-            [((2,) + tile, BF16), (tile, BF16)] + [((2,) + tile, BF16)] * 2,
+            at_vmem(value) + at_hbm(own, low_own),
+            [((2,) + tile, BF16), ((4,) + tile, BF16)] + [((2,) + tile, BF16)] * 2,
             [packed_scratch(2), kept(2, pixels), kept(2, pixels), dma((2,))],
         )
 
-    outs_a, last_a, *rows_a = pair(FIRST, images)
-    outs_b, last_b, *rows_b = pair(SECOND, move(last_a, [(FIRST, SECOND)]))
-    hop = move(last_b, [(SECOND, MIDDLE)])
-    left, right, later, hop = barrier((left, right, own, hop))
+    outs_a, _, *rows_a = pair(FIRST, images)
+    outs_b, skip, *rows_b = pair(SECOND, move(outs_a, [(FIRST, SECOND)]))
+    hop = move(outs_b[1], [(SECOND, MIDDLE)])
+    partner = move(barrier((own, low_own))[0], [(chip, chip) for chip in holders], cross=True)
+    left, right, later, partner, hop = barrier((left, right, own, partner, hop))
     left_partner = move(left, [(chip, chip) for chip in holders], cross=True)
     right_partner = move(right, [(chip, chip) for chip in holders], cross=True)
     weights = at_hbm(left, left_partner, own, partner, right, right_partner)
-    four, six = (4,) + tile, (6,) + tile
-    four_state, six_state = (4, 2) + tile, (6, 2) + tile
-
-    outs, inflows, hop, states, pres = call(
-        middle_forward_kernel,
-        "middle_forward",
-        at_vmem(hop) + weights,
-        [(six, BF16), (six, BF16), ((3,) + tile, BF16), (six_state, F32), (six_state, F32)],
-        [packed_scratch(6), dma((6,))],
-        us=3,
-    )
-    skip0, skip1, hop = barrier((outs_a, outs_b, hop))
+    four, six, four_state = (4,) + tile, (6,) + tile, (4, 2) + tile
+
+    def middle(first_slot, slots, value, refs):
+        slots, state_shape = (slots,) + tile, (slots, 2) + tile
+        return call(
+            functools.partial(middle_forward_kernel, first_slot),
+            "middle_forward",
+            at_vmem(*value) + refs,
+            [(slots, BF16), (slots, BF16), (state_shape, F32), (state_shape, F32)],
+            [packed_scratch(slots[0]), dma((slots[0],))],
+            us=slots[0] // 2,
+        )
+
+    outs_low, *kept_low = middle(0, 4, [hop], weights[:4])
+    outs_high, *kept_high = middle(4, 2, [outs_low[3], outs_low], weights[4:])
+    skip2 = move(outs_low[:2], [(MIDDLE, LAST)])
+    hop = outs_high[1]
+    skip, hop = barrier((skip, hop))
     hop = move(hop, [(MIDDLE, LAST)])
-    skip0 = move(skip0, [(FIRST, LAST)])
-    skip1 = move(skip1, [(SECOND, LAST)])
+    skip = move(skip, [(SECOND, LAST)])
     low_left = move(later, [(SECOND - 1, SECOND)])
     low_partner = move(low_left, [(SECOND, SECOND)], cross=True)
-    low_weights = at_hbm(low_left, low_partner, own, partner)
+    low_weights = at_hbm(low_left, low_partner, own, low_own)
     *to_owners, hop, skips, ups_last = call(
         last_kernel,
         "last_both",
-        at_vmem(hop, skip0, skip1, cotangent, outs, inflows) + weights,
+        at_vmem(hop, skip2, skip, cotangent, outs_low, outs_high, kept_low[0], kept_high[0]) + weights,
         [((2,) + tile, BF16)] * 6 + [((2,) + tile, BF16), (four, BF16), (six, BF16)],
         [
             packed_scratch(6),
@@ -535,15 +549,14 @@
     hop, ups_middle, low_states, low_pres = call(
         middle_backward_kernel,
         "middle_backward",
-        at_vmem(hop, states, pres, images) + weights + low_weights[:2],
+        at_vmem(hop, *kept_low[1:], *kept_high[1:], images) + weights + low_weights,
         [(tile, BF16), (six, BF16), (four_state, F32), (four_state, F32)],
         [packed_scratch(6), pltpu.VMEM(six, BF16), pltpu.VMEM(tile, F32), dma((6,))],
         us=5,
     )
     rows_left, hop = barrier((rows_left, hop))
     hop = move(hop, [(MIDDLE, SECOND)])
-    rows_left = deliver((MIDDLE, LAST), *rows_left, None, None)
-    rows = rows_left + rows_right
+    rows = deliver((MIDDLE, LAST), *rows_left) + rows_right
     *away, own_other, own_same = call(
         first_backward_kernel,
         "first_backward",

time: 118 us -> 115 us (0.975)
  the two profiles are of different devices: /device:TPU:1 before, /device:TPU:16 now
where the time goes in v4:
time: 115 us; the launch traced here: 114 us
  waiting for transfers between devices  72.5 us (63%)
  starting transfers between devices  32.8 us (29%)
  Pallas kernels  4.63 us (4%)
  local copies, waits for them, and re-layouts  2.7 us (2%)
  between operations  1.77 us (2%)
    ppermute x25, waiting for transfers between devices, move(): return lax.ppermute(value, 'section', pairs)  54.2 us
    ppermute x25, starting transfers between devices, move(): return lax.ppermute(value, 'section', pairs)  22.5 us
    all_to_all x1, waiting for transfers between devices, body(): parts = lax.all_to_all(parts, 'dp', 0, 0, tiled=True)  18.3 us
    all_to_all x1, starting transfers between devices, body(): parts = lax.all_to_all(parts, 'dp', 0, 0, tiled=True)  10.3 us
    pallas_call x10, Pallas kernels, call(): pl.pallas_call(kernel, out_shape=outputs, in_specs=[specs[memory]() for m...  4.63 us
    unnamed x14, local copies, waits for them, and re-layouts  2.6 us
  transfers between devices with their start and end apart: 26, of which 6 were waited for; matrix products, arithmetic and copies ran while one was open for 0% of the time, Pallas kernels for 1%

profile of v4, /device:TPU:16, one launch (start us, length us, event | category | flops | bytes accessed | tf_op | source)
XLA Modules:
  0.0 114.4 jit_solution(17293200743511528804)
XLA Ops:
  1.3 0.7 copy-done
  2.0 0.9 copy-done.1
  2.9 0.9 copy-done.3
  3.9 0.7 pack.1.refs_1_.refs_2_.refs_8_
  4.6 0.7 collective-permute-start
  5.3 3.5 %collective-permute-start.2 = (bf16[1040,256]{1,0:T(8,128)(2,1)S(1)}, bf16[1040,256]{1,0:T(8,128)(2,1)S(1)}, u32[]{:S(2)}, u32[]{:S(2)}) collective-permute-start(bf16[1040,256]{1,0:T(8,128)(2,1)S(1)} %pack.1.refs_1_.refs_2_.refs_8_), channel_id=1, source_target_pairs={{128,192},{160,224},{320,384},{352,416},{129,193},{161,225},{321,3... | collective-permute-start | bytes 1597448 | tf_op jit(solution)/shard_map/ppermute | solution.py:450
  8.8 0.7 collective-permute-start.3
  9.5 0.0 collective-permute-done.refs_2_.refs_9_
  9.5 0.7 collective-permute-start.4
  10.3 0.7 pair_forward.2
  11.0 0.7 collective-permute-start.1
  11.7 0.0 collective-permute-done.1.refs_0_
  11.7 0.7 collective-permute-start.5
  12.4 7.7 %collective-permute-done.2.refs_0_ = bf16[1040,256]{1,0:T(8,128)(2,1)S(1)} collective-permute-done((bf16[1040,256]{1,0:T(8,128)(2,1)S(1)}, bf16[1040,256]{1,0:T(8,128)(2,1)S(1)}, u32[]{:S(2)}, u32[]{:S(2)}) %collective-permute-start.2) | collective-permute-done | bytes 532512 | tf_op jit(solution)/shard_map/ppermute | solution.py:450
  20.1 0.0 collective-permute-done.3.refs_1_.refs_4_
  20.1 0.0 collective-permute-done.5.hop_ref
  20.1 0.0 collective-permute-done.4.refs_3_
  20.1 0.7 collective-permute-start.6
  20.8 0.7 collective-permute-start.7
  21.6 0.7 collective-permute-start.14
  22.3 0.0 collective-permute-done.6.refs_1_
  22.3 0.1 middle_forward.2
  22.3 0.0 collective-permute-done.7.refs_2_.refs_5_
  22.4 0.0 copy-start.5
  22.4 0.8 collective-permute-start.10
  23.3 0.7 collective-permute-start.9
  23.9 0.7 collective-permute-start.8
  24.6 0.0 collective-permute-done.14.refs_6_
  24.6 0.7 collective-permute-start.15
  25.3 0.0 collective-permute-done.8.hop_ref
  25.3 0.0 collective-permute-done.9.skip2_ref
  25.4 0.0 collective-permute-done.10.skip_ref
  25.4 0.1 last_both.1
  25.5 0.7 collective-permute-start.11
  26.1 0.7 collective-permute-start.12
  26.8 0.7 collective-permute-start.13
  27.5 0.7 collective-permute-start.19
  28.2 0.0 collective-permute-done.11.hop_ref
  28.2 0.0 collective-permute-done.12.refs_2_
  28.2 0.0 collective-permute-done.13.refs_3_
  28.2 0.3 middle_backward.1
  28.5 0.7 collective-permute-start.18
  29.2 0.0 collective-permute-done.19.skip_ref
  29.2 0.0 collective-permute-done.18.hop_ref
  29.2 0.0 copy-start.2
  29.2 0.0 copy-start.4
  29.2 0.1 first_backward.1
  29.3 0.8 collective-permute-start.24
  30.1 1.3 %collective-permute-start.20 = (bf16[128,256]{1,0:T(8,128)(2,1)S(1)}, bf16[128,256]{1,0:T(8,128)(2,1)S(1)}, u32[]{:S(2)}, u32[]{:S(2)}) collective-permute-start(bf16[128,256]{1,0:T(8,128)(2,1)S(1)} %get-tuple-element.99), channel_id=1, source_target_pairs={{64,0},{96,32},{192,128},{224,160},{384,320},{416,352},{65,1},{97,... | collective-permute-start | bytes 196616 | tf_op jit(solution)/shard_map/ppermute | solution.py:450
  31.4 1.3 %collective-permute-start.21 = (bf16[128,256]{1,0:T(8,128)(2,1)S(1)}, bf16[128,256]{1,0:T(8,128)(2,1)S(1)}, u32[]{:S(2)}, u32[]{:S(2)}) collective-permute-start(bf16[128,256]{1,0:T(8,128)(2,1)S(1)} %get-tuple-element.100), channel_id=1, source_target_pairs={{64,32},{96,0},{192,160},{224,128},{384,352},{416,320},{65,33},{97... | collective-permute-start | bytes 196616 | tf_op jit(solution)/shard_map/ppermute | solution.py:450
  32.8 1.3 %collective-permute-start.16 = (bf16[2,128,256]{2,1,0:T(8,128)(2,1)S(1)}, bf16[2,128,256]{2,1,0:T(8,128)(2,1)S(1)}, u32[]{:S(2)}, u32[]{:S(2)}) collective-permute-start(bf16[2,128,256]{2,1,0:T(8,128)(2,1)S(1)} %get-tuple-element.83), channel_id=1, source_target_pairs={{192,128},{224,160},{384,320},{416,352},{193,129},{225,161},{385,3... | collective-permute-start | bytes 393224 | tf_op jit(solution)/shard_map/ppermute | solution.py:450
  34.0 1.3 %collective-permute-start.17 = (bf16[2,128,256]{2,1,0:T(8,128)(2,1)S(1)}, bf16[2,128,256]{2,1,0:T(8,128)(2,1)S(1)}, u32[]{:S(2)}, u32[]{:S(2)}) collective-permute-start(bf16[2,128,256]{2,1,0:T(8,128)(2,1)S(1)} %get-tuple-element.84), channel_id=1, source_target_pairs={{192,160},{224,128},{384,352},{416,320},{193,161},{225,129},{385,3... | collective-permute-start | bytes 393224 | tf_op jit(solution)/shard_map/ppermute | solution.py:450
  35.4 41.0 %collective-permute-done.20.refs_4_ = bf16[128,256]{1,0:T(8,128)(2,1)S(1)} collective-permute-done((bf16[128,256]{1,0:T(8,128)(2,1)S(1)}, bf16[128,256]{1,0:T(8,128)(2,1)S(1)}, u32[]{:S(2)}, u32[]{:S(2)}) %collective-permute-start.20) | collective-permute-done | bytes 65568 | tf_op jit(solution)/shard_map/ppermute | solution.py:450
  76.3 0.7 collective-permute-start.22
  77.0 0.6 collective-permute-done.21.refs_5_
  77.5 0.7 collective-permute-start.23
  78.2 0.0 collective-permute-done.23.refs_7_
  78.2 2.3 %collective-permute-done.16.refs_0_ = bf16[2,128,256]{2,1,0:T(8,128)(2,1)S(1)} collective-permute-done((bf16[2,128,256]{2,1,0:T(8,128)(2,1)S(1)}, bf16[2,128,256]{2,1,0:T(8,128)(2,1)S(1)}, u32[]{:S(2)}, u32[]{:S(2)}) %collective-permute-start.16) | collective-permute-done | bytes 131104 | tf_op jit(solution)/shard_map/ppermute | solution.py:450
  80.5 2.6 %collective-permute-done.17.refs_1_ = bf16[2,128,256]{2,1,0:T(8,128)(2,1)S(1)} collective-permute-done((bf16[2,128,256]{2,1,0:T(8,128)(2,1)S(1)}, bf16[2,128,256]{2,1,0:T(8,128)(2,1)S(1)}, u32[]{:S(2)}, u32[]{:S(2)}) %collective-permute-start.17) | collective-permute-done | bytes 131104 | tf_op jit(solution)/shard_map/ppermute | solution.py:450
  83.2 1.8 %owner_gradients.1 = (bf16[2,128,256]{2,1,0:T(8,128)(2,1)}, bf16[32,16,512]{2,1,0:T(8,128)(2,1)}) custom-call(s32[1]{0:T(128)S(6)} %copy.10.counts, f32[2,256]{1,0:T(2,128)S(1)} %bitcast.19, bf16[2,256,256]{2,1,0:T(8,128)(2,1)S(1)} %bitcast.21, bf16[2,256,256]{2,1,0:T(8,128)(2,1)S(1)} %bitcast.23, bf16[2,128,256]{2,1,0:T(8,128)(2,1)S(1)} %collective-permute-done.16.refs_0_, ...), custom_call_target="tpu_custom_call" | custom-call | flops 1000000000 | bytes 1048576 | tf_op jit(solution)/shard_map/owner_gradients/pallas_call | solution.py:428
  85.0 10.3 %all-to-all-start = ((bf16[32,16,512]{2,1,0:T(8,128)(2,1)}), bf16[32,16,512]{2,1,0:T(8,128)(2,1)S(1)}, u32[]{:S(2)}, u32[]{:S(2)}) async-start(bf16[32,16,512]{2,1,0:T(8,128)(2,1)} %get-tuple-element.106), calls=%async_computation | async-start | bytes 1048576 | tf_op jit(solution)/shard_map/all_to_all | solution.py:581
  95.3 0.1 dynamic-slice_bitcast_fusion.g_ref
  95.4 18.3 %all-to-all-done.parts_ref = bf16[32,16,512]{2,1,0:T(8,128)(2,1)S(1)} async-done(((bf16[32,16,512]{2,1,0:T(8,128)(2,1)}), bf16[32,16,512]{2,1,0:T(8,128)(2,1)S(1)}, u32[]{:S(2)}, u32[]{:S(2)}) %all-to-all-start) | async-done | bytes 524320 | tf_op jit(solution)/shard_map/all_to_all | solution.py:581
  113.7 0.8 sum_parts.1
  (18 shorter events, 0.1 us)
Async XLA Ops:
  1.3 0.7 copy-start
  2.0 0.9 copy-start.1
  2.9 0.9 copy-start.3
  3.9 6.4 %copy-start.6 = (bf16[2,128,256]{2,1,0:T(8,128)(2,1)S(1)}, bf16[2,128,256]{2,1,0:T(8,128)(2,1)}, u32[]{:S(2)}) copy-start(bf16[2,128,256]{2,1,0:T(8,128)(2,1)} %x_ref.1) | copy-start | bytes 393220
  4.6 4.9 %collective-permute-start = (bf16[1040,256]{1,0:T(8,128)(2,1)S(1)}, bf16[1040,256]{1,0:T(8,128)(2,1)S(1)}, u32[]{:S(2)}, u32[]{:S(2)}) collective-permute-start(bf16[1040,256]{1,0:T(8,128)(2,1)S(1)} %pack.1.refs_1_.refs_2_.refs_8_), channel_id=1, source_target_pairs={{0,32},{32,0},{64,96},{96,64},{1,33},{33,1},{65,97},{97,65},{2,34}... | collective-permute-start | bytes 1597448 | tf_op jit(solution)/shard_map/ppermute | solution.py:450
  5.3 14.8 %collective-permute-start.2 = (bf16[1040,256]{1,0:T(8,128)(2,1)S(1)}, bf16[1040,256]{1,0:T(8,128)(2,1)S(1)}, u32[]{:S(2)}, u32[]{:S(2)}) collective-permute-start(bf16[1040,256]{1,0:T(8,128)(2,1)S(1)} %pack.1.refs_1_.refs_2_.refs_8_), channel_id=1, source_target_pairs={{128,192},{160,224},{320,384},{352,416},{129,193},{161,225},{321,3... | collective-permute-start | bytes 1597448 | tf_op jit(solution)/shard_map/ppermute | solution.py:450
  8.8 11.3 %collective-permute-start.3 = (bf16[1040,256]{1,0:T(8,128)(2,1)S(1)}, bf16[1040,256]{1,0:T(8,128)(2,1)S(1)}, u32[]{:S(2)}, u32[]{:S(2)}) collective-permute-start(bf16[1040,256]{1,0:T(8,128)(2,1)S(1)} %pack.1.refs_1_.refs_2_.refs_8_), channel_id=1, source_target_pairs={{256,192},{288,224},{448,384},{480,416},{257,193},{289,225},{449,3... | collective-permute-start | bytes 1597448 | tf_op jit(solution)/shard_map/ppermute | solution.py:450
  9.5 10.6 %collective-permute-start.4 = (bf16[1040,256]{1,0:T(8,128)(2,1)S(1)}, bf16[1040,256]{1,0:T(8,128)(2,1)S(1)}, u32[]{:S(2)}, u32[]{:S(2)}) collective-permute-start(bf16[1040,256]{1,0:T(8,128)(2,1)S(1)} %pack.1.refs_1_.refs_2_.refs_8_), channel_id=1, source_target_pairs={{192,224},{224,192},{384,416},{416,384},{193,225},{225,193},{385,4... | collective-permute-start | bytes 1597448 | tf_op jit(solution)/shard_map/ppermute | solution.py:450
  11.0 0.7 collective-permute-start.1
  11.7 8.4 %collective-permute-start.5 = (bf16[128,256]{1,0:T(8,128)(2,1)S(1)}, bf16[128,256]{1,0:T(8,128)(2,1)S(1)}, u32[]{:S(2)}, u32[]{:S(2)}) collective-permute-start(bf16[128,256]{1,0:T(8,128)(2,1)S(1)} %slice_bitcast_fusion.2), channel_id=1, source_target_pairs={{64,192},{96,224},{65,193},{97,225},{66,194},{98,226},{67,195},{99... | collective-permute-start | bytes 196616 | tf_op jit(solution)/shard_map/ppermute | solution.py:450
  20.1 2.1 %collective-permute-start.6 = (bf16[1040,256]{1,0:T(8,128)(2,1)S(1)}, bf16[1040,256]{1,0:T(8,128)(2,1)S(1)}, u32[]{:S(2)}, u32[]{:S(2)}) collective-permute-start(bf16[1040,256]{1,0:T(8,128)(2,1)S(1)} %collective-permute-done.2.refs_0_), channel_id=1, source_target_pairs={{192,224},{224,192},{384,416},{416,384},{193,225},{225,193},{385,4... | collective-permute-start | bytes 1597448 | tf_op jit(solution)/shard_map/ppermute | solution.py:450
  20.8 1.5 %collective-permute-start.7 = (bf16[1040,256]{1,0:T(8,128)(2,1)S(1)}, bf16[1040,256]{1,0:T(8,128)(2,1)S(1)}, u32[]{:S(2)}, u32[]{:S(2)}) collective-permute-start(bf16[1040,256]{1,0:T(8,128)(2,1)S(1)} %collective-permute-done.3.refs_1_.refs_4_), channel_id=1, source_target_pairs={{192,224},{224,192},{384,416},{416,384},{193,225},{225,193},{385,4... | collective-permute-start | bytes 1597448 | tf_op jit(solution)/shard_map/ppermute | solution.py:450
  21.6 3.1 %collective-permute-start.14 = (bf16[1040,256]{1,0:T(8,128)(2,1)S(1)}, bf16[1040,256]{1,0:T(8,128)(2,1)S(1)}, u32[]{:S(2)}, u32[]{:S(2)}) collective-permute-start(bf16[1040,256]{1,0:T(8,128)(2,1)S(1)} %pack.1.refs_1_.refs_2_.refs_8_), channel_id=1, source_target_pairs={{0,64},{32,96},{1,65},{33,97},{2,66},{34,98},{3,67},{35,99},{4,68}... | collective-permute-start | bytes 1597448 | tf_op jit(solution)/shard_map/ppermute | solution.py:450
  22.4 2.9 %copy-start.5 = (bf16[2,128,256]{2,1,0:T(8,128)(2,1)S(1)}, bf16[2,128,256]{2,1,0:T(8,128)(2,1)}, u32[]{:S(2)}) copy-start(bf16[2,128,256]{2,1,0:T(8,128)(2,1)} %ct_ref.1) | copy-start | bytes 393220
  22.4 2.9 %collective-permute-start.10 = (bf16[4,128,256]{2,1,0:T(8,128)(2,1)S(1)}, bf16[4,128,256]{2,1,0:T(8,128)(2,1)S(1)}, u32[]{:S(2)}, u32[]{:S(2)}) collective-permute-start(bf16[4,128,256]{2,1,0:T(8,128)(2,1)S(1)} %get-tuple-element.68), channel_id=1, source_target_pairs={{64,384},{96,416},{65,385},{97,417},{66,386},{98,418},{67,387},{99... | collective-permute-start | bytes 786440 | tf_op jit(solution)/shard_map/ppermute | solution.py:450
  23.3 2.1 %collective-permute-start.9 = (bf16[2,128,256]{2,1,0:T(8,128)(2,1)S(1)}, bf16[2,128,256]{2,1,0:T(8,128)(2,1)S(1)}, u32[]{:S(2)}, u32[]{:S(2)}) collective-permute-start(bf16[2,128,256]{2,1,0:T(8,128)(2,1)S(1)} %slice.15), channel_id=1, source_target_pairs={{192,384},{224,416},{193,385},{225,417},{194,386},{226,418},{195,3... | collective-permute-start | bytes 393224 | tf_op jit(solution)/shard_map/ppermute | solution.py:450
  23.9 1.4 %collective-permute-start.8 = (bf16[128,256]{1,0:T(8,128)(2,1)S(1)}, bf16[128,256]{1,0:T(8,128)(2,1)S(1)}, u32[]{:S(2)}, u32[]{:S(2)}) collective-permute-start(bf16[128,256]{1,0:T(8,128)(2,1)S(1)} %slice_bitcast_fusion), channel_id=1, source_target_pairs={{192,384},{224,416},{193,385},{225,417},{194,386},{226,418},{195,3... | collective-permute-start | bytes 196616 | tf_op jit(solution)/shard_map/ppermute | solution.py:450
  24.6 3.6 %collective-permute-start.15 = (bf16[1040,256]{1,0:T(8,128)(2,1)S(1)}, bf16[1040,256]{1,0:T(8,128)(2,1)S(1)}, u32[]{:S(2)}, u32[]{:S(2)}) collective-permute-start(bf16[1040,256]{1,0:T(8,128)(2,1)S(1)} %collective-permute-done.14.refs_6_), channel_id=1, source_target_pairs={{64,96},{96,64},{65,97},{97,65},{66,98},{98,66},{67,99},{99,67},{6... | collective-permute-start | bytes 1597448 | tf_op jit(solution)/shard_map/ppermute | solution.py:450
  25.5 2.7 %collective-permute-start.11 = (bf16[2,128,256]{2,1,0:T(8,128)(2,1)S(1)}, bf16[2,128,256]{2,1,0:T(8,128)(2,1)S(1)}, u32[]{:S(2)}, u32[]{:S(2)}) collective-permute-start(bf16[2,128,256]{2,1,0:T(8,128)(2,1)S(1)} %get-tuple-element.73), channel_id=1, source_target_pairs={{384,192},{416,224},{385,193},{417,225},{386,194},{418,226},{387,1... | collective-permute-start | bytes 393224 | tf_op jit(solution)/shard_map/ppermute | solution.py:450
  26.1 2.1 %collective-permute-start.12 = (bf16[2,128,256]{2,1,0:T(8,128)(2,1)S(1)}, bf16[2,128,256]{2,1,0:T(8,128)(2,1)S(1)}, u32[]{:S(2)}, u32[]{:S(2)}) collective-permute-start(bf16[2,128,256]{2,1,0:T(8,128)(2,1)S(1)} %get-tuple-element.74), channel_id=1, source_target_pairs={{192,256},{224,288},{384,448},{416,480},{193,257},{225,289},{385,4... | collective-permute-start | bytes 393224 | tf_op jit(solution)/shard_map/ppermute | solution.py:450
  26.8 1.4 %collective-permute-start.13 = (bf16[2,128,256]{2,1,0:T(8,128)(2,1)S(1)}, bf16[2,128,256]{2,1,0:T(8,128)(2,1)S(1)}, u32[]{:S(2)}, u32[]{:S(2)}) collective-permute-start(bf16[2,128,256]{2,1,0:T(8,128)(2,1)S(1)} %get-tuple-element.75), channel_id=1, source_target_pairs={{192,288},{224,256},{384,480},{416,448},{193,289},{225,257},{385,4... | collective-permute-start | bytes 393224 | tf_op jit(solution)/shard_map/ppermute | solution.py:450
  27.5 1.7 %collective-permute-start.19 = (bf16[4,128,256]{2,1,0:T(8,128)(2,1)S(1)}, bf16[4,128,256]{2,1,0:T(8,128)(2,1)S(1)}, u32[]{:S(2)}, u32[]{:S(2)}) collective-permute-start(bf16[4,128,256]{2,1,0:T(8,128)(2,1)S(1)} %get-tuple-element.88), channel_id=1, source_target_pairs={{384,64},{416,96},{385,65},{417,97},{386,66},{418,98},{387,67},{41... | collective-permute-start | bytes 786440 | tf_op jit(solution)/shard_map/ppermute | solution.py:450
  28.5 0.7 collective-permute-start.18
  29.2 54.0 %copy-start.2 = (bf16[1,2,256,256]{3,2,1,0:T(8,128)(2,1)S(1)}, bf16[1,2,256,256]{3,2,1,0:T(8,128)(2,1)}, u32[]{:S(2)}) copy-start(bf16[1,2,256,256]{3,2,1,0:T(8,128)(2,1)} %param.8) | copy-start | bytes 786436
  29.2 53.9 %copy-start.4 = (bf16[1,2,256,256]{3,2,1,0:T(8,128)(2,1)S(1)}, bf16[1,2,256,256]{3,2,1,0:T(8,128)(2,1)}, u32[]{:S(2)}) copy-start(bf16[1,2,256,256]{3,2,1,0:T(8,128)(2,1)} %param.9) | copy-start | bytes 786436
  29.3 53.8 %collective-permute-start.24 = (bf16[3,128,256]{2,1,0:T(8,128)(2,1)S(1)}, bf16[3,128,256]{2,1,0:T(8,128)(2,1)S(1)}, u32[]{:S(2)}, u32[]{:S(2)}) collective-permute-start(bf16[3,128,256]{2,1,0:T(8,128)(2,1)S(1)} %get-tuple-element.103), channel_id=1, source_target_pairs={{0,32},{32,0},{64,96},{96,64},{192,224},{224,192},{384,416},{416,3... | collective-permute-start | bytes 589832 | tf_op jit(solution)/shard_map/ppermute | solution.py:450
  30.1 46.2 %collective-permute-start.20 = (bf16[128,256]{1,0:T(8,128)(2,1)S(1)}, bf16[128,256]{1,0:T(8,128)(2,1)S(1)}, u32[]{:S(2)}, u32[]{:S(2)}) collective-permute-start(bf16[128,256]{1,0:T(8,128)(2,1)S(1)} %get-tuple-element.99), channel_id=1, source_target_pairs={{64,0},{96,32},{192,128},{224,160},{384,320},{416,352},{65,1},{97,... | collective-permute-start | bytes 196616 | tf_op jit(solution)/shard_map/ppermute | solution.py:450
  31.4 46.1 %collective-permute-start.21 = (bf16[128,256]{1,0:T(8,128)(2,1)S(1)}, bf16[128,256]{1,0:T(8,128)(2,1)S(1)}, u32[]{:S(2)}, u32[]{:S(2)}) collective-permute-start(bf16[128,256]{1,0:T(8,128)(2,1)S(1)} %get-tuple-element.100), channel_id=1, source_target_pairs={{64,32},{96,0},{192,160},{224,128},{384,352},{416,320},{65,33},{97... | collective-permute-start | bytes 196616 | tf_op jit(solution)/shard_map/ppermute | solution.py:450
  32.8 47.8 %collective-permute-start.16 = (bf16[2,128,256]{2,1,0:T(8,128)(2,1)S(1)}, bf16[2,128,256]{2,1,0:T(8,128)(2,1)S(1)}, u32[]{:S(2)}, u32[]{:S(2)}) collective-permute-start(bf16[2,128,256]{2,1,0:T(8,128)(2,1)S(1)} %get-tuple-element.83), channel_id=1, source_target_pairs={{192,128},{224,160},{384,320},{416,352},{193,129},{225,161},{385,3... | collective-permute-start | bytes 393224 | tf_op jit(solution)/shard_map/ppermute | solution.py:450
  34.0 49.1 %collective-permute-start.17 = (bf16[2,128,256]{2,1,0:T(8,128)(2,1)S(1)}, bf16[2,128,256]{2,1,0:T(8,128)(2,1)S(1)}, u32[]{:S(2)}, u32[]{:S(2)}) collective-permute-start(bf16[2,128,256]{2,1,0:T(8,128)(2,1)S(1)} %get-tuple-element.84), channel_id=1, source_target_pairs={{192,160},{224,128},{384,352},{416,320},{193,161},{225,129},{385,3... | collective-permute-start | bytes 393224 | tf_op jit(solution)/shard_map/ppermute | solution.py:450
  76.3 1.9 %collective-permute-start.22 = (bf16[128,256]{1,0:T(8,128)(2,1)S(1)}, bf16[128,256]{1,0:T(8,128)(2,1)S(1)}, u32[]{:S(2)}, u32[]{:S(2)}) collective-permute-start(bf16[128,256]{1,0:T(8,128)(2,1)S(1)} %get-tuple-element.101), channel_id=1, source_target_pairs={{192,256},{224,288},{384,448},{416,480},{193,257},{225,289},{385,4... | collective-permute-start | bytes 196616 | tf_op jit(solution)/shard_map/ppermute | solution.py:450
  77.5 0.7 collective-permute-start.23
  85.0 28.7 %all-to-all-start = ((bf16[32,16,512]{2,1,0:T(8,128)(2,1)}), bf16[32,16,512]{2,1,0:T(8,128)(2,1)S(1)}, u32[]{:S(2)}, u32[]{:S(2)}) async-start(bf16[32,16,512]{2,1,0:T(8,128)(2,1)} %get-tuple-element.106), calls=%async_computation | async-start | bytes 1048576 | tf_op jit(solution)/shard_map/all_to_all | solution.py:581

commit v5 on v4

--- a/solution.py
+++ b/solution.py
@@ -120,23 +120,29 @@
         return layer(0).astype(BF16)
 
 
-def pack_kernel(counts, w_in_ref, w_out_ref, g_ref, packed_ref, tail_ref, sems):
+def pack_kernel(counts, w_in_ref, w_out_ref, g_ref, packed_ref, gains_ref, sems):
     copies = [
-        pltpu.make_async_copy(ref.at[layer], packed_ref.at[pl.ds((2 * side + layer) * C, C)], sems.at[2 * side + layer])
+        pltpu.make_async_copy(
+            ref.at[layer, pl.ds(part * C // 2, C // 2)],
+            packed_ref.at[pl.ds((2 * side + layer) * C + part * C // 2, C // 2)],
+            sems.at[4 * side + 2 * layer + part],
+        )
         for side, ref in enumerate((w_in_ref, w_out_ref))
         for layer in range(2)
+        for part in range(2)
     ]
+    gains_copy = pltpu.make_async_copy(g_ref, gains_ref, sems.at[8])
+    gains_copy.start()
     for copy in copies:
         copy.start()
-    gains = g_ref[...]
+    gains_copy.wait()
+    gains = gains_ref[...]
     coarse = gains.astype(BF16).astype(F32)
     rest = gains - coarse
     fine = rest.astype(BF16).astype(F32)
     count = jnp.full((2, C), counts[0].astype(F32))
     rows = [coarse, fine, rest - fine, jnp.zeros_like(coarse), count, jnp.zeros((6, C), F32)]
-    tail_ref[...] = jnp.concatenate(rows, 0).astype(BF16)
-    copies.append(pltpu.make_async_copy(tail_ref, packed_ref.at[pl.ds(4 * C, 16)], sems.at[4]))
-    copies[-1].start()
+    packed_ref[4 * C :] = jnp.concatenate(rows, 0).astype(BF16)
     for copy in copies:
         copy.wait()
 
@@ -468,9 +474,10 @@
     (own,) = call(
         pack_kernel,
         "pack",
-        [("smem", layer_counts)] + at_hbm(w_in[0], w_out[0]) + at_vmem(gains[0]),
+        [("smem", layer_counts)] + at_hbm(w_in[0], w_out[0], gains[0]),
         [((PACK, C), BF16)],
-        [pltpu.VMEM((16, C), BF16), dma((5,))],
+        [pltpu.VMEM((2, C), F32), dma((9,))],
+        limit=62600000,
     )
     holders = (MIDDLE, LAST)
     low_own = move(own, [(chip, chip) for chip in (FIRST, SECOND)], cross=True)

time: 115 us -> 116 us (level)
  the two profiles are of different devices: /device:TPU:16 before, /device:TPU:1 now
where the time goes in v5:
time: 116 us; the launch traced here: 115 us
  waiting for transfers between devices  57.6 us (50%)
  starting transfers between devices  47.1 us (41%)
  Pallas kernels  8.64 us (7%)
  between operations  1.82 us (2%)
    ppermute x25, waiting for transfers between devices, move(): return lax.ppermute(value, 'section', pairs)  41.1 us
    ppermute x25, starting transfers between devices, move(): return lax.ppermute(value, 'section', pairs)  39.5 us
    all_to_all x1, waiting for transfers between devices, body(): parts = lax.all_to_all(parts, 'dp', 0, 0, tiled=True)  16.5 us
    pallas_call x10, Pallas kernels, call(): pl.pallas_call(kernel, out_shape=outputs, in_specs=[specs[memory]() for m...  8.64 us
    all_to_all x1, starting transfers between devices, body(): parts = lax.all_to_all(parts, 'dp', 0, 0, tiled=True)  7.65 us
  transfers between devices with their start and end apart: 26, of which 6 were waited for; matrix products, arithmetic and copies ran while one was open for 0% of the time, Pallas kernels for 3%

profile of v5, /device:TPU:1, one launch (start us, length us, event | category | flops | bytes accessed | tf_op | source)
XLA Modules:
  0.0 115.3 jit_solution(11093254120044541248)
XLA Ops:
  1.3 2.0 %pack.1.refs_1_.refs_2_.refs_8_ = bf16[1040,256]{1,0:T(8,128)(2,1)} custom-call(s32[1]{0:T(128)S(6)} %copy.10.counts, bf16[2,256,256]{2,1,0:T(8,128)(2,1)} %bitcast.20, bf16[2,256,256]{2,1,0:T(8,128)(2,1)} %bitcast.22, f32[2,256]{1,0:T(2,128)} %bitcast.18), custom_call_target="tpu_custom_call" | custom-call | flops 1000000000 | bytes 1048576 | tf_op jit(solution)/shard_map/pack/pallas_call | solution.py:434
  3.3 8.8 %collective-permute-start = (bf16[1040,256]{1,0:T(8,128)(2,1)}, bf16[1040,256]{1,0:T(8,128)(2,1)S(1)}, u32[]{:S(2)}, u32[]{:S(2)}) collective-permute-start(bf16[1040,256]{1,0:T(8,128)(2,1)} %pack.1.refs_1_.refs_2_.refs_8_), channel_id=1, source_target_pairs={{0,32},{32,0},{64,96},{96,64},{1,33},{33,1},{65,97},{97,65},{2,34}... | collective-permute-start | bytes 1597448 | tf_op jit(solution)/shard_map/ppermute | solution.py:456
  12.1 0.7 collective-permute-start.2
  12.8 0.7 collective-permute-start.3
  13.5 0.3 collective-permute-done.refs_2_.refs_9_
  13.8 0.7 collective-permute-start.4
  14.5 2.5 %pair_forward.2 = (bf16[2,128,256]{2,1,0:T(8,128)(2,1)S(1)}, bf16[4,128,256]{2,1,0:T(8,128)(2,1)}, bf16[2,128,256]{2,1,0:T(8,128)(2,1)S(1)}, bf16[2,128,256]{2,1,0:T(8,128)(2,1)S(1)}) custom-call(bf16[2,128,256]{2,1,0:T(8,128)(2,1)S(1)} %copy-done.4, bf16[1040,256]{1,0:T(8,128)(2,1)} %pack.1.refs_1_.refs_2_.refs_8_, ...), custom_call_target="tpu_custom_call" | custom-call | flops 1000000000 | bytes 1048576 | tf_op jit(solution)/shard_map/pair_forward/pallas_call | solution.py:434
  17.0 1.3 %collective-permute-start.1 = (bf16[2,128,256]{2,1,0:T(8,128)(2,1)S(1)}, bf16[2,128,256]{2,1,0:T(8,128)(2,1)S(1)}, u32[]{:S(2)}, u32[]{:S(2)}) collective-permute-start(bf16[2,128,256]{2,1,0:T(8,128)(2,1)S(1)} %get-tuple-element.57), channel_id=1, source_target_pairs={{0,64},{32,96},{1,65},{33,97},{2,66},{34,98},{3,67},{35,99},{4,68}... | collective-permute-start | bytes 393224 | tf_op jit(solution)/shard_map/ppermute | solution.py:456
  18.4 1.9 %collective-permute-done.1.refs_0_ = bf16[2,128,256]{2,1,0:T(8,128)(2,1)S(1)} collective-permute-done((bf16[2,128,256]{2,1,0:T(8,128)(2,1)S(1)}, bf16[2,128,256]{2,1,0:T(8,128)(2,1)S(1)}, u32[]{:S(2)}, u32[]{:S(2)}) %collective-permute-start.1) | collective-permute-done | bytes 131104 | tf_op jit(solution)/shard_map/ppermute | solution.py:456
  20.3 0.7 collective-permute-start.5
  21.0 0.0 collective-permute-done.2.refs_0_
  21.0 0.0 collective-permute-done.3.refs_1_.refs_4_
  21.0 0.0 collective-permute-done.5.hop_ref
  21.0 0.0 collective-permute-done.4.refs_3_
  21.0 0.7 collective-permute-start.6
  21.7 0.7 collective-permute-start.7
  22.4 7.9 %collective-permute-start.14 = (bf16[1040,256]{1,0:T(8,128)(2,1)}, bf16[1040,256]{1,0:T(8,128)(2,1)S(1)}, u32[]{:S(2)}, u32[]{:S(2)}) collective-permute-start(bf16[1040,256]{1,0:T(8,128)(2,1)} %pack.1.refs_1_.refs_2_.refs_8_), channel_id=1, source_target_pairs={{0,64},{32,96},{1,65},{33,97},{2,66},{34,98},{3,67},{35,99},{4,68}... | collective-permute-start | bytes 1597448 | tf_op jit(solution)/shard_map/ppermute | solution.py:456
  30.3 0.0 collective-permute-done.6.refs_1_
  30.3 0.1 middle_forward.2
  30.4 0.0 collective-permute-done.7.refs_2_.refs_5_
  30.5 0.0 copy-start.3
  30.5 0.8 collective-permute-start.10
  31.3 0.7 collective-permute-start.9
  32.0 0.7 collective-permute-start.8
  32.7 6.2 %collective-permute-done.14.refs_6_ = bf16[1040,256]{1,0:T(8,128)(2,1)S(1)} collective-permute-done((bf16[1040,256]{1,0:T(8,128)(2,1)}, bf16[1040,256]{1,0:T(8,128)(2,1)S(1)}, u32[]{:S(2)}, u32[]{:S(2)}) %collective-permute-start.14) | collective-permute-done | bytes 532512 | tf_op jit(solution)/shard_map/ppermute | solution.py:456
  38.9 0.7 collective-permute-start.15
  39.6 0.0 collective-permute-done.8.hop_ref
  39.6 0.0 collective-permute-done.9.skip2_ref
  39.6 0.0 collective-permute-done.10.skip_ref
  39.6 0.1 last_both.1
  39.7 0.7 collective-permute-start.11
  40.4 0.7 collective-permute-start.12
  41.1 0.7 collective-permute-start.13
  41.8 0.7 collective-permute-start.19
  42.5 0.0 collective-permute-done.11.hop_ref
  42.5 0.0 collective-permute-done.12.refs_2_
  42.5 0.0 collective-permute-done.13.refs_3_
  42.5 0.0 collective-permute-done.15.refs_7_
  42.5 0.3 middle_backward.1
  42.8 0.7 collective-permute-start.18
  43.4 0.0 collective-permute-done.19.skip_ref
  43.5 0.0 collective-permute-done.18.hop_ref
  43.5 0.0 copy-start.1
  43.5 0.0 copy-start.2
  43.5 0.4 first_backward.1
  43.9 5.9 %collective-permute-start.24 = (bf16[3,128,256]{2,1,0:T(8,128)(2,1)S(1)}, bf16[3,128,256]{2,1,0:T(8,128)(2,1)S(1)}, u32[]{:S(2)}, u32[]{:S(2)}) collective-permute-start(bf16[3,128,256]{2,1,0:T(8,128)(2,1)S(1)} %get-tuple-element.103), channel_id=1, source_target_pairs={{0,32},{32,0},{64,96},{96,64},{192,224},{224,192},{384,416},{416,3... | collective-permute-start | bytes 589832 | tf_op jit(solution)/shard_map/ppermute | solution.py:456
  49.8 1.3 %collective-permute-start.20 = (bf16[128,256]{1,0:T(8,128)(2,1)S(1)}, bf16[128,256]{1,0:T(8,128)(2,1)S(1)}, u32[]{:S(2)}, u32[]{:S(2)}) collective-permute-start(bf16[128,256]{1,0:T(8,128)(2,1)S(1)} %get-tuple-element.99), channel_id=1, source_target_pairs={{64,0},{96,32},{192,128},{224,160},{384,320},{416,352},{65,1},{97,... | collective-permute-start | bytes 196616 | tf_op jit(solution)/shard_map/ppermute | solution.py:456
  51.1 1.3 %collective-permute-start.21 = (bf16[128,256]{1,0:T(8,128)(2,1)S(1)}, bf16[128,256]{1,0:T(8,128)(2,1)S(1)}, u32[]{:S(2)}, u32[]{:S(2)}) collective-permute-start(bf16[128,256]{1,0:T(8,128)(2,1)S(1)} %get-tuple-element.100), channel_id=1, source_target_pairs={{64,32},{96,0},{192,160},{224,128},{384,352},{416,320},{65,33},{97... | collective-permute-start | bytes 196616 | tf_op jit(solution)/shard_map/ppermute | solution.py:456
  52.4 0.7 collective-permute-start.16
  53.1 0.7 collective-permute-start.17
  53.8 31.9 %collective-permute-done.20.refs_4_ = bf16[128,256]{1,0:T(8,128)(2,1)S(1)} collective-permute-done((bf16[128,256]{1,0:T(8,128)(2,1)S(1)}, bf16[128,256]{1,0:T(8,128)(2,1)S(1)}, u32[]{:S(2)}, u32[]{:S(2)}) %collective-permute-start.20) | collective-permute-done | bytes 65568 | tf_op jit(solution)/shard_map/ppermute | solution.py:456
  85.6 0.8 collective-permute-start.22
  86.4 0.7 collective-permute-done.21.refs_5_
  87.1 0.7 collective-permute-start.23
  87.8 0.0 collective-permute-done.22.refs_6_
  87.8 0.0 collective-permute-done.23.refs_7_
  87.8 0.0 collective-permute-done.16.refs_0_
  87.8 0.0 collective-permute-done.17.refs_1_
  87.8 0.0 collective-permute-done.24.refs_8_
  87.9 2.4 %owner_gradients.1 = (bf16[2,128,256]{2,1,0:T(8,128)(2,1)}, bf16[32,16,512]{2,1,0:T(8,128)(2,1)}) custom-call(s32[1]{0:T(128)S(6)} %copy.10.counts, f32[2,256]{1,0:T(2,128)S(1)} %bitcast.19, bf16[2,256,256]{2,1,0:T(8,128)(2,1)S(1)} %bitcast.21, bf16[2,256,256]{2,1,0:T(8,128)(2,1)S(1)} %bitcast.23, bf16[2,128,256]{2,1,0:T(8,128)(2,1)S(1)} %collective-permute-done.16.refs_0_, ...), custom_call_target="tpu_custom_call" | custom-call | flops 1000000000 | bytes 1048576 | tf_op jit(solution)/shard_map/owner_gradients/pallas_call | solution.py:434
  90.3 7.6 %all-to-all-start = ((bf16[32,16,512]{2,1,0:T(8,128)(2,1)}), bf16[32,16,512]{2,1,0:T(8,128)(2,1)S(1)}, u32[]{:S(2)}, u32[]{:S(2)}) async-start(bf16[32,16,512]{2,1,0:T(8,128)(2,1)} %get-tuple-element.106), calls=%async_computation | async-start | bytes 1048576 | tf_op jit(solution)/shard_map/all_to_all | solution.py:588
  98.0 0.1 dynamic-slice_bitcast_fusion.g_ref
  98.1 16.5 %all-to-all-done.parts_ref = bf16[32,16,512]{2,1,0:T(8,128)(2,1)S(1)} async-done(((bf16[32,16,512]{2,1,0:T(8,128)(2,1)}), bf16[32,16,512]{2,1,0:T(8,128)(2,1)S(1)}, u32[]{:S(2)}, u32[]{:S(2)}) %all-to-all-start) | async-done | bytes 524320 | tf_op jit(solution)/shard_map/all_to_all | solution.py:588
  114.6 0.8 sum_parts.1
  (14 shorter events, 0.1 us)
Async XLA Ops:
  1.3 13.2 %copy-start.4 = (bf16[2,128,256]{2,1,0:T(8,128)(2,1)S(1)}, bf16[2,128,256]{2,1,0:T(8,128)(2,1)}, u32[]{:S(2)}) copy-start(bf16[2,128,256]{2,1,0:T(8,128)(2,1)} %x_ref.1) | copy-start | bytes 393220
  3.3 10.5 %collective-permute-start = (bf16[1040,256]{1,0:T(8,128)(2,1)}, bf16[1040,256]{1,0:T(8,128)(2,1)S(1)}, u32[]{:S(2)}, u32[]{:S(2)}) collective-permute-start(bf16[1040,256]{1,0:T(8,128)(2,1)} %pack.1.refs_1_.refs_2_.refs_8_), channel_id=1, source_target_pairs={{0,32},{32,0},{64,96},{96,64},{1,33},{33,1},{65,97},{97,65},{2,34}... | collective-permute-start | bytes 1597448 | tf_op jit(solution)/shard_map/ppermute | solution.py:456
  12.1 8.9 %collective-permute-start.2 = (bf16[1040,256]{1,0:T(8,128)(2,1)}, bf16[1040,256]{1,0:T(8,128)(2,1)S(1)}, u32[]{:S(2)}, u32[]{:S(2)}) collective-permute-start(bf16[1040,256]{1,0:T(8,128)(2,1)} %pack.1.refs_1_.refs_2_.refs_8_), channel_id=1, source_target_pairs={{128,192},{160,224},{320,384},{352,416},{129,193},{161,225},{321,3... | collective-permute-start | bytes 1597448 | tf_op jit(solution)/shard_map/ppermute | solution.py:456
  12.8 8.2 %collective-permute-start.3 = (bf16[1040,256]{1,0:T(8,128)(2,1)}, bf16[1040,256]{1,0:T(8,128)(2,1)S(1)}, u32[]{:S(2)}, u32[]{:S(2)}) collective-permute-start(bf16[1040,256]{1,0:T(8,128)(2,1)} %pack.1.refs_1_.refs_2_.refs_8_), channel_id=1, source_target_pairs={{256,192},{288,224},{448,384},{480,416},{257,193},{289,225},{449,3... | collective-permute-start | bytes 1597448 | tf_op jit(solution)/shard_map/ppermute | solution.py:456
  13.8 7.2 %collective-permute-start.4 = (bf16[1040,256]{1,0:T(8,128)(2,1)}, bf16[1040,256]{1,0:T(8,128)(2,1)S(1)}, u32[]{:S(2)}, u32[]{:S(2)}) collective-permute-start(bf16[1040,256]{1,0:T(8,128)(2,1)} %pack.1.refs_1_.refs_2_.refs_8_), channel_id=1, source_target_pairs={{192,224},{224,192},{384,416},{416,384},{193,225},{225,193},{385,4... | collective-permute-start | bytes 1597448 | tf_op jit(solution)/shard_map/ppermute | solution.py:456
  17.0 3.2 %collective-permute-start.1 = (bf16[2,128,256]{2,1,0:T(8,128)(2,1)S(1)}, bf16[2,128,256]{2,1,0:T(8,128)(2,1)S(1)}, u32[]{:S(2)}, u32[]{:S(2)}) collective-permute-start(bf16[2,128,256]{2,1,0:T(8,128)(2,1)S(1)} %get-tuple-element.57), channel_id=1, source_target_pairs={{0,64},{32,96},{1,65},{33,97},{2,66},{34,98},{3,67},{35,99},{4,68}... | collective-permute-start | bytes 393224 | tf_op jit(solution)/shard_map/ppermute | solution.py:456
  20.3 0.7 collective-permute-start.5
  21.0 9.3 %collective-permute-start.6 = (bf16[1040,256]{1,0:T(8,128)(2,1)S(1)}, bf16[1040,256]{1,0:T(8,128)(2,1)S(1)}, u32[]{:S(2)}, u32[]{:S(2)}) collective-permute-start(bf16[1040,256]{1,0:T(8,128)(2,1)S(1)} %collective-permute-done.2.refs_0_), channel_id=1, source_target_pairs={{192,224},{224,192},{384,416},{416,384},{193,225},{225,193},{385,4... | collective-permute-start | bytes 1597448 | tf_op jit(solution)/shard_map/ppermute | solution.py:456
  21.7 8.7 %collective-permute-start.7 = (bf16[1040,256]{1,0:T(8,128)(2,1)S(1)}, bf16[1040,256]{1,0:T(8,128)(2,1)S(1)}, u32[]{:S(2)}, u32[]{:S(2)}) collective-permute-start(bf16[1040,256]{1,0:T(8,128)(2,1)S(1)} %collective-permute-done.3.refs_1_.refs_4_), channel_id=1, source_target_pairs={{192,224},{224,192},{384,416},{416,384},{193,225},{225,193},{385,4... | collective-permute-start | bytes 1597448 | tf_op jit(solution)/shard_map/ppermute | solution.py:456
  22.4 16.5 %collective-permute-start.14 = (bf16[1040,256]{1,0:T(8,128)(2,1)}, bf16[1040,256]{1,0:T(8,128)(2,1)S(1)}, u32[]{:S(2)}, u32[]{:S(2)}) collective-permute-start(bf16[1040,256]{1,0:T(8,128)(2,1)} %pack.1.refs_1_.refs_2_.refs_8_), channel_id=1, source_target_pairs={{0,64},{32,96},{1,65},{33,97},{2,66},{34,98},{3,67},{35,99},{4,68}... | collective-permute-start | bytes 1597448 | tf_op jit(solution)/shard_map/ppermute | solution.py:456
  30.5 9.2 %copy-start.3 = (bf16[2,128,256]{2,1,0:T(8,128)(2,1)S(1)}, bf16[2,128,256]{2,1,0:T(8,128)(2,1)}, u32[]{:S(2)}) copy-start(bf16[2,128,256]{2,1,0:T(8,128)(2,1)} %ct_ref.1) | copy-start | bytes 393220
  30.5 9.1 %collective-permute-start.10 = (bf16[4,128,256]{2,1,0:T(8,128)(2,1)S(1)}, bf16[4,128,256]{2,1,0:T(8,128)(2,1)S(1)}, u32[]{:S(2)}, u32[]{:S(2)}) collective-permute-start(bf16[4,128,256]{2,1,0:T(8,128)(2,1)S(1)} %get-tuple-element.68), channel_id=1, source_target_pairs={{64,384},{96,416},{65,385},{97,417},{66,386},{98,418},{67,387},{99... | collective-permute-start | bytes 786440 | tf_op jit(solution)/shard_map/ppermute | solution.py:456
  31.3 8.3 %collective-permute-start.9 = (bf16[2,128,256]{2,1,0:T(8,128)(2,1)S(1)}, bf16[2,128,256]{2,1,0:T(8,128)(2,1)S(1)}, u32[]{:S(2)}, u32[]{:S(2)}) collective-permute-start(bf16[2,128,256]{2,1,0:T(8,128)(2,1)S(1)} %slice.15), channel_id=1, source_target_pairs={{192,384},{224,416},{193,385},{225,417},{194,386},{226,418},{195,3... | collective-permute-start | bytes 393224 | tf_op jit(solution)/shard_map/ppermute | solution.py:456
  32.0 7.6 %collective-permute-start.8 = (bf16[128,256]{1,0:T(8,128)(2,1)S(1)}, bf16[128,256]{1,0:T(8,128)(2,1)S(1)}, u32[]{:S(2)}, u32[]{:S(2)}) collective-permute-start(bf16[128,256]{1,0:T(8,128)(2,1)S(1)} %slice_bitcast_fusion), channel_id=1, source_target_pairs={{192,384},{224,416},{193,385},{225,417},{194,386},{226,418},{195,3... | collective-permute-start | bytes 196616 | tf_op jit(solution)/shard_map/ppermute | solution.py:456
  38.9 3.6 %collective-permute-start.15 = (bf16[1040,256]{1,0:T(8,128)(2,1)S(1)}, bf16[1040,256]{1,0:T(8,128)(2,1)S(1)}, u32[]{:S(2)}, u32[]{:S(2)}) collective-permute-start(bf16[1040,256]{1,0:T(8,128)(2,1)S(1)} %collective-permute-done.14.refs_6_), channel_id=1, source_target_pairs={{64,96},{96,64},{65,97},{97,65},{66,98},{98,66},{67,99},{99,67},{6... | collective-permute-start | bytes 1597448 | tf_op jit(solution)/shard_map/ppermute | solution.py:456
  39.7 2.7 %collective-permute-start.11 = (bf16[2,128,256]{2,1,0:T(8,128)(2,1)S(1)}, bf16[2,128,256]{2,1,0:T(8,128)(2,1)S(1)}, u32[]{:S(2)}, u32[]{:S(2)}) collective-permute-start(bf16[2,128,256]{2,1,0:T(8,128)(2,1)S(1)} %get-tuple-element.73), channel_id=1, source_target_pairs={{384,192},{416,224},{385,193},{417,225},{386,194},{418,226},{387,1... | collective-permute-start | bytes 393224 | tf_op jit(solution)/shard_map/ppermute | solution.py:456
  40.4 2.1 %collective-permute-start.12 = (bf16[2,128,256]{2,1,0:T(8,128)(2,1)S(1)}, bf16[2,128,256]{2,1,0:T(8,128)(2,1)S(1)}, u32[]{:S(2)}, u32[]{:S(2)}) collective-permute-start(bf16[2,128,256]{2,1,0:T(8,128)(2,1)S(1)} %get-tuple-element.74), channel_id=1, source_target_pairs={{192,256},{224,288},{384,448},{416,480},{193,257},{225,289},{385,4... | collective-permute-start | bytes 393224 | tf_op jit(solution)/shard_map/ppermute | solution.py:456
  41.1 1.4 %collective-permute-start.13 = (bf16[2,128,256]{2,1,0:T(8,128)(2,1)S(1)}, bf16[2,128,256]{2,1,0:T(8,128)(2,1)S(1)}, u32[]{:S(2)}, u32[]{:S(2)}) collective-permute-start(bf16[2,128,256]{2,1,0:T(8,128)(2,1)S(1)} %get-tuple-element.75), channel_id=1, source_target_pairs={{192,288},{224,256},{384,480},{416,448},{193,289},{225,257},{385,4... | collective-permute-start | bytes 393224 | tf_op jit(solution)/shard_map/ppermute | solution.py:456
  41.8 1.7 %collective-permute-start.19 = (bf16[4,128,256]{2,1,0:T(8,128)(2,1)S(1)}, bf16[4,128,256]{2,1,0:T(8,128)(2,1)S(1)}, u32[]{:S(2)}, u32[]{:S(2)}) collective-permute-start(bf16[4,128,256]{2,1,0:T(8,128)(2,1)S(1)} %get-tuple-element.88), channel_id=1, source_target_pairs={{384,64},{416,96},{385,65},{417,97},{386,66},{418,98},{387,67},{41... | collective-permute-start | bytes 786440 | tf_op jit(solution)/shard_map/ppermute | solution.py:456
  42.8 0.7 collective-permute-start.18
  43.5 44.4 %copy-start.1 = (bf16[1,2,256,256]{3,2,1,0:T(8,128)(2,1)S(1)}, bf16[1,2,256,256]{3,2,1,0:T(8,128)(2,1)}, u32[]{:S(2)}) copy-start(bf16[1,2,256,256]{3,2,1,0:T(8,128)(2,1)} %param.8) | copy-start | bytes 786436
  43.5 44.4 %copy-start.2 = (bf16[1,2,256,256]{3,2,1,0:T(8,128)(2,1)S(1)}, bf16[1,2,256,256]{3,2,1,0:T(8,128)(2,1)}, u32[]{:S(2)}) copy-start(bf16[1,2,256,256]{3,2,1,0:T(8,128)(2,1)} %param.9) | copy-start | bytes 786436
  43.9 43.9 %collective-permute-start.24 = (bf16[3,128,256]{2,1,0:T(8,128)(2,1)S(1)}, bf16[3,128,256]{2,1,0:T(8,128)(2,1)S(1)}, u32[]{:S(2)}, u32[]{:S(2)}) collective-permute-start(bf16[3,128,256]{2,1,0:T(8,128)(2,1)S(1)} %get-tuple-element.103), channel_id=1, source_target_pairs={{0,32},{32,0},{64,96},{96,64},{192,224},{224,192},{384,416},{416,3... | collective-permute-start | bytes 589832 | tf_op jit(solution)/shard_map/ppermute | solution.py:456
  49.8 35.8 %collective-permute-start.20 = (bf16[128,256]{1,0:T(8,128)(2,1)S(1)}, bf16[128,256]{1,0:T(8,128)(2,1)S(1)}, u32[]{:S(2)}, u32[]{:S(2)}) collective-permute-start(bf16[128,256]{1,0:T(8,128)(2,1)S(1)} %get-tuple-element.99), channel_id=1, source_target_pairs={{64,0},{96,32},{192,128},{224,160},{384,320},{416,352},{65,1},{97,... | collective-permute-start | bytes 196616 | tf_op jit(solution)/shard_map/ppermute | solution.py:456
  51.1 36.0 %collective-permute-start.21 = (bf16[128,256]{1,0:T(8,128)(2,1)S(1)}, bf16[128,256]{1,0:T(8,128)(2,1)S(1)}, u32[]{:S(2)}, u32[]{:S(2)}) collective-permute-start(bf16[128,256]{1,0:T(8,128)(2,1)S(1)} %get-tuple-element.100), channel_id=1, source_target_pairs={{64,32},{96,0},{192,160},{224,128},{384,352},{416,320},{65,33},{97... | collective-permute-start | bytes 196616 | tf_op jit(solution)/shard_map/ppermute | solution.py:456
  52.4 35.4 %collective-permute-start.16 = (bf16[2,128,256]{2,1,0:T(8,128)(2,1)S(1)}, bf16[2,128,256]{2,1,0:T(8,128)(2,1)S(1)}, u32[]{:S(2)}, u32[]{:S(2)}) collective-permute-start(bf16[2,128,256]{2,1,0:T(8,128)(2,1)S(1)} %get-tuple-element.83), channel_id=1, source_target_pairs={{192,128},{224,160},{384,320},{416,352},{193,129},{225,161},{385,3... | collective-permute-start | bytes 393224 | tf_op jit(solution)/shard_map/ppermute | solution.py:456
  53.1 34.7 %collective-permute-start.17 = (bf16[2,128,256]{2,1,0:T(8,128)(2,1)S(1)}, bf16[2,128,256]{2,1,0:T(8,128)(2,1)S(1)}, u32[]{:S(2)}, u32[]{:S(2)}) collective-permute-start(bf16[2,128,256]{2,1,0:T(8,128)(2,1)S(1)} %get-tuple-element.84), channel_id=1, source_target_pairs={{192,160},{224,128},{384,352},{416,320},{193,161},{225,129},{385,3... | collective-permute-start | bytes 393224 | tf_op jit(solution)/shard_map/ppermute | solution.py:456
  85.6 2.2 %copy-start = (f32[1,2,256]{2,1,0:T(2,128)S(1)}, f32[1,2,256]{2,1,0:T(2,128)}, u32[]{:S(2)}) copy-start(f32[1,2,256]{2,1,0:T(2,128)} %param.10) | copy-start | bytes 6148
  85.6 2.2 %collective-permute-start.22 = (bf16[128,256]{1,0:T(8,128)(2,1)S(1)}, bf16[128,256]{1,0:T(8,128)(2,1)S(1)}, u32[]{:S(2)}, u32[]{:S(2)}) collective-permute-start(bf16[128,256]{1,0:T(8,128)(2,1)S(1)} %get-tuple-element.101), channel_id=1, source_target_pairs={{192,256},{224,288},{384,448},{416,480},{193,257},{225,289},{385,4... | collective-permute-start | bytes 196616 | tf_op jit(solution)/shard_map/ppermute | solution.py:456
  87.1 0.7 collective-permute-start.23
  90.3 24.2 %all-to-all-start = ((bf16[32,16,512]{2,1,0:T(8,128)(2,1)}), bf16[32,16,512]{2,1,0:T(8,128)(2,1)S(1)}, u32[]{:S(2)}, u32[]{:S(2)}) async-start(bf16[32,16,512]{2,1,0:T(8,128)(2,1)} %get-tuple-element.106), calls=%async_computation | async-start | bytes 1048576 | tf_op jit(solution)/shard_map/all_to_all | solution.py:588

commit v6 on v3

--- a/solution.py
+++ b/solution.py
@@ -1,3 +1,5 @@
+import functools
+
 import jax
 import jax.numpy as jnp
 from jax import lax
@@ -118,28 +120,34 @@
         return layer(0).astype(BF16)
 
 
-def pack_kernel(counts, w_in_ref, w_out_ref, g_ref, packed_ref, tail_ref, sems):
+def pack_kernel(counts, w_in_ref, w_out_ref, g_ref, packed_ref, gains_ref, sems):
     copies = [
-        pltpu.make_async_copy(ref.at[layer], packed_ref.at[pl.ds((2 * side + layer) * C, C)], sems.at[2 * side + layer])
+        pltpu.make_async_copy(
+            ref.at[layer, pl.ds(part * C // 2, C // 2)],
+            packed_ref.at[pl.ds((2 * side + layer) * C + part * C // 2, C // 2)],
+            sems.at[4 * side + 2 * layer + part],
+        )
         for side, ref in enumerate((w_in_ref, w_out_ref))
         for layer in range(2)
+        for part in range(2)
     ]
+    gains_copy = pltpu.make_async_copy(g_ref, gains_ref, sems.at[8])
+    gains_copy.start()
     for copy in copies:
         copy.start()
-    gains = g_ref[...]
+    gains_copy.wait()
+    gains = gains_ref[...]
     coarse = gains.astype(BF16).astype(F32)
     rest = gains - coarse
     fine = rest.astype(BF16).astype(F32)
     count = jnp.full((2, C), counts[0].astype(F32))
     rows = [coarse, fine, rest - fine, jnp.zeros_like(coarse), count, jnp.zeros((6, C), F32)]
-    tail_ref[...] = jnp.concatenate(rows, 0).astype(BF16)
-    copies.append(pltpu.make_async_copy(tail_ref, packed_ref.at[pl.ds(4 * C, 16)], sems.at[4]))
-    copies[-1].start()
+    packed_ref[4 * C :] = jnp.concatenate(rows, 0).astype(BF16)
     for copy in copies:
         copy.wait()
 
 
-def pair_kernel(chip, x_ref, same, other, outs_ref, last_ref, rows_same, rows_other, packed, states, pres, sems):
+def pair_kernel(chip, x_ref, same, other, outs_ref, skip_ref, rows_same, rows_other, packed, states, pres, sems):
     here, core = position()
 
     def keep(slot, index, value):
@@ -155,14 +163,16 @@
     def _():
         weights = Weights(core, [same, other], packed, sems)
         weights.start(0)
-        state = (x_ref[core] if chip == FIRST else x_ref[...]).astype(F32)
+        state = (x_ref[core] if chip == FIRST else x_ref[1]).astype(F32)
         for slot in range(2):
             weights.wait(slot)
             weights.forward(slot, state, states, pres, outs_ref)
             keep(slot, 0, outs_ref[slot])
             keep(slot, 1, state.astype(BF16))
             state = outs_ref[slot].astype(F32)
-        last_ref[...] = outs_ref[1]
+        if chip == SECOND:
+            skip_ref[:2] = x_ref[...]
+            skip_ref[2:] = outs_ref[...]
 
 
 def middle_forward_kernel(hop_ref, *refs):
@@ -181,8 +191,8 @@
                 state = state + outs_ref[7 - slot].astype(F32)
             inflow_ref[slot] = state.astype(BF16)
             weights.forward(slot, state, state_ref, pre_ref, outs_ref)
-        hop_out[0] = outs_ref[5]
-        hop_out[1:] = outs_ref[:2]
+        hop_out[0] = (outs_ref[5].astype(F32) + outs_ref[1].astype(F32)).astype(BF16)
+        hop_out[1] = outs_ref[0]
 
 
 def store_by_owner(core, slot, refs, index, value):
@@ -198,7 +208,7 @@
         other[index] = value
 
 
-def last_kernel(hop_ref, skip0_ref, skip1_ref, ct_ref, outs_in, inflow_in, *refs):
+def last_kernel(hop_ref, skip_ref, ct_ref, outs_in, inflow_in, *refs):
     refs, refs_out = refs[:6], refs[6:]
     owners, (hop_out, sent_out, up_ref) = refs_out[:6], refs_out[6:9]
     packed, outs_ref, inflow_ref, state_ref, pre_ref, sent_ref, grad_ref, sems = refs_out[9:]
@@ -214,11 +224,12 @@
         weights = Weights(core, refs, packed, sems)
         for pair in range(3):
             weights.start(pair)
-        skips = [hop_ref.at[2], hop_ref.at[1]] + [ref.at[index] for ref in (skip1_ref, skip0_ref) for index in (1, 0)]
+        skips = [None, hop_ref.at[1]] + [skip_ref.at[index] for index in (3, 2, 1, 0)]
         for slot in range(6):
             weights.wait(slot)
             state = (hop_ref[0] if slot == 0 else outs_ref[slot - 1]).astype(F32)
-            state = state + skips[slot][...].astype(F32)
+            if slot:
+                state = state + skips[slot][...].astype(F32)
             inflow_ref[slot] = state.astype(BF16)
             weights.forward(slot, state, state_ref, pre_ref, outs_ref)
         for slot in reversed(range(6)):
@@ -235,7 +246,7 @@
 
 
 def middle_backward_kernel(hop_ref, state_ref, pre_ref, x_ref, *refs):
-    refs, low_refs, refs_out = refs[:6], refs[6:8] + refs[2:4], refs[8:]
+    refs, low_refs, refs_out = refs[:6], refs[6:10], refs[10:]
     hop_out, up_ref, low_state, low_pre, packed, sent_ref, grad_ref, sems = refs_out
     here, core = position()
 
@@ -460,12 +471,13 @@
     (own,) = call(
         pack_kernel,
         "pack",
-        [("smem", layer_counts)] + at_hbm(w_in[0], w_out[0]) + at_vmem(gains[0]),
+        [("smem", layer_counts)] + at_hbm(w_in[0], w_out[0], gains[0]),
         [((PACK, C), BF16)],
-        [pltpu.VMEM((16, C), BF16), dma((5,))],
+        [pltpu.VMEM((2, C), F32), dma((9,))],
+        limit=62600000,
     )
     holders = (MIDDLE, LAST)
-    partner = move(own, [(chip, chip) for chip in (FIRST, SECOND, MIDDLE, LAST)], cross=True)
+    low_own = move(own, [(chip, chip) for chip in (FIRST, SECOND)], cross=True)
     left = move(own, [(chip - 1, chip) for chip in holders])
     right = move(own, [(chip + 1, chip) for chip in holders])
 
@@ -473,15 +485,17 @@
         return call(
             lambda *refs: pair_kernel(chip, *refs),
             "pair_forward",
-            at_vmem(value) + at_hbm(own, partner),
-            [((2,) + tile, BF16), (tile, BF16)] + [((2,) + tile, BF16)] * 2,
+            at_vmem(value) + at_hbm(own, low_own),
+            [((2,) + tile, BF16), ((4,) + tile, BF16)] + [((2,) + tile, BF16)] * 2,
             [packed_scratch(2), kept(2, pixels), kept(2, pixels), dma((2,))],
         )
 
-    outs_a, last_a, *rows_a = pair(FIRST, images)
-    outs_b, last_b, *rows_b = pair(SECOND, move(last_a, [(FIRST, SECOND)]))
-    hop = move(last_b, [(SECOND, MIDDLE)])
-    left, right, later, hop = barrier((left, right, own, hop))
+    outs_a, _, *rows_a = pair(FIRST, images)
+    outs_b, skip, *rows_b = pair(SECOND, move(outs_a, [(FIRST, SECOND)]))
+    hop = move(outs_b[1], [(SECOND, MIDDLE)])
+    partner = move(barrier((own, low_own))[0], [(chip, chip) for chip in holders], cross=True)
+    left, right, later, partner, skip, hop = barrier((left, right, own, partner, skip, hop))
+    skip = move(skip, [(SECOND, LAST)])
     left_partner = move(left, [(chip, chip) for chip in holders], cross=True)
     right_partner = move(right, [(chip, chip) for chip in holders], cross=True)
     weights = at_hbm(left, left_partner, own, partner, right, right_partner)
@@ -492,21 +506,18 @@
         middle_forward_kernel,
         "middle_forward",
         at_vmem(hop) + weights,
-        [(six, BF16), (six, BF16), ((3,) + tile, BF16), (six_state, F32), (six_state, F32)],
+        [(six, BF16), (six, BF16), ((2,) + tile, BF16), (six_state, F32), (six_state, F32)],
         [packed_scratch(6), dma((6,))],
         us=3,
     )
-    skip0, skip1, hop = barrier((outs_a, outs_b, hop))
     hop = move(hop, [(MIDDLE, LAST)])
-    skip0 = move(skip0, [(FIRST, LAST)])
-    skip1 = move(skip1, [(SECOND, LAST)])
     low_left = move(later, [(SECOND - 1, SECOND)])
     low_partner = move(low_left, [(SECOND, SECOND)], cross=True)
-    low_weights = at_hbm(low_left, low_partner, own, partner)
+    low_weights = at_hbm(low_left, low_partner, own, low_own)
     *to_owners, hop, skips, ups_last = call(
         last_kernel,
         "last_both",
-        at_vmem(hop, skip0, skip1, cotangent, outs, inflows) + weights,
+        at_vmem(hop, skip, cotangent, outs, inflows) + weights,
         [((2,) + tile, BF16)] * 6 + [((2,) + tile, BF16), (four, BF16), (six, BF16)],
         [
             packed_scratch(6),
@@ -535,15 +546,14 @@
     hop, ups_middle, low_states, low_pres = call(
         middle_backward_kernel,
         "middle_backward",
-        at_vmem(hop, states, pres, images) + weights + low_weights[:2],
+        at_vmem(hop, states, pres, images) + weights + low_weights,
         [(tile, BF16), (six, BF16), (four_state, F32), (four_state, F32)],
         [packed_scratch(6), pltpu.VMEM(six, BF16), pltpu.VMEM(tile, F32), dma((6,))],
         us=5,
     )
     rows_left, hop = barrier((rows_left, hop))
     hop = move(hop, [(MIDDLE, SECOND)])
-    rows_left = deliver((MIDDLE, LAST), *rows_left, None, None)
-    rows = rows_left + rows_right
+    rows = deliver((MIDDLE, LAST), *rows_left) + rows_right
     *away, own_other, own_same = call(
         first_backward_kernel,
         "first_backward",

time: 118 us -> 113 us (0.958)
  starting transfers between devices: 59.3 us -> 44.4 us
  waiting for transfers between devices: 46.7 us -> 56.1 us
  Pallas kernels: 6.41 us -> 8.38 us
  local copies, waits for them, and re-layouts: 2.68 us -> 1.15 us
    ppermute x24, starting transfers between devices: 46.5 us -> 36.5 us  [move(): return lax.ppermute(value, 'section', pairs)]
    ppermute x24, waiting for transfers between devices: 30.2 us -> 39.6 us  [move(): return lax.ppermute(value, 'section', pairs)]
    all_to_all x1, starting transfers between devices: 12.9 us -> 7.95 us  [body(): parts = lax.all_to_all(parts, 'dp', 0, 0, tiled=True)]
    pallas_call x9, Pallas kernels: 6.41 us -> 8.38 us  [call(): pl.pallas_call(kernel, out_shape=outputs, in_specs=[specs[memory]() for m...]
    unnamed x16 -> x14, local copies, waits for them, and re-layouts: 2.6 us -> 1.07 us
where the time goes in v6:
time: 113 us; the launch traced here: 112 us
  waiting for transfers between devices  56.1 us (50%)
  starting transfers between devices  44.4 us (39%)
  Pallas kernels  8.38 us (7%)
  between operations  1.79 us (2%)
  local copies, waits for them, and re-layouts  1.15 us (1%)
    ppermute x24, waiting for transfers between devices, move(): return lax.ppermute(value, 'section', pairs)  39.6 us
    ppermute x24, starting transfers between devices, move(): return lax.ppermute(value, 'section', pairs)  36.5 us
    all_to_all x1, waiting for transfers between devices, body(): parts = lax.all_to_all(parts, 'dp', 0, 0, tiled=True)  16.5 us
    pallas_call x9, Pallas kernels, call(): pl.pallas_call(kernel, out_shape=outputs, in_specs=[specs[memory]() for m...  8.38 us
    all_to_all x1, starting transfers between devices, body(): parts = lax.all_to_all(parts, 'dp', 0, 0, tiled=True)  7.95 us
  transfers between devices with their start and end apart: 25, of which 6 were waited for; matrix products, arithmetic and copies ran while one was open for 0% of the time, Pallas kernels for 2%

profile of v6, /device:TPU:1, one launch (start us, length us, event | category | flops | bytes accessed | tf_op | source)
XLA Modules:
  0.0 111.8 jit_solution(5237763573337545547)
XLA Ops:
  1.3 2.0 %pack.1.refs_1_.refs_2_.refs_8_ = bf16[1040,256]{1,0:T(8,128)(2,1)} custom-call(s32[1]{0:T(128)S(6)} %copy.10.counts, bf16[2,256,256]{2,1,0:T(8,128)(2,1)} %bitcast.16, bf16[2,256,256]{2,1,0:T(8,128)(2,1)} %bitcast.18, f32[2,256]{1,0:T(2,128)} %bitcast.14), custom_call_target="tpu_custom_call" | custom-call | flops 1000000000 | bytes 1048576 | tf_op jit(solution)/shard_map/pack/pallas_call | solution.py:431
  3.3 8.8 %collective-permute-start.2 = (bf16[1040,256]{1,0:T(8,128)(2,1)}, bf16[1040,256]{1,0:T(8,128)(2,1)S(1)}, u32[]{:S(2)}, u32[]{:S(2)}) collective-permute-start(bf16[1040,256]{1,0:T(8,128)(2,1)} %pack.1.refs_1_.refs_2_.refs_8_), channel_id=1, source_target_pairs={{0,32},{32,0},{64,96},{96,64},{1,33},{33,1},{65,97},{97,65},{2,34}... | collective-permute-start | bytes 1597448 | tf_op jit(solution)/shard_map/ppermute | solution.py:453
  12.1 0.7 collective-permute-start
  12.8 0.7 collective-permute-start.1
  13.5 0.3 collective-permute-done.2.refs_2_.refs_9_
  13.8 0.7 collective-permute-start.3
  14.5 1.0 copy-done.2
  15.6 2.3 %pair_forward.2 = (bf16[2,128,256]{2,1,0:T(8,128)(2,1)S(1)}, bf16[4,128,256]{2,1,0:T(8,128)(2,1)}, bf16[2,128,256]{2,1,0:T(8,128)(2,1)S(1)}, bf16[2,128,256]{2,1,0:T(8,128)(2,1)S(1)}) custom-call(bf16[2,128,256]{2,1,0:T(8,128)(2,1)S(1)} %copy-done.6, bf16[1040,256]{1,0:T(8,128)(2,1)S(1)} %copy-done.2, ...), custom_call_target="tpu_custom_call" | custom-call | flops 1000000000 | bytes 1048576 | tf_op jit(solution)/shard_map/pair_forward/pallas_call | solution.py:431
  17.9 1.3 %collective-permute-start.4 = (bf16[2,128,256]{2,1,0:T(8,128)(2,1)S(1)}, bf16[2,128,256]{2,1,0:T(8,128)(2,1)S(1)}, u32[]{:S(2)}, u32[]{:S(2)}) collective-permute-start(bf16[2,128,256]{2,1,0:T(8,128)(2,1)S(1)} %get-tuple-element.54), channel_id=1, source_target_pairs={{0,64},{32,96},{1,65},{33,97},{2,66},{34,98},{3,67},{35,99},{4,68}... | collective-permute-start | bytes 393224 | tf_op jit(solution)/shard_map/ppermute | solution.py:453
  19.2 2.8 %collective-permute-done.4.refs_0_ = bf16[2,128,256]{2,1,0:T(8,128)(2,1)S(1)} collective-permute-done((bf16[2,128,256]{2,1,0:T(8,128)(2,1)S(1)}, bf16[2,128,256]{2,1,0:T(8,128)(2,1)S(1)}, u32[]{:S(2)}, u32[]{:S(2)}) %collective-permute-start.4) | collective-permute-done | bytes 131104 | tf_op jit(solution)/shard_map/ppermute | solution.py:453
  22.0 0.7 collective-permute-start.5
  22.7 0.0 collective-permute-done.refs_0_
  22.7 0.0 collective-permute-done.1.refs_4_
  22.7 0.0 collective-permute-done.5.hop_ref
  22.7 0.0 collective-permute-done.3.refs_3_
  22.7 0.0 copy-start.5
  22.8 0.8 collective-permute-start.6
  23.6 0.7 collective-permute-start.7
  24.3 7.3 %collective-permute-start.13 = (bf16[1040,256]{1,0:T(8,128)(2,1)S(1)}, bf16[1040,256]{1,0:T(8,128)(2,1)S(1)}, u32[]{:S(2)}, u32[]{:S(2)}) collective-permute-start(bf16[1040,256]{1,0:T(8,128)(2,1)S(1)} %copy-done.3), channel_id=1, source_target_pairs={{0,64},{32,96},{1,65},{33,97},{2,66},{34,98},{3,67},{35,99},{4,68}... | collective-permute-start | bytes 1597448 | tf_op jit(solution)/shard_map/ppermute | solution.py:453
  31.5 0.7 collective-permute-start.9
  32.2 0.0 collective-permute-done.6.refs_1_
  32.2 0.0 collective-permute-done.7.refs_5_
  32.3 0.1 middle_forward.1
  32.3 0.7 collective-permute-start.8
  33.0 8.4 %collective-permute-done.13.refs_6_ = bf16[1040,256]{1,0:T(8,128)(2,1)S(1)} collective-permute-done((bf16[1040,256]{1,0:T(8,128)(2,1)S(1)}, bf16[1040,256]{1,0:T(8,128)(2,1)S(1)}, u32[]{:S(2)}, u32[]{:S(2)}) %collective-permute-start.13) | collective-permute-done | bytes 532512 | tf_op jit(solution)/shard_map/ppermute | solution.py:453
  41.4 0.7 collective-permute-start.14
  42.1 0.0 collective-permute-done.9.skip_ref
  42.1 0.0 collective-permute-done.8.hop_ref
  42.2 0.1 last_both.1
  42.2 0.7 collective-permute-start.10
  42.9 0.7 collective-permute-start.11
  43.6 0.7 collective-permute-start.12
  44.3 0.7 collective-permute-start.18
  45.0 0.0 collective-permute-done.10.hop_ref
  45.0 0.0 collective-permute-done.11.refs_2_
  45.0 0.0 collective-permute-done.12.refs_3_
  45.0 0.0 collective-permute-done.14.refs_7_
  45.0 0.3 middle_backward.1
  45.3 0.7 collective-permute-start.17
  46.0 0.0 collective-permute-done.18.skip_ref
  46.0 0.0 collective-permute-done.17.hop_ref
  46.0 0.0 copy-start
  46.0 0.0 copy-start.1
  46.0 0.0 copy-start.4
  46.0 0.4 first_backward.1
  46.5 4.3 %collective-permute-start.23 = (bf16[3,128,256]{2,1,0:T(8,128)(2,1)S(1)}, bf16[3,128,256]{2,1,0:T(8,128)(2,1)S(1)}, u32[]{:S(2)}, u32[]{:S(2)}) collective-permute-start(bf16[3,128,256]{2,1,0:T(8,128)(2,1)S(1)} %get-tuple-element.95), channel_id=1, source_target_pairs={{0,32},{32,0},{64,96},{96,64},{192,224},{224,192},{384,416},{416,3... | collective-permute-start | bytes 589832 | tf_op jit(solution)/shard_map/ppermute | solution.py:453
  50.8 1.3 %collective-permute-start.19 = (bf16[128,256]{1,0:T(8,128)(2,1)S(1)}, bf16[128,256]{1,0:T(8,128)(2,1)S(1)}, u32[]{:S(2)}, u32[]{:S(2)}) collective-permute-start(bf16[128,256]{1,0:T(8,128)(2,1)S(1)} %get-tuple-element.91), channel_id=1, source_target_pairs={{64,0},{96,32},{192,128},{224,160},{384,320},{416,352},{65,1},{97,... | collective-permute-start | bytes 196616 | tf_op jit(solution)/shard_map/ppermute | solution.py:453
  52.1 1.3 %collective-permute-start.20 = (bf16[128,256]{1,0:T(8,128)(2,1)S(1)}, bf16[128,256]{1,0:T(8,128)(2,1)S(1)}, u32[]{:S(2)}, u32[]{:S(2)}) collective-permute-start(bf16[128,256]{1,0:T(8,128)(2,1)S(1)} %get-tuple-element.92), channel_id=1, source_target_pairs={{64,32},{96,0},{192,160},{224,128},{384,352},{416,320},{65,33},{97... | collective-permute-start | bytes 196616 | tf_op jit(solution)/shard_map/ppermute | solution.py:453
  53.4 0.7 collective-permute-start.15
  54.0 0.7 collective-permute-start.16
  54.7 27.2 %collective-permute-done.19.refs_4_ = bf16[128,256]{1,0:T(8,128)(2,1)S(1)} collective-permute-done((bf16[128,256]{1,0:T(8,128)(2,1)S(1)}, bf16[128,256]{1,0:T(8,128)(2,1)S(1)}, u32[]{:S(2)}, u32[]{:S(2)}) %collective-permute-start.19) | collective-permute-done | bytes 65568 | tf_op jit(solution)/shard_map/ppermute | solution.py:453
  81.9 0.7 collective-permute-start.21
  82.5 0.8 collective-permute-done.20.refs_5_
  83.4 0.7 collective-permute-start.22
  84.0 0.0 collective-permute-done.21.refs_6_
  84.0 0.0 collective-permute-done.22.refs_7_
  84.1 0.0 collective-permute-done.15.refs_0_
  84.1 0.0 collective-permute-done.16.refs_1_
  84.1 0.0 collective-permute-done.23.refs_8_
  84.1 2.4 %owner_gradients.1 = (bf16[2,128,256]{2,1,0:T(8,128)(2,1)}, bf16[32,16,512]{2,1,0:T(8,128)(2,1)}) custom-call(s32[1]{0:T(128)S(6)} %copy.10.counts, f32[2,256]{1,0:T(2,128)S(1)} %bitcast.15, bf16[2,256,256]{2,1,0:T(8,128)(2,1)S(1)} %bitcast.17, bf16[2,256,256]{2,1,0:T(8,128)(2,1)S(1)} %bitcast.19, bf16[2,128,256]{2,1,0:T(8,128)(2,1)S(1)} %collective-permute-done.15.refs_0_, ...), custom_call_target="tpu_custom_call" | custom-call | flops 1000000000 | bytes 1048576 | tf_op jit(solution)/shard_map/owner_gradients/pallas_call | solution.py:431
  86.6 7.9 %all-to-all-start = ((bf16[32,16,512]{2,1,0:T(8,128)(2,1)}), bf16[32,16,512]{2,1,0:T(8,128)(2,1)S(1)}, u32[]{:S(2)}, u32[]{:S(2)}) async-start(bf16[32,16,512]{2,1,0:T(8,128)(2,1)} %get-tuple-element.98), calls=%async_computation | async-start | bytes 1048576 | tf_op jit(solution)/shard_map/all_to_all | solution.py:578
  94.5 0.1 dynamic-slice_bitcast_fusion.g_ref
  94.6 16.5 %all-to-all-done.parts_ref = bf16[32,16,512]{2,1,0:T(8,128)(2,1)S(1)} async-done(((bf16[32,16,512]{2,1,0:T(8,128)(2,1)}), bf16[32,16,512]{2,1,0:T(8,128)(2,1)S(1)}, u32[]{:S(2)}, u32[]{:S(2)}) %all-to-all-start) | async-done | bytes 524320 | tf_op jit(solution)/shard_map/all_to_all | solution.py:578
  111.1 0.8 sum_parts.1
  (12 shorter events, 0.0 us)
Async XLA Ops:
  1.3 13.2 %copy-start.6 = (bf16[2,128,256]{2,1,0:T(8,128)(2,1)S(1)}, bf16[2,128,256]{2,1,0:T(8,128)(2,1)}, u32[]{:S(2)}) copy-start(bf16[2,128,256]{2,1,0:T(8,128)(2,1)} %x_ref.1) | copy-start | bytes 393220
  3.3 10.5 %collective-permute-start.2 = (bf16[1040,256]{1,0:T(8,128)(2,1)}, bf16[1040,256]{1,0:T(8,128)(2,1)S(1)}, u32[]{:S(2)}, u32[]{:S(2)}) collective-permute-start(bf16[1040,256]{1,0:T(8,128)(2,1)} %pack.1.refs_1_.refs_2_.refs_8_), channel_id=1, source_target_pairs={{0,32},{32,0},{64,96},{96,64},{1,33},{33,1},{65,97},{97,65},{2,34}... | collective-permute-start | bytes 1597448 | tf_op jit(solution)/shard_map/ppermute | solution.py:453
  12.1 10.6 %collective-permute-start = (bf16[1040,256]{1,0:T(8,128)(2,1)}, bf16[1040,256]{1,0:T(8,128)(2,1)S(1)}, u32[]{:S(2)}, u32[]{:S(2)}) collective-permute-start(bf16[1040,256]{1,0:T(8,128)(2,1)} %pack.1.refs_1_.refs_2_.refs_8_), channel_id=1, source_target_pairs={{128,192},{160,224},{320,384},{352,416},{129,193},{161,225},{321,3... | collective-permute-start | bytes 1597448 | tf_op jit(solution)/shard_map/ppermute | solution.py:453
  12.8 9.9 %collective-permute-start.1 = (bf16[1040,256]{1,0:T(8,128)(2,1)}, bf16[1040,256]{1,0:T(8,128)(2,1)S(1)}, u32[]{:S(2)}, u32[]{:S(2)}) collective-permute-start(bf16[1040,256]{1,0:T(8,128)(2,1)} %pack.1.refs_1_.refs_2_.refs_8_), channel_id=1, source_target_pairs={{256,192},{288,224},{448,384},{480,416},{257,193},{289,225},{449,3... | collective-permute-start | bytes 1597448 | tf_op jit(solution)/shard_map/ppermute | solution.py:453
  13.8 8.9 %collective-permute-start.3 = (bf16[1040,256]{1,0:T(8,128)(2,1)}, bf16[1040,256]{1,0:T(8,128)(2,1)S(1)}, u32[]{:S(2)}, u32[]{:S(2)}) collective-permute-start(bf16[1040,256]{1,0:T(8,128)(2,1)} %pack.1.refs_1_.refs_2_.refs_8_), channel_id=1, source_target_pairs={{192,224},{224,192},{384,416},{416,384},{193,225},{225,193},{385,4... | collective-permute-start | bytes 1597448 | tf_op jit(solution)/shard_map/ppermute | solution.py:453
  14.5 1.0 copy-start.2
  15.6 6.4 %copy-start.3 = (bf16[1040,256]{1,0:T(8,128)(2,1)S(1)}, bf16[1040,256]{1,0:T(8,128)(2,1)}, u32[]{:S(2)}) copy-start(bf16[1040,256]{1,0:T(8,128)(2,1)} %pack.1.refs_1_.refs_2_.refs_8_) | copy-start | bytes 1597444
  17.9 4.1 %collective-permute-start.4 = (bf16[2,128,256]{2,1,0:T(8,128)(2,1)S(1)}, bf16[2,128,256]{2,1,0:T(8,128)(2,1)S(1)}, u32[]{:S(2)}, u32[]{:S(2)}) collective-permute-start(bf16[2,128,256]{2,1,0:T(8,128)(2,1)S(1)} %get-tuple-element.54), channel_id=1, source_target_pairs={{0,64},{32,96},{1,65},{33,97},{2,66},{34,98},{3,67},{35,99},{4,68}... | collective-permute-start | bytes 393224 | tf_op jit(solution)/shard_map/ppermute | solution.py:453
  22.0 0.7 collective-permute-start.5
  22.7 19.4 %copy-start.5 = (bf16[2,128,256]{2,1,0:T(8,128)(2,1)S(1)}, bf16[2,128,256]{2,1,0:T(8,128)(2,1)}, u32[]{:S(2)}) copy-start(bf16[2,128,256]{2,1,0:T(8,128)(2,1)} %ct_ref.1) | copy-start | bytes 393220
  22.8 9.5 %collective-permute-start.6 = (bf16[1040,256]{1,0:T(8,128)(2,1)S(1)}, bf16[1040,256]{1,0:T(8,128)(2,1)S(1)}, u32[]{:S(2)}, u32[]{:S(2)}) collective-permute-start(bf16[1040,256]{1,0:T(8,128)(2,1)S(1)} %collective-permute-done.refs_0_), channel_id=1, source_target_pairs={{192,224},{224,192},{384,416},{416,384},{193,225},{225,193},{385,4... | collective-permute-start | bytes 1597448 | tf_op jit(solution)/shard_map/ppermute | solution.py:453
  23.6 8.7 %collective-permute-start.7 = (bf16[1040,256]{1,0:T(8,128)(2,1)S(1)}, bf16[1040,256]{1,0:T(8,128)(2,1)S(1)}, u32[]{:S(2)}, u32[]{:S(2)}) collective-permute-start(bf16[1040,256]{1,0:T(8,128)(2,1)S(1)} %collective-permute-done.1.refs_4_), channel_id=1, source_target_pairs={{192,224},{224,192},{384,416},{416,384},{193,225},{225,193},{385,4... | collective-permute-start | bytes 1597448 | tf_op jit(solution)/shard_map/ppermute | solution.py:453
  24.3 17.1 %collective-permute-start.13 = (bf16[1040,256]{1,0:T(8,128)(2,1)S(1)}, bf16[1040,256]{1,0:T(8,128)(2,1)S(1)}, u32[]{:S(2)}, u32[]{:S(2)}) collective-permute-start(bf16[1040,256]{1,0:T(8,128)(2,1)S(1)} %copy-done.3), channel_id=1, source_target_pairs={{0,64},{32,96},{1,65},{33,97},{2,66},{34,98},{3,67},{35,99},{4,68}... | collective-permute-start | bytes 1597448 | tf_op jit(solution)/shard_map/ppermute | solution.py:453
  31.5 10.6 %collective-permute-start.9 = (bf16[4,128,256]{2,1,0:T(8,128)(2,1)S(1)}, bf16[4,128,256]{2,1,0:T(8,128)(2,1)S(1)}, u32[]{:S(2)}, u32[]{:S(2)}) collective-permute-start(bf16[4,128,256]{2,1,0:T(8,128)(2,1)S(1)} %get-tuple-element.62), channel_id=1, source_target_pairs={{64,384},{96,416},{65,385},{97,417},{66,386},{98,418},{67,387},{99... | collective-permute-start | bytes 786440 | tf_op jit(solution)/shard_map/ppermute | solution.py:453
  32.3 9.8 %collective-permute-start.8 = (bf16[2,128,256]{2,1,0:T(8,128)(2,1)S(1)}, bf16[2,128,256]{2,1,0:T(8,128)(2,1)S(1)}, u32[]{:S(2)}, u32[]{:S(2)}) collective-permute-start(bf16[2,128,256]{2,1,0:T(8,128)(2,1)S(1)} %get-tuple-element.61), channel_id=1, source_target_pairs={{192,384},{224,416},{193,385},{225,417},{194,386},{226,418},{195,3... | collective-permute-start | bytes 393224 | tf_op jit(solution)/shard_map/ppermute | solution.py:453
  41.4 3.6 %collective-permute-start.14 = (bf16[1040,256]{1,0:T(8,128)(2,1)S(1)}, bf16[1040,256]{1,0:T(8,128)(2,1)S(1)}, u32[]{:S(2)}, u32[]{:S(2)}) collective-permute-start(bf16[1040,256]{1,0:T(8,128)(2,1)S(1)} %collective-permute-done.13.refs_6_), channel_id=1, source_target_pairs={{64,96},{96,64},{65,97},{97,65},{66,98},{98,66},{67,99},{99,67},{6... | collective-permute-start | bytes 1597448 | tf_op jit(solution)/shard_map/ppermute | solution.py:453
  42.2 2.7 %collective-permute-start.10 = (bf16[2,128,256]{2,1,0:T(8,128)(2,1)S(1)}, bf16[2,128,256]{2,1,0:T(8,128)(2,1)S(1)}, u32[]{:S(2)}, u32[]{:S(2)}) collective-permute-start(bf16[2,128,256]{2,1,0:T(8,128)(2,1)S(1)} %get-tuple-element.67), channel_id=1, source_target_pairs={{384,192},{416,224},{385,193},{417,225},{386,194},{418,226},{387,1... | collective-permute-start | bytes 393224 | tf_op jit(solution)/shard_map/ppermute | solution.py:453
  42.9 2.1 %collective-permute-start.11 = (bf16[2,128,256]{2,1,0:T(8,128)(2,1)S(1)}, bf16[2,128,256]{2,1,0:T(8,128)(2,1)S(1)}, u32[]{:S(2)}, u32[]{:S(2)}) collective-permute-start(bf16[2,128,256]{2,1,0:T(8,128)(2,1)S(1)} %get-tuple-element.68), channel_id=1, source_target_pairs={{192,256},{224,288},{384,448},{416,480},{193,257},{225,289},{385,4... | collective-permute-start | bytes 393224 | tf_op jit(solution)/shard_map/ppermute | solution.py:453
  43.6 1.4 %collective-permute-start.12 = (bf16[2,128,256]{2,1,0:T(8,128)(2,1)S(1)}, bf16[2,128,256]{2,1,0:T(8,128)(2,1)S(1)}, u32[]{:S(2)}, u32[]{:S(2)}) collective-permute-start(bf16[2,128,256]{2,1,0:T(8,128)(2,1)S(1)} %get-tuple-element.69), channel_id=1, source_target_pairs={{192,288},{224,256},{384,480},{416,448},{193,289},{225,257},{385,4... | collective-permute-start | bytes 393224 | tf_op jit(solution)/shard_map/ppermute | solution.py:453
  44.3 1.7 %collective-permute-start.18 = (bf16[4,128,256]{2,1,0:T(8,128)(2,1)S(1)}, bf16[4,128,256]{2,1,0:T(8,128)(2,1)S(1)}, u32[]{:S(2)}, u32[]{:S(2)}) collective-permute-start(bf16[4,128,256]{2,1,0:T(8,128)(2,1)S(1)} %get-tuple-element.80), channel_id=1, source_target_pairs={{384,64},{416,96},{385,65},{417,97},{386,66},{418,98},{387,67},{41... | collective-permute-start | bytes 786440 | tf_op jit(solution)/shard_map/ppermute | solution.py:453
  45.3 0.7 collective-permute-start.17
  46.0 38.1 %copy-start = (f32[1,2,256]{2,1,0:T(2,128)S(1)}, f32[1,2,256]{2,1,0:T(2,128)}, u32[]{:S(2)}) copy-start(f32[1,2,256]{2,1,0:T(2,128)} %param.10) | copy-start | bytes 6148
  46.0 38.1 %copy-start.1 = (bf16[1,2,256,256]{3,2,1,0:T(8,128)(2,1)S(1)}, bf16[1,2,256,256]{3,2,1,0:T(8,128)(2,1)}, u32[]{:S(2)}) copy-start(bf16[1,2,256,256]{3,2,1,0:T(8,128)(2,1)} %param.8) | copy-start | bytes 786436
  46.0 38.1 %copy-start.4 = (bf16[1,2,256,256]{3,2,1,0:T(8,128)(2,1)S(1)}, bf16[1,2,256,256]{3,2,1,0:T(8,128)(2,1)}, u32[]{:S(2)}) copy-start(bf16[1,2,256,256]{3,2,1,0:T(8,128)(2,1)} %param.9) | copy-start | bytes 786436
  46.5 37.6 %collective-permute-start.23 = (bf16[3,128,256]{2,1,0:T(8,128)(2,1)S(1)}, bf16[3,128,256]{2,1,0:T(8,128)(2,1)S(1)}, u32[]{:S(2)}, u32[]{:S(2)}) collective-permute-start(bf16[3,128,256]{2,1,0:T(8,128)(2,1)S(1)} %get-tuple-element.95), channel_id=1, source_target_pairs={{0,32},{32,0},{64,96},{96,64},{192,224},{224,192},{384,416},{416,3... | collective-permute-start | bytes 589832 | tf_op jit(solution)/shard_map/ppermute | solution.py:453
  50.8 31.1 %collective-permute-start.19 = (bf16[128,256]{1,0:T(8,128)(2,1)S(1)}, bf16[128,256]{1,0:T(8,128)(2,1)S(1)}, u32[]{:S(2)}, u32[]{:S(2)}) collective-permute-start(bf16[128,256]{1,0:T(8,128)(2,1)S(1)} %get-tuple-element.91), channel_id=1, source_target_pairs={{64,0},{96,32},{192,128},{224,160},{384,320},{416,352},{65,1},{97,... | collective-permute-start | bytes 196616 | tf_op jit(solution)/shard_map/ppermute | solution.py:453
  52.1 31.3 %collective-permute-start.20 = (bf16[128,256]{1,0:T(8,128)(2,1)S(1)}, bf16[128,256]{1,0:T(8,128)(2,1)S(1)}, u32[]{:S(2)}, u32[]{:S(2)}) collective-permute-start(bf16[128,256]{1,0:T(8,128)(2,1)S(1)} %get-tuple-element.92), channel_id=1, source_target_pairs={{64,32},{96,0},{192,160},{224,128},{384,352},{416,320},{65,33},{97... | collective-permute-start | bytes 196616 | tf_op jit(solution)/shard_map/ppermute | solution.py:453
  53.4 30.7 %collective-permute-start.15 = (bf16[2,128,256]{2,1,0:T(8,128)(2,1)S(1)}, bf16[2,128,256]{2,1,0:T(8,128)(2,1)S(1)}, u32[]{:S(2)}, u32[]{:S(2)}) collective-permute-start(bf16[2,128,256]{2,1,0:T(8,128)(2,1)S(1)} %get-tuple-element.75), channel_id=1, source_target_pairs={{192,128},{224,160},{384,320},{416,352},{193,129},{225,161},{385,3... | collective-permute-start | bytes 393224 | tf_op jit(solution)/shard_map/ppermute | solution.py:453
  54.0 30.0 %collective-permute-start.16 = (bf16[2,128,256]{2,1,0:T(8,128)(2,1)S(1)}, bf16[2,128,256]{2,1,0:T(8,128)(2,1)S(1)}, u32[]{:S(2)}, u32[]{:S(2)}) collective-permute-start(bf16[2,128,256]{2,1,0:T(8,128)(2,1)S(1)} %get-tuple-element.76), channel_id=1, source_target_pairs={{192,160},{224,128},{384,352},{416,320},{193,161},{225,129},{385,3... | collective-permute-start | bytes 393224 | tf_op jit(solution)/shard_map/ppermute | solution.py:453
  81.9 2.2 %collective-permute-start.21 = (bf16[128,256]{1,0:T(8,128)(2,1)S(1)}, bf16[128,256]{1,0:T(8,128)(2,1)S(1)}, u32[]{:S(2)}, u32[]{:S(2)}) collective-permute-start(bf16[128,256]{1,0:T(8,128)(2,1)S(1)} %get-tuple-element.93), channel_id=1, source_target_pairs={{192,256},{224,288},{384,448},{416,480},{193,257},{225,289},{385,4... | collective-permute-start | bytes 196616 | tf_op jit(solution)/shard_map/ppermute | solution.py:453
  83.4 0.7 collective-permute-start.22
  86.6 24.5 %all-to-all-start = ((bf16[32,16,512]{2,1,0:T(8,128)(2,1)}), bf16[32,16,512]{2,1,0:T(8,128)(2,1)S(1)}, u32[]{:S(2)}, u32[]{:S(2)}) async-start(bf16[32,16,512]{2,1,0:T(8,128)(2,1)} %get-tuple-element.98), calls=%async_computation | async-start | bytes 1048576 | tf_op jit(solution)/shard_map/all_to_all | solution.py:578

commit v7 on v6

--- a/solution.py
+++ b/solution.py
@@ -230,15 +230,15 @@
             state = (hop_ref[0] if slot == 0 else outs_ref[slot - 1]).astype(F32)
             if slot:
                 state = state + skips[slot][...].astype(F32)
-            inflow_ref[slot] = state.astype(BF16)
+            store_by_owner(core, slot, owners, 1, state.astype(BF16))
             weights.forward(slot, state, state_ref, pre_ref, outs_ref)
+        sent = [hop_out.at[0], hop_out.at[1]] + [sent_out.at[index] for index in range(4)]
         for slot in reversed(range(6)):
-            up_ref[slot] = ct_ref[core] if slot == 5 else sent_ref[slot + 1]
+            up_ref[slot] = ct_ref[core] if slot == 5 else sent[slot + 1][...]
             grad = up_ref[slot].astype(F32)
-            sent_ref[slot] = weights.backward(slot, grad, state_ref, pre_ref, grad_ref)
-        hop_out[...] = sent_ref[:2]
-        sent_out[...] = sent_ref[2:]
-        keep_rows(range(6), outs_ref, inflow_ref)
+            sent[slot][...] = weights.backward(slot, grad, state_ref, pre_ref, grad_ref)
+        for slot in range(6):
+            store_by_owner(core, slot, owners, 0, outs_ref[slot])
 
     @pl.when(here == MIDDLE)
     def _():

time: 113 us -> 114 us (level)
  the two profiles are of different devices: /device:TPU:1 before, /device:TPU:16 now
where the time goes in v7:
time: 114 us; the launch traced here: 112 us
  waiting for transfers between devices  72.4 us (64%)
  starting transfers between devices  30.8 us (27%)
  Pallas kernels  5.88 us (5%)
  between operations  1.75 us (2%)
  local copies, waits for them, and re-layouts  1.15 us (1%)
    ppermute x24, waiting for transfers between devices, move(): return lax.ppermute(value, 'section', pairs)  54.4 us
    ppermute x24, starting transfers between devices, move(): return lax.ppermute(value, 'section', pairs)  21.8 us
    all_to_all x1, waiting for transfers between devices, body(): parts = lax.all_to_all(parts, 'dp', 0, 0, tiled=True)  18 us
    all_to_all x1, starting transfers between devices, body(): parts = lax.all_to_all(parts, 'dp', 0, 0, tiled=True)  8.94 us
    pallas_call x9, Pallas kernels, call(): pl.pallas_call(kernel, out_shape=outputs, in_specs=[specs[memory]() for m...  5.88 us
  transfers between devices with their start and end apart: 25, of which 6 were waited for; matrix products, arithmetic and copies ran while one was open for 0% of the time, Pallas kernels for 1%

profile of v7, /device:TPU:16, one launch (start us, length us, event | category | flops | bytes accessed | tf_op | source)
XLA Modules:
  0.0 112.0 jit_solution(13403105996063461666)
XLA Ops:
  1.3 2.0 %pack.1.refs_1_.refs_2_.refs_8_ = bf16[1040,256]{1,0:T(8,128)(2,1)} custom-call(s32[1]{0:T(128)S(6)} %copy.10.counts, bf16[2,256,256]{2,1,0:T(8,128)(2,1)} %bitcast.16, bf16[2,256,256]{2,1,0:T(8,128)(2,1)} %bitcast.18, f32[2,256]{1,0:T(2,128)} %bitcast.14), custom_call_target="tpu_custom_call" | custom-call | flops 1000000000 | bytes 1048576 | tf_op jit(solution)/shard_map/pack/pallas_call | solution.py:431
  3.3 0.7 collective-permute-start.2
  4.0 3.5 %collective-permute-start = (bf16[1040,256]{1,0:T(8,128)(2,1)}, bf16[1040,256]{1,0:T(8,128)(2,1)S(1)}, u32[]{:S(2)}, u32[]{:S(2)}) collective-permute-start(bf16[1040,256]{1,0:T(8,128)(2,1)} %pack.1.refs_1_.refs_2_.refs_8_), channel_id=1, source_target_pairs={{128,192},{160,224},{320,384},{352,416},{129,193},{161,225},{321,3... | collective-permute-start | bytes 1597448 | tf_op jit(solution)/shard_map/ppermute | solution.py:453
  7.5 0.7 collective-permute-start.1
  8.2 0.0 collective-permute-done.2.refs_2_.refs_9_
  8.2 0.7 collective-permute-start.3
  8.9 1.0 copy-done.2
  10.0 0.7 pair_forward.2
  10.7 0.7 collective-permute-start.4
  11.4 0.0 collective-permute-done.4.refs_0_
  11.5 0.7 collective-permute-start.5
  12.1 7.0 %collective-permute-done.refs_0_ = bf16[1040,256]{1,0:T(8,128)(2,1)S(1)} collective-permute-done((bf16[1040,256]{1,0:T(8,128)(2,1)}, bf16[1040,256]{1,0:T(8,128)(2,1)S(1)}, u32[]{:S(2)}, u32[]{:S(2)}) %collective-permute-start) | collective-permute-done | bytes 532512 | tf_op jit(solution)/shard_map/ppermute | solution.py:453
  19.1 0.0 collective-permute-done.1.refs_4_
  19.1 0.0 collective-permute-done.5.hop_ref
  19.1 0.0 collective-permute-done.3.refs_3_
  19.1 0.0 copy-start.5
  19.2 0.8 collective-permute-start.6
  20.0 0.7 collective-permute-start.7
  20.7 0.7 collective-permute-start.13
  21.4 0.7 collective-permute-start.9
  22.1 0.0 collective-permute-done.6.refs_1_
  22.1 0.0 collective-permute-done.7.refs_5_
  22.1 0.1 middle_forward.1
  22.2 0.7 collective-permute-start.8
  22.9 0.0 collective-permute-done.13.refs_6_
  22.9 0.7 collective-permute-start.14
  23.6 0.0 collective-permute-done.9.skip_ref
  23.6 0.0 collective-permute-done.8.hop_ref
  23.6 0.1 last_both.1
  23.7 0.7 collective-permute-start.10
  24.4 0.7 collective-permute-start.11
  25.1 0.7 collective-permute-start.12
  25.7 0.7 collective-permute-start.18
  26.4 0.0 collective-permute-done.10.hop_ref
  26.4 0.0 collective-permute-done.11.refs_2_
  26.4 0.0 collective-permute-done.12.refs_3_
  26.5 0.0 collective-permute-done.14.refs_7_
  26.5 0.3 middle_backward.1
  26.7 0.7 collective-permute-start.17
  27.4 0.0 collective-permute-done.18.skip_ref
  27.4 0.0 collective-permute-done.17.hop_ref
  27.4 0.0 copy-start
  27.4 0.0 copy-start.1
  27.5 0.0 copy-start.4
  27.5 0.1 first_backward.1
  27.6 0.8 collective-permute-start.23
  28.4 1.3 %collective-permute-start.19 = (bf16[128,256]{1,0:T(8,128)(2,1)S(1)}, bf16[128,256]{1,0:T(8,128)(2,1)S(1)}, u32[]{:S(2)}, u32[]{:S(2)}) collective-permute-start(bf16[128,256]{1,0:T(8,128)(2,1)S(1)} %get-tuple-element.91), channel_id=1, source_target_pairs={{64,0},{96,32},{192,128},{224,160},{384,320},{416,352},{65,1},{97,... | collective-permute-start | bytes 196616 | tf_op jit(solution)/shard_map/ppermute | solution.py:453
  29.7 1.3 %collective-permute-start.20 = (bf16[128,256]{1,0:T(8,128)(2,1)S(1)}, bf16[128,256]{1,0:T(8,128)(2,1)S(1)}, u32[]{:S(2)}, u32[]{:S(2)}) collective-permute-start(bf16[128,256]{1,0:T(8,128)(2,1)S(1)} %get-tuple-element.92), channel_id=1, source_target_pairs={{64,32},{96,0},{192,160},{224,128},{384,352},{416,320},{65,33},{97... | collective-permute-start | bytes 196616 | tf_op jit(solution)/shard_map/ppermute | solution.py:453
  31.0 1.3 %collective-permute-start.15 = (bf16[2,128,256]{2,1,0:T(8,128)(2,1)S(1)}, bf16[2,128,256]{2,1,0:T(8,128)(2,1)S(1)}, u32[]{:S(2)}, u32[]{:S(2)}) collective-permute-start(bf16[2,128,256]{2,1,0:T(8,128)(2,1)S(1)} %get-tuple-element.75), channel_id=1, source_target_pairs={{192,128},{224,160},{384,320},{416,352},{193,129},{225,161},{385,3... | collective-permute-start | bytes 393224 | tf_op jit(solution)/shard_map/ppermute | solution.py:453
  32.3 1.3 %collective-permute-start.16 = (bf16[2,128,256]{2,1,0:T(8,128)(2,1)S(1)}, bf16[2,128,256]{2,1,0:T(8,128)(2,1)S(1)}, u32[]{:S(2)}, u32[]{:S(2)}) collective-permute-start(bf16[2,128,256]{2,1,0:T(8,128)(2,1)S(1)} %get-tuple-element.76), channel_id=1, source_target_pairs={{192,160},{224,128},{384,352},{416,320},{193,161},{225,129},{385,3... | collective-permute-start | bytes 393224 | tf_op jit(solution)/shard_map/ppermute | solution.py:453
  33.6 41.9 %collective-permute-done.19.refs_4_ = bf16[128,256]{1,0:T(8,128)(2,1)S(1)} collective-permute-done((bf16[128,256]{1,0:T(8,128)(2,1)S(1)}, bf16[128,256]{1,0:T(8,128)(2,1)S(1)}, u32[]{:S(2)}, u32[]{:S(2)}) %collective-permute-start.19) | collective-permute-done | bytes 65568 | tf_op jit(solution)/shard_map/ppermute | solution.py:453
  75.5 0.7 collective-permute-start.21
  76.2 0.6 collective-permute-done.20.refs_5_
  76.7 0.7 collective-permute-start.22
  77.4 0.0 collective-permute-done.21.refs_6_
  77.4 0.0 collective-permute-done.22.refs_7_
  77.4 2.3 %collective-permute-done.15.refs_0_ = bf16[2,128,256]{2,1,0:T(8,128)(2,1)S(1)} collective-permute-done((bf16[2,128,256]{2,1,0:T(8,128)(2,1)S(1)}, bf16[2,128,256]{2,1,0:T(8,128)(2,1)S(1)}, u32[]{:S(2)}, u32[]{:S(2)}) %collective-permute-start.15) | collective-permute-done | bytes 131104 | tf_op jit(solution)/shard_map/ppermute | solution.py:453
  79.7 2.6 %collective-permute-done.16.refs_1_ = bf16[2,128,256]{2,1,0:T(8,128)(2,1)S(1)} collective-permute-done((bf16[2,128,256]{2,1,0:T(8,128)(2,1)S(1)}, bf16[2,128,256]{2,1,0:T(8,128)(2,1)S(1)}, u32[]{:S(2)}, u32[]{:S(2)}) %collective-permute-start.16) | collective-permute-done | bytes 131104 | tf_op jit(solution)/shard_map/ppermute | solution.py:453
  82.3 0.0 collective-permute-done.23.refs_8_
  82.4 1.8 %owner_gradients.1 = (bf16[2,128,256]{2,1,0:T(8,128)(2,1)}, bf16[32,16,512]{2,1,0:T(8,128)(2,1)}) custom-call(s32[1]{0:T(128)S(6)} %copy.10.counts, f32[2,256]{1,0:T(2,128)S(1)} %bitcast.15, bf16[2,256,256]{2,1,0:T(8,128)(2,1)S(1)} %bitcast.17, bf16[2,256,256]{2,1,0:T(8,128)(2,1)S(1)} %bitcast.19, bf16[2,128,256]{2,1,0:T(8,128)(2,1)S(1)} %collective-permute-done.15.refs_0_, ...), custom_call_target="tpu_custom_call" | custom-call | flops 1000000000 | bytes 1048576 | tf_op jit(solution)/shard_map/owner_gradients/pallas_call | solution.py:431
  84.2 8.9 %all-to-all-start = ((bf16[32,16,512]{2,1,0:T(8,128)(2,1)}), bf16[32,16,512]{2,1,0:T(8,128)(2,1)S(1)}, u32[]{:S(2)}, u32[]{:S(2)}) async-start(bf16[32,16,512]{2,1,0:T(8,128)(2,1)} %get-tuple-element.98), calls=%async_computation | async-start | bytes 1048576 | tf_op jit(solution)/shard_map/all_to_all | solution.py:578
  93.1 0.1 dynamic-slice_bitcast_fusion.g_ref
  93.2 18.0 %all-to-all-done.parts_ref = bf16[32,16,512]{2,1,0:T(8,128)(2,1)S(1)} async-done(((bf16[32,16,512]{2,1,0:T(8,128)(2,1)}), bf16[32,16,512]{2,1,0:T(8,128)(2,1)S(1)}, u32[]{:S(2)}, u32[]{:S(2)}) %all-to-all-start) | async-done | bytes 524320 | tf_op jit(solution)/shard_map/all_to_all | solution.py:578
  111.2 0.8 sum_parts.1
  (12 shorter events, 0.1 us)
Async XLA Ops:
  1.3 7.6 %copy-start.6 = (bf16[2,128,256]{2,1,0:T(8,128)(2,1)S(1)}, bf16[2,128,256]{2,1,0:T(8,128)(2,1)}, u32[]{:S(2)}) copy-start(bf16[2,128,256]{2,1,0:T(8,128)(2,1)} %x_ref.1) | copy-start | bytes 393220
  3.3 4.9 %collective-permute-start.2 = (bf16[1040,256]{1,0:T(8,128)(2,1)}, bf16[1040,256]{1,0:T(8,128)(2,1)S(1)}, u32[]{:S(2)}, u32[]{:S(2)}) collective-permute-start(bf16[1040,256]{1,0:T(8,128)(2,1)} %pack.1.refs_1_.refs_2_.refs_8_), channel_id=1, source_target_pairs={{0,32},{32,0},{64,96},{96,64},{1,33},{33,1},{65,97},{97,65},{2,34}... | collective-permute-start | bytes 1597448 | tf_op jit(solution)/shard_map/ppermute | solution.py:453
  4.0 15.1 %collective-permute-start = (bf16[1040,256]{1,0:T(8,128)(2,1)}, bf16[1040,256]{1,0:T(8,128)(2,1)S(1)}, u32[]{:S(2)}, u32[]{:S(2)}) collective-permute-start(bf16[1040,256]{1,0:T(8,128)(2,1)} %pack.1.refs_1_.refs_2_.refs_8_), channel_id=1, source_target_pairs={{128,192},{160,224},{320,384},{352,416},{129,193},{161,225},{321,3... | collective-permute-start | bytes 1597448 | tf_op jit(solution)/shard_map/ppermute | solution.py:453
  7.5 11.6 %collective-permute-start.1 = (bf16[1040,256]{1,0:T(8,128)(2,1)}, bf16[1040,256]{1,0:T(8,128)(2,1)S(1)}, u32[]{:S(2)}, u32[]{:S(2)}) collective-permute-start(bf16[1040,256]{1,0:T(8,128)(2,1)} %pack.1.refs_1_.refs_2_.refs_8_), channel_id=1, source_target_pairs={{256,192},{288,224},{448,384},{480,416},{257,193},{289,225},{449,3... | collective-permute-start | bytes 1597448 | tf_op jit(solution)/shard_map/ppermute | solution.py:453
  8.2 10.9 %collective-permute-start.3 = (bf16[1040,256]{1,0:T(8,128)(2,1)}, bf16[1040,256]{1,0:T(8,128)(2,1)S(1)}, u32[]{:S(2)}, u32[]{:S(2)}) collective-permute-start(bf16[1040,256]{1,0:T(8,128)(2,1)} %pack.1.refs_1_.refs_2_.refs_8_), channel_id=1, source_target_pairs={{192,224},{224,192},{384,416},{416,384},{193,225},{225,193},{385,4... | collective-permute-start | bytes 1597448 | tf_op jit(solution)/shard_map/ppermute | solution.py:453
  8.9 1.0 copy-start.2
  10.0 1.4 %copy-start.3 = (bf16[1040,256]{1,0:T(8,128)(2,1)S(1)}, bf16[1040,256]{1,0:T(8,128)(2,1)}, u32[]{:S(2)}) copy-start(bf16[1040,256]{1,0:T(8,128)(2,1)} %pack.1.refs_1_.refs_2_.refs_8_) | copy-start | bytes 1597444
  10.7 0.7 collective-permute-start.4
  11.5 7.7 %collective-permute-start.5 = (bf16[128,256]{1,0:T(8,128)(2,1)S(1)}, bf16[128,256]{1,0:T(8,128)(2,1)S(1)}, u32[]{:S(2)}, u32[]{:S(2)}) collective-permute-start(bf16[128,256]{1,0:T(8,128)(2,1)S(1)} %slice_bitcast_fusion), channel_id=1, source_target_pairs={{64,192},{96,224},{65,193},{97,225},{66,194},{98,226},{67,195},{99... | collective-permute-start | bytes 196616 | tf_op jit(solution)/shard_map/ppermute | solution.py:453
  19.1 4.5 %copy-start.5 = (bf16[2,128,256]{2,1,0:T(8,128)(2,1)S(1)}, bf16[2,128,256]{2,1,0:T(8,128)(2,1)}, u32[]{:S(2)}) copy-start(bf16[2,128,256]{2,1,0:T(8,128)(2,1)} %ct_ref.1) | copy-start | bytes 393220
  19.2 2.9 %collective-permute-start.6 = (bf16[1040,256]{1,0:T(8,128)(2,1)S(1)}, bf16[1040,256]{1,0:T(8,128)(2,1)S(1)}, u32[]{:S(2)}, u32[]{:S(2)}) collective-permute-start(bf16[1040,256]{1,0:T(8,128)(2,1)S(1)} %collective-permute-done.refs_0_), channel_id=1, source_target_pairs={{192,224},{224,192},{384,416},{416,384},{193,225},{225,193},{385,4... | collective-permute-start | bytes 1597448 | tf_op jit(solution)/shard_map/ppermute | solution.py:453
  20.0 2.1 %collective-permute-start.7 = (bf16[1040,256]{1,0:T(8,128)(2,1)S(1)}, bf16[1040,256]{1,0:T(8,128)(2,1)S(1)}, u32[]{:S(2)}, u32[]{:S(2)}) collective-permute-start(bf16[1040,256]{1,0:T(8,128)(2,1)S(1)} %collective-permute-done.1.refs_4_), channel_id=1, source_target_pairs={{192,224},{224,192},{384,416},{416,384},{193,225},{225,193},{385,4... | collective-permute-start | bytes 1597448 | tf_op jit(solution)/shard_map/ppermute | solution.py:453
  20.7 2.2 %collective-permute-start.13 = (bf16[1040,256]{1,0:T(8,128)(2,1)S(1)}, bf16[1040,256]{1,0:T(8,128)(2,1)S(1)}, u32[]{:S(2)}, u32[]{:S(2)}) collective-permute-start(bf16[1040,256]{1,0:T(8,128)(2,1)S(1)} %copy-done.3), channel_id=1, source_target_pairs={{0,64},{32,96},{1,65},{33,97},{2,66},{34,98},{3,67},{35,99},{4,68}... | collective-permute-start | bytes 1597448 | tf_op jit(solution)/shard_map/ppermute | solution.py:453
  21.4 2.2 %collective-permute-start.9 = (bf16[4,128,256]{2,1,0:T(8,128)(2,1)S(1)}, bf16[4,128,256]{2,1,0:T(8,128)(2,1)S(1)}, u32[]{:S(2)}, u32[]{:S(2)}) collective-permute-start(bf16[4,128,256]{2,1,0:T(8,128)(2,1)S(1)} %get-tuple-element.62), channel_id=1, source_target_pairs={{64,384},{96,416},{65,385},{97,417},{66,386},{98,418},{67,387},{99... | collective-permute-start | bytes 786440 | tf_op jit(solution)/shard_map/ppermute | solution.py:453
  22.2 1.4 %collective-permute-start.8 = (bf16[2,128,256]{2,1,0:T(8,128)(2,1)S(1)}, bf16[2,128,256]{2,1,0:T(8,128)(2,1)S(1)}, u32[]{:S(2)}, u32[]{:S(2)}) collective-permute-start(bf16[2,128,256]{2,1,0:T(8,128)(2,1)S(1)} %get-tuple-element.61), channel_id=1, source_target_pairs={{192,384},{224,416},{193,385},{225,417},{194,386},{226,418},{195,3... | collective-permute-start | bytes 393224 | tf_op jit(solution)/shard_map/ppermute | solution.py:453
  22.9 3.6 %collective-permute-start.14 = (bf16[1040,256]{1,0:T(8,128)(2,1)S(1)}, bf16[1040,256]{1,0:T(8,128)(2,1)S(1)}, u32[]{:S(2)}, u32[]{:S(2)}) collective-permute-start(bf16[1040,256]{1,0:T(8,128)(2,1)S(1)} %collective-permute-done.13.refs_6_), channel_id=1, source_target_pairs={{64,96},{96,64},{65,97},{97,65},{66,98},{98,66},{67,99},{99,67},{6... | collective-permute-start | bytes 1597448 | tf_op jit(solution)/shard_map/ppermute | solution.py:453
  23.7 2.7 %collective-permute-start.10 = (bf16[2,128,256]{2,1,0:T(8,128)(2,1)S(1)}, bf16[2,128,256]{2,1,0:T(8,128)(2,1)S(1)}, u32[]{:S(2)}, u32[]{:S(2)}) collective-permute-start(bf16[2,128,256]{2,1,0:T(8,128)(2,1)S(1)} %get-tuple-element.67), channel_id=1, source_target_pairs={{384,192},{416,224},{385,193},{417,225},{386,194},{418,226},{387,1... | collective-permute-start | bytes 393224 | tf_op jit(solution)/shard_map/ppermute | solution.py:453
  24.4 2.1 %collective-permute-start.11 = (bf16[2,128,256]{2,1,0:T(8,128)(2,1)S(1)}, bf16[2,128,256]{2,1,0:T(8,128)(2,1)S(1)}, u32[]{:S(2)}, u32[]{:S(2)}) collective-permute-start(bf16[2,128,256]{2,1,0:T(8,128)(2,1)S(1)} %get-tuple-element.68), channel_id=1, source_target_pairs={{192,256},{224,288},{384,448},{416,480},{193,257},{225,289},{385,4... | collective-permute-start | bytes 393224 | tf_op jit(solution)/shard_map/ppermute | solution.py:453
  25.1 1.4 %collective-permute-start.12 = (bf16[2,128,256]{2,1,0:T(8,128)(2,1)S(1)}, bf16[2,128,256]{2,1,0:T(8,128)(2,1)S(1)}, u32[]{:S(2)}, u32[]{:S(2)}) collective-permute-start(bf16[2,128,256]{2,1,0:T(8,128)(2,1)S(1)} %get-tuple-element.69), channel_id=1, source_target_pairs={{192,288},{224,256},{384,480},{416,448},{193,289},{225,257},{385,4... | collective-permute-start | bytes 393224 | tf_op jit(solution)/shard_map/ppermute | solution.py:453
  25.7 1.7 %collective-permute-start.18 = (bf16[4,128,256]{2,1,0:T(8,128)(2,1)S(1)}, bf16[4,128,256]{2,1,0:T(8,128)(2,1)S(1)}, u32[]{:S(2)}, u32[]{:S(2)}) collective-permute-start(bf16[4,128,256]{2,1,0:T(8,128)(2,1)S(1)} %get-tuple-element.80), channel_id=1, source_target_pairs={{384,64},{416,96},{385,65},{417,97},{386,66},{418,98},{387,67},{41... | collective-permute-start | bytes 786440 | tf_op jit(solution)/shard_map/ppermute | solution.py:453
  26.7 0.7 collective-permute-start.17
  27.4 54.9 %copy-start = (f32[1,2,256]{2,1,0:T(2,128)S(1)}, f32[1,2,256]{2,1,0:T(2,128)}, u32[]{:S(2)}) copy-start(f32[1,2,256]{2,1,0:T(2,128)} %param.10) | copy-start | bytes 6148
  27.4 54.9 %copy-start.1 = (bf16[1,2,256,256]{3,2,1,0:T(8,128)(2,1)S(1)}, bf16[1,2,256,256]{3,2,1,0:T(8,128)(2,1)}, u32[]{:S(2)}) copy-start(bf16[1,2,256,256]{3,2,1,0:T(8,128)(2,1)} %param.8) | copy-start | bytes 786436
  27.5 54.9 %copy-start.4 = (bf16[1,2,256,256]{3,2,1,0:T(8,128)(2,1)S(1)}, bf16[1,2,256,256]{3,2,1,0:T(8,128)(2,1)}, u32[]{:S(2)}) copy-start(bf16[1,2,256,256]{3,2,1,0:T(8,128)(2,1)} %param.9) | copy-start | bytes 786436
  27.6 54.8 %collective-permute-start.23 = (bf16[3,128,256]{2,1,0:T(8,128)(2,1)S(1)}, bf16[3,128,256]{2,1,0:T(8,128)(2,1)S(1)}, u32[]{:S(2)}, u32[]{:S(2)}) collective-permute-start(bf16[3,128,256]{2,1,0:T(8,128)(2,1)S(1)} %get-tuple-element.95), channel_id=1, source_target_pairs={{0,32},{32,0},{64,96},{96,64},{192,224},{224,192},{384,416},{416,3... | collective-permute-start | bytes 589832 | tf_op jit(solution)/shard_map/ppermute | solution.py:453
  28.4 47.1 %collective-permute-start.19 = (bf16[128,256]{1,0:T(8,128)(2,1)S(1)}, bf16[128,256]{1,0:T(8,128)(2,1)S(1)}, u32[]{:S(2)}, u32[]{:S(2)}) collective-permute-start(bf16[128,256]{1,0:T(8,128)(2,1)S(1)} %get-tuple-element.91), channel_id=1, source_target_pairs={{64,0},{96,32},{192,128},{224,160},{384,320},{416,352},{65,1},{97,... | collective-permute-start | bytes 196616 | tf_op jit(solution)/shard_map/ppermute | solution.py:453
  29.7 47.0 %collective-permute-start.20 = (bf16[128,256]{1,0:T(8,128)(2,1)S(1)}, bf16[128,256]{1,0:T(8,128)(2,1)S(1)}, u32[]{:S(2)}, u32[]{:S(2)}) collective-permute-start(bf16[128,256]{1,0:T(8,128)(2,1)S(1)} %get-tuple-element.92), channel_id=1, source_target_pairs={{64,32},{96,0},{192,160},{224,128},{384,352},{416,320},{65,33},{97... | collective-permute-start | bytes 196616 | tf_op jit(solution)/shard_map/ppermute | solution.py:453
  31.0 48.7 %collective-permute-start.15 = (bf16[2,128,256]{2,1,0:T(8,128)(2,1)S(1)}, bf16[2,128,256]{2,1,0:T(8,128)(2,1)S(1)}, u32[]{:S(2)}, u32[]{:S(2)}) collective-permute-start(bf16[2,128,256]{2,1,0:T(8,128)(2,1)S(1)} %get-tuple-element.75), channel_id=1, source_target_pairs={{192,128},{224,160},{384,320},{416,352},{193,129},{225,161},{385,3... | collective-permute-start | bytes 393224 | tf_op jit(solution)/shard_map/ppermute | solution.py:453
  32.3 50.1 %collective-permute-start.16 = (bf16[2,128,256]{2,1,0:T(8,128)(2,1)S(1)}, bf16[2,128,256]{2,1,0:T(8,128)(2,1)S(1)}, u32[]{:S(2)}, u32[]{:S(2)}) collective-permute-start(bf16[2,128,256]{2,1,0:T(8,128)(2,1)S(1)} %get-tuple-element.76), channel_id=1, source_target_pairs={{192,160},{224,128},{384,352},{416,320},{193,161},{225,129},{385,3... | collective-permute-start | bytes 393224 | tf_op jit(solution)/shard_map/ppermute | solution.py:453
  75.5 1.9 %collective-permute-start.21 = (bf16[128,256]{1,0:T(8,128)(2,1)S(1)}, bf16[128,256]{1,0:T(8,128)(2,1)S(1)}, u32[]{:S(2)}, u32[]{:S(2)}) collective-permute-start(bf16[128,256]{1,0:T(8,128)(2,1)S(1)} %get-tuple-element.93), channel_id=1, source_target_pairs={{192,256},{224,288},{384,448},{416,480},{193,257},{225,289},{385,4... | collective-permute-start | bytes 196616 | tf_op jit(solution)/shard_map/ppermute | solution.py:453
  76.7 0.7 collective-permute-start.22
  84.2 27.0 %all-to-all-start = ((bf16[32,16,512]{2,1,0:T(8,128)(2,1)}), bf16[32,16,512]{2,1,0:T(8,128)(2,1)S(1)}, u32[]{:S(2)}, u32[]{:S(2)}) async-start(bf16[32,16,512]{2,1,0:T(8,128)(2,1)} %get-tuple-element.98), calls=%async_computation | async-start | bytes 1048576 | tf_op jit(solution)/shard_map/all_to_all | solution.py:578
